TPU v7x, 32 devices: a whole 2x2x4 slice. The times are simulated.
32 devices in a mesh: sens: 2 (over core), pts: 16 (over z, y, x).
Axes of the slice: x: 2, y: 2, z: 4, core: 2. Of those that a mesh axis runs over, the one named last changes fastest.
Arguments:
- kernel: float32 [16, 1024, 384], P('sens', 'pts'), may hold values from -0.009765625 to 0.009765625
- vectors: float32 [8, 1024, 384], P(None, 'pts'), may hold values from -6 to 6
- noise_scale: float32 [16], P('sens'), may hold values from 0.5 to 2
- sensor_group: int32 [16], P('sens'), may hold values from 0 to 3
- correlation: float32 [4, 384, 384], replicated, may hold values from -0.3125 to 0.3125
- stiffness: float32 [1024], P('pts'), may hold values from 0.2 to 1
- couplings: float32 [4, 1024], P(None, 'pts'), may hold values from 0.05 to 0.5
- neighbors: int32 [4, 1024], P(None, 'pts'), may hold values from 0 to 1023, as said below
Outputs:
- hessian_action: float32 [8, 1024, 384], P('sens', 'pts')
Inputs may be any that keep to these rules, and one draw needn't show every extreme that they name: `neighbors`: points are numbered row by row on a grid of rows of 16 points; every neighbor of point p lies in p's grid row or in one of the two rows beside it.
All inputs are finite; a program needn't handle non-finite values.
Results may differ from a plain program's by a relative error of at most 0.0001.
Values sent between devices are 32-bit elements; how exact they have to be, the bound alone decides.
No kernel may reach another device: no remote copies, remote signals or barrier semaphores. Data moves between devices by JAX's collectives and lax.ppermute only.
A program may use at most 64 MiB of HBM per device.

v0:
```python
import math

import jax
import jax.numpy as jnp
from jax import lax
from jax.sharding import PartitionSpec as P

COLS = 16


HIGHEST = lax.Precision.HIGHEST


def padded_2(block, sides, width):
    for axis, dim in sides:
        count = lax.axis_size(axis)
        forward = [(i, i + 1) for i in range(count - 1)]
        backward = [(target, source) for source, target in forward]
        low = lax.ppermute(
            lax.slice_in_dim(block, block.shape[dim] - width, None, axis=dim), axis, forward
        )
        high = lax.ppermute(lax.slice_in_dim(block, 0, width, axis=dim), axis, backward)
        block = jnp.concatenate([low, block, high], axis=dim)
    return block


def tables(length):
    span = 2 * length
    steps = lax.iota(jnp.int32, length)
    phase = steps[:, None] * steps[None, :] % span
    angle = phase.astype(jnp.float32) * (2.0 * math.pi / span)
    cosine = jnp.cos(angle)
    sine = jnp.sin(angle)
    nyquist = jnp.where(steps % 2 == 0, 1.0, -1.0).astype(jnp.float32)
    first_col = steps == 0
    second = jnp.where(first_col[None, :], nyquist[:, None], -sine)
    forward = jnp.concatenate([cosine, second], axis=1)
    weight = jnp.where(first_col, 1.0, 2.0).astype(jnp.float32)
    back_first = cosine * weight[:, None]
    back_second = jnp.where(first_col[:, None], nyquist[None, :], -2.0 * sine)
    inverse = jnp.concatenate([back_first, back_second], axis=0) / span
    return (forward, inverse)


def spectral(left, right, form, half):
    left_x, left_y = (left[..., :half], left[..., half:])
    right_x, right_y = (right[..., :half], right[..., half:])
    prod_xx = jnp.einsum(form, left_x, right_x, precision=HIGHEST)
    prod_yy = jnp.einsum(form, left_y, right_y, precision=HIGHEST)
    prod_xy = jnp.einsum(form, left_x, right_y, precision=HIGHEST)
    prod_yx = jnp.einsum(form, left_y, right_x, precision=HIGHEST)
    keep = (lax.iota(jnp.int32, half) > 0).astype(jnp.float32)
    real_part = prod_xx - keep * prod_yy
    imag_part = keep * (prod_xy + prod_yx) + (1.0 - keep) * prod_yy
    return jnp.concatenate([real_part, imag_part], axis=-1)


def weight_rows(rows, row_ids, noise_scale, sensor_group, correlation):
    sensors = noise_scale.shape[0]
    groups = correlation.shape[0]
    pick = (row_ids[:, None] % sensors == lax.iota(jnp.int32, sensors)[None, :]).astype(jnp.float32)
    group_table = (sensor_group[:, None] == lax.iota(jnp.int32, groups)[None, :]).astype(
        jnp.float32
    )
    row_scale = jnp.dot(pick, noise_scale, precision=HIGHEST)
    row_group = jnp.dot(pick, group_table, precision=HIGHEST)
    mixed = jnp.einsum("rt,but->rbu", rows, correlation, precision=HIGHEST)
    extra = jnp.einsum("rbu,rb->ru", mixed, row_group, precision=HIGHEST)
    return row_scale[:, None] * (rows + extra)


def local(kernel, vectors, noise_scale, sensor_group, correlation, stiffness, couplings, neighbors):
    sensors, points, length = kernel.shape
    count = vectors.shape[0]
    forward, inverse = tables(length)
    kern_hat = jnp.einsum("spt,tf->spf", kernel, forward, precision=HIGHEST)
    vec_hat = jnp.einsum("kpt,tf->kpf", vectors, forward, precision=HIGHEST)
    pred_hat = spectral(vec_hat, kern_hat, "kpf,spf->ksf", length)
    partial_value = jnp.einsum("ksf,ft->kst", pred_hat, inverse, precision=HIGHEST)
    flat = partial_value.reshape(count * sensors, length)
    predicted = lax.psum(flat, "pts")
    row_ids = lax.iota(jnp.int32, count * sensors)
    weighted = weight_rows(predicted, row_ids, noise_scale, sensor_group, correlation)
    residual = weighted.reshape(count, sensors, length)
    res_hat = jnp.einsum("kst,tf->ksf", residual, forward, precision=HIGHEST)
    columns = lax.iota(jnp.int32, 2 * length)
    flip = jnp.where(columns > length, -1.0, 1.0).astype(jnp.float32)
    conj_hat = kern_hat * flip
    grad_hat = spectral(res_hat, conj_hat, "ksf,spf->kpf", length)
    own_count = count // lax.axis_size("sens")
    own_hat = lax.psum_scatter(grad_hat, "sens", scatter_dimension=0, tiled=True)
    data_term = jnp.einsum("kpf,ft->kpt", own_hat, inverse, precision=HIGHEST)
    own_vectors = lax.dynamic_slice_in_dim(
        vectors, lax.axis_index("sens") * own_count, own_count, 0
    )
    padded = padded_2(own_vectors, (("pts", 1),), COLS)
    local_index = neighbors - lax.axis_index("pts") * points + COLS
    gathered = jnp.take(padded, local_index, axis=1)
    prior_term = stiffness[None, :, None] * own_vectors
    prior_term = prior_term + jnp.sum(
        couplings[None, :, :, None] * (own_vectors[:, None] - gathered), axis=1
    )
    return data_term + prior_term


def solution(mesh):
    in_specs = (
        P("sens", "pts", None),
        P(None, "pts", None),
        P("sens"),
        P("sens"),
        P(),
        P("pts"),
        P(None, "pts"),
        P(None, "pts"),
    )
    out_specs = P("sens", "pts", None)
    return jax.shard_map(local, mesh=mesh, in_specs=in_specs, out_specs=out_specs, check_vma=False)
```

profile of v0, /device:TPU:6, one launch (start us, length us, event | category | flops | bytes accessed | tf_op | source)
XLA Modules:
  0.0 226.9 jit_solution(6374704331866650512)
XLA Ops:
  8.8 3.3 %multiply_select_fusion = (f32[384,384]{1,0:T(8,128)}, f32[384,384]{1,0:T(8,128)S(1)}) fusion(f32[384]{0:T(512)S(1)} %fusion.35, pred[384]{0:T(512)(128)(4,1)S(1)} %iota_compare_fusion.7), kind=kLoop, calls=%fused_computation.25 | loop fusion | flops 1916928 | bytes 1181568 | tf_op jit(solution)/shard_map/jit(_where)/select_n | solution.py:40
  12.2 2.7 %broadcast_multiply_fusion = (f32[8,64,768]{2,1,0:T(8,128)S(1)}, f32[8,64,768]{2,1,0:T(8,128)S(1)}) fusion(f32[768]{0:T(1024)S(1)} %fusion.30, f32[8,64,384]{2,1,0:T(8,128)S(1)} %copy-done.13, f32[384,384]{1,0:T(8,128)S(1)} %get-tuple-element.18, f32[384,384]{1,0:T(8,128)S(1)} %fusion.13), kind=kOutput, calls=%fused_computation.18 | convolution fusion | flops 1812627456 | bytes 5114880 | tf_op jit(solution)/shard_map/spt,tf->spf/dot_general | solution.py:76
  16.7 2.8 %copy.25 = f32[8,64,384]{1,0,2:T(8,128)} copy(f32[8,64,384]{2,1,0:T(8,128)} %get-tuple-element.21) | data formatting | bytes 1572864 | tf_op jit(solution)/shard_map/slice | solution.py:47
  19.4 3.8 %convolution_bitcast_fusion = f32[8,64,768]{2,1,0:T(8,128)S(1)} fusion(f32[8,64,384]{2,1,0:T(8,128)} %param.9, f32[384,384]{1,0:T(8,128)S(1)} %get-tuple-element.18, f32[384,384]{1,0:T(8,128)S(1)} %fusion.13), kind=kOutput, calls=%fused_computation.9 | convolution fusion | flops 1812234240 | bytes 3538944 | tf_op jit(solution)/shard_map/kpt,tf->kpf/dot_general | solution.py:77
  24.6 2.8 %copy.26 = f32[8,64,384]{1,0,2:T(8,128)} copy(f32[8,64,384]{2,1,0:T(8,128)} %get-tuple-element.12) | data formatting | bytes 1572864 | tf_op jit(solution)/shard_map/slice | solution.py:46
  27.4 2.8 %copy.24 = f32[8,64,384]{1,0,2:T(8,128)} copy(f32[8,64,384]{2,1,0:T(8,128)} %get-tuple-element.11) | data formatting | bytes 1572864 | tf_op jit(solution)/shard_map/slice | solution.py:46
  30.2 5.8 %fusion.50 = f32[384,8,8]{2,1,0:T(8,128)} fusion(f32[8,64,384]{1,0,2:T(8,128)} %copy.25, f32[8,64,384]{1,0,2:T(8,128)} %copy.26), kind=kOutput, calls=%fused_computation.86 | convolution fusion | flops 18874368 | bytes 1671168 | tf_op jit(solution)/shard_map/kpf,spf->ksf/dot_general | solution.py:49
  36.1 4.0 %fusion.51 = f32[384,8,8]{2,1,0:T(8,128)} fusion(f32[8,64,384]{1,0,2:T(8,128)S(1)} %copy-done.7, f32[8,64,384]{1,0,2:T(8,128)S(1)} %copy-done.8), kind=kOutput, calls=%fused_computation.87 | convolution fusion | flops 18874368 | bytes 1671168 | tf_op jit(solution)/shard_map/kpf,spf->ksf/dot_general | solution.py:50
  40.1 2.9 %copy.23 = f32[8,64,384]{1,0,2:T(8,128)} copy(f32[8,64,384]{2,1,0:T(8,128)} %get-tuple-element.22) | data formatting | bytes 1572864 | tf_op jit(solution)/shard_map/slice | solution.py:47
  43.0 6.4 %subtract_bitcast_fusion.1 = f32[8,8,384]{0,1,2:T(8,128)} fusion(f32[384,8,8]{2,1,0:T(8,128)} %fusion.50, f32[8,64,384]{1,0,2:T(8,128)} %copy.23, f32[8,64,384]{1,0,2:T(8,128)} %copy.24, f32[384]{0:T(512)S(1)} %fusion.37), kind=kOutput, calls=%fused_computation.8 | convolution fusion | flops 18923520 | bytes 1771008 | tf_op jit(solution)/shard_map/kpf,spf->ksf/dot_general | solution.py:48
  49.4 4.4 %add_bitcast_fusion.1 = f32[8,8,384]{0,1,2:T(8,128)} fusion(f32[384,8,8]{2,1,0:T(8,128)S(1)} %copy-done.4, f32[384,8,8]{2,1,0:T(8,128)S(1)} %copy-done.10, f32[8,64,384]{1,0,2:T(8,128)S(1)} %copy-done.5, f32[8,64,384]{1,0,2:T(8,128)S(1)} %copy-done.3, f32[384]{0:T(512)S(1)} %broadcast_subtract_fusion, f32[384]{0:T(512)S(1)} %fusion.37), kind=kOutput, calls=%fused_computation.7 | convolution fusion | flops 18972672 | bytes 1870848 | tf_op jit(solution)/shard_map/kpf,spf->ksf/dot_general | solution.py:51
  65.4 2.8 %copy.35 = f32[8,64,384]{1,0,2:T(8,128)} copy(f32[8,64,384]{2,1,0:T(8,128)} %get-tuple-element.8) | data formatting | bytes 1572864 | tf_op jit(solution)/shard_map/slice | solution.py:47
  68.2 2.8 %copy.33 = f32[8,64,384]{1,0,2:T(8,128)} copy(f32[8,64,384]{2,1,0:T(8,128)} %get-tuple-element.7) | data formatting | bytes 1572864 | tf_op jit(solution)/shard_map/slice | solution.py:47
  73.2 95.8 %all-reduce.2.cloned.1.call-done = f32[64,384]{1,0:T(8,128)} async-done(((f32[64,384]{1,0:T(8,128)}), f32[64,384]{1,0:T(8,128)}) %all-reduce.2.cloned.1.call-update) | async-done | bytes 98320 | tf_op jit(solution)/shard_map/psum | solution.py:81
  169.0 3.4 %fusion.23 = f32[64,4,384]{2,0,1:T(8,128)S(1)} fusion(f32[4,384,384]{2,1,0:T(8,128)S(1)} %copy-done, f32[64,384]{1,0:T(8,128)} %all-reduce.2.cloned.1.call-done), kind=kOutput, calls=%fused_computation.43 | convolution fusion | flops 452984832 | bytes 2850816 | tf_op jit(solution)/shard_map/rt,but->rbu/dot_general | solution.py:67
  177.9 4.8 %fusion.52 = f32[384,64,8]{1,2,0:T(8,128)S(1)} fusion(f32[8,64,384]{1,0,2:T(8,128)} %copy.35, f32[8,8,384]{1,0,2:T(8,128)} %copy.36), kind=kOutput, calls=%fused_computation.88 | convolution fusion | flops 18874368 | bytes 1671168 | tf_op jit(solution)/shard_map/ksf,spf->kpf/dot_general | solution.py:49
  182.7 2.8 %fusion.53 = f32[384,64,8]{1,2,0:T(8,128)S(1)} fusion(f32[8,64,384]{1,0,2:T(8,128)S(1)} %copy-done.6, f32[8,8,384]{1,0,2:T(8,128)S(1)} %copy-done.9), kind=kOutput, calls=%fused_computation.89 | convolution fusion | flops 18874368 | bytes 1671168 | tf_op jit(solution)/shard_map/ksf,spf->kpf/dot_general | solution.py:50
  185.5 3.1 %subtract_bitcast_fusion = f32[8,64,384]{1,0,2:T(8,128)S(1)} fusion(f32[384,64,8]{1,2,0:T(8,128)S(1)} %fusion.52, f32[8,64,384]{1,0,2:T(8,128)S(1)} %copy-done.1, f32[8,8,384]{1,0,2:T(8,128)S(1)} %copy-done.9, f32[384]{0:T(512)S(1)} %fusion.37), kind=kOutput, calls=%fused_computation.6 | convolution fusion | flops 19267584 | bytes 2459136 | tf_op jit(solution)/shard_map/ksf,spf->kpf/dot_general | solution.py:48
  188.7 3.5 %add_bitcast_fusion = f32[8,64,384]{1,0,2:T(8,128)S(1)} fusion(f32[384,64,8]{1,2,0:T(8,128)S(1)} %fusion.52, f32[384,64,8]{1,2,0:T(8,128)S(1)} %fusion.53, f32[8,64,384]{1,0,2:T(8,128)S(1)} %copy-done.1, f32[8,8,384]{1,0,2:T(8,128)S(1)} %copy-done.2, f32[384]{0:T(512)S(1)} %broadcast_subtract_fusion, f32[384]{0:T(512)S(1)} %fusion.37), kind=kOutput, calls=%fused_computation.5 | convolution fusion | flops 19660800 | bytes 3247104 | tf_op jit(solution)/shard_map/ksf,spf->kpf/dot_general | solution.py:51
  194.0 3.3 %copy.41 = f32[8,64,768]{2,1,0:T(8,128)} copy(f32[8,64,768]{1,0,2:T(8,128)} %pad_maximum_fusion) | data formatting | bytes 3145728 | tf_op jit(solution)/shard_map/concatenate | solution.py:55
  198.3 3.6 %collective-permute-start = (f32[4,16,384]{2,1,0:T(8,128)S(1)}, f32[4,16,384]{2,1,0:T(8,128)S(1)}, u32[]{:S(2)}, u32[]{:S(2)}) collective-permute-start(f32[4,16,384]{2,1,0:T(8,128)S(1)} %get-tuple-element.13), channel_id=1, source_target_pairs={{0,1},{1,2},{2,3},{3,4},{4,5},{5,6},{6,7},{7,8},{8,9},{9,10},{10,1... | collective-permute-start | bytes 294920 | tf_op jit(solution)/shard_map/ppermute | solution.py:19
  206.3 3.9 %collective-permute-done.1 = f32[4,16,384]{2,1,0:T(8,128)S(1)} collective-permute-done((f32[4,16,384]{2,1,0:T(8,128)S(1)}, f32[4,16,384]{2,1,0:T(8,128)S(1)}, u32[]{:S(2)}, u32[]{:S(2)}) %collective-permute-start.1) | collective-permute-done | bytes 98336 | tf_op jit(solution)/shard_map/ppermute | solution.py:22
  213.3 2.9 %fusion.1 = f32[4,64,384]{2,0,1:T(4,128)} fusion(f32[4,64,4,384]{3,2,1,0:T(4,128)} %bitcast.73, f32[4,64,384]{2,0,1:T(4,128)} %copy.42, f32[4,64]{1,0:T(4,128)S(1)} %copy-done.17, pred[4,64]{1,0:T(4,128)(4,1)S(1)} %get-tuple-element.5), kind=kLoop, calls=%fused_computation.4 | loop fusion | flops 1474560 | bytes 2360576 | tf_op jit(solution)/shard_map/reduce_sum | solution.py:100
  216.2 3.6 %convolution_add_fusion = f32[4,64,384]{2,1,0:T(8,128)} fusion(f32[4,64,768]{2,1,0:T(8,128)} %reduce-scatter.2.cloned.1.call-done, f32[384,384]{1,0:T(8,128)} %get-tuple-element.17, f32[384,384]{1,0:T(8,128)S(1)} %copy-done.12, f32[4,64,384]{2,0,1:T(4,128)} %fusion.1, f32[4,64,384]{2,1,0:T(8,128)S(1)} %constant_dynamic-slice_fusion.2, f32[64]{0:T(128)S(1)} %copy-done.18), kind=kOutput, calls=%fused_computation.11 | convolution fusion | flops 906854400 | bytes 3145984 | tf_op jit(solution)/shard_map/kpf,ft->kpt/dot_general | solution.py:92
  (80 shorter events, 34.9 us)
Async XLA Ops:
  6.5 162.5 %copy-start = (f32[4,384,384]{2,1,0:T(8,128)S(1)}, f32[4,384,384]{2,1,0:T(8,128)}, u32[]{:S(2)}) copy-start(f32[4,384,384]{2,1,0:T(8,128)} %param.12) | copy-start | bytes 7077892
  6.5 162.5 %all-reduce.2.cloned.1.call-start = ((), (), s32[]{:S(2)}) async-start(), calls=%async_computation.1 | async-start | bytes 196608 | tf_op jit(solution)/shard_map/psum | solution.py:81
  6.5 5.6 %copy-start.13 = (f32[8,64,384]{2,1,0:T(8,128)S(1)}, f32[8,64,384]{2,1,0:T(8,128)}, u32[]{:S(2)}) copy-start(f32[8,64,384]{2,1,0:T(8,128)} %param.8) | copy-start | bytes 2359300
  30.2 5.9 %copy-start.7 = (f32[8,64,384]{1,0,2:T(8,128)S(1)}, f32[8,64,384]{1,0,2:T(8,128)}, u32[]{:S(2)}) copy-start(f32[8,64,384]{1,0,2:T(8,128)} %copy.25) | copy-start | bytes 2359300
  30.2 5.9 %copy-start.8 = (f32[8,64,384]{1,0,2:T(8,128)S(1)}, f32[8,64,384]{1,0,2:T(8,128)}, u32[]{:S(2)}) copy-start(f32[8,64,384]{1,0,2:T(8,128)} %copy.24) | copy-start | bytes 2359300
  43.0 6.4 %copy-start.3 = (f32[8,64,384]{1,0,2:T(8,128)S(1)}, f32[8,64,384]{1,0,2:T(8,128)}, u32[]{:S(2)}) copy-start(f32[8,64,384]{1,0,2:T(8,128)} %copy.26) | copy-start | bytes 2359300
  43.0 6.4 %copy-start.4 = (f32[384,8,8]{2,1,0:T(8,128)S(1)}, f32[384,8,8]{2,1,0:T(8,128)}, u32[]{:S(2)}) copy-start(f32[384,8,8]{2,1,0:T(8,128)} %fusion.50) | copy-start | bytes 294916
  43.0 6.4 %copy-start.5 = (f32[8,64,384]{1,0,2:T(8,128)S(1)}, f32[8,64,384]{1,0,2:T(8,128)}, u32[]{:S(2)}) copy-start(f32[8,64,384]{1,0,2:T(8,128)} %copy.23) | copy-start | bytes 2359300
  43.0 6.4 %copy-start.10 = (f32[384,8,8]{2,1,0:T(8,128)S(1)}, f32[384,8,8]{2,1,0:T(8,128)}, u32[]{:S(2)}) copy-start(f32[384,8,8]{2,1,0:T(8,128)} %fusion.51) | copy-start | bytes 294916
  64.5 151.7 %reduce-scatter.2.cloned.1.call-start = ((), (), s32[]{:S(2)}) async-start(), calls=%async_computation.2 | async-start | bytes 2359296 | tf_op jit(solution)/shard_map/reduce_scatter | solution.py:91
  68.2 2.8 %copy-start.19 = (s32[8]{0:T(128)S(1)}, s32[8]{0:T(128)}, u32[]{:S(2)}) copy-start(s32[8]{0:T(128)} %param.11) | copy-start | bytes 100
  68.2 4.2 %copy-start.20 = (f32[8]{0:T(128)S(1)}, f32[8]{0:T(128)}, u32[]{:S(2)}) copy-start(f32[8]{0:T(128)} %param.10) | copy-start | bytes 100
  169.0 3.4 %copy-start.15 = (f32[64,4]{1,0:T(8,128)S(1)}, f32[64,4]{1,0:T(8,128)}, u32[]{:S(2)}) copy-start(f32[64,4]{1,0:T(8,128)} %fusion.27) | copy-start | bytes 3076
  169.0 4.6 %copy-start.14 = (f32[64,384]{1,0:T(8,128)S(1)}, f32[64,384]{1,0:T(8,128)}, u32[]{:S(2)}) copy-start(f32[64,384]{1,0:T(8,128)} %all-reduce.2.cloned.1.call-done) | copy-start | bytes 294916
  177.9 4.8 %copy-start.6 = (f32[8,64,384]{1,0,2:T(8,128)S(1)}, f32[8,64,384]{1,0,2:T(8,128)}, u32[]{:S(2)}) copy-start(f32[8,64,384]{1,0,2:T(8,128)} %copy.35) | copy-start | bytes 2359300
  177.9 4.8 %copy-start.9 = (f32[8,8,384]{1,0,2:T(8,128)S(1)}, f32[8,8,384]{1,0,2:T(8,128)}, u32[]{:S(2)}) copy-start(f32[8,8,384]{1,0,2:T(8,128)} %copy.34) | copy-start | bytes 294916
  182.7 2.8 %copy-start.1 = (f32[8,64,384]{1,0,2:T(8,128)S(1)}, f32[8,64,384]{1,0,2:T(8,128)}, u32[]{:S(2)}) copy-start(f32[8,64,384]{1,0,2:T(8,128)} %copy.33) | copy-start | bytes 2359300
  185.5 3.1 %copy-start.2 = (f32[8,8,384]{1,0,2:T(8,128)S(1)}, f32[8,8,384]{1,0,2:T(8,128)}, u32[]{:S(2)}) copy-start(f32[8,8,384]{1,0,2:T(8,128)} %copy.36) | copy-start | bytes 294916
  197.3 6.9 %copy-start.16 = (s32[4,64]{1,0:T(4,128)S(1)}, s32[4,64]{1,0:T(4,128)}, u32[]{:S(2)}) copy-start(s32[4,64]{1,0:T(4,128)} %param.15) | copy-start | bytes 3076
  198.3 8.0 %collective-permute-start = (f32[4,16,384]{2,1,0:T(8,128)S(1)}, f32[4,16,384]{2,1,0:T(8,128)S(1)}, u32[]{:S(2)}, u32[]{:S(2)}) collective-permute-start(f32[4,16,384]{2,1,0:T(8,128)S(1)} %get-tuple-element.13), channel_id=1, source_target_pairs={{0,1},{1,2},{2,3},{3,4},{4,5},{5,6},{6,7},{7,8},{8,9},{9,10},{10,1... | collective-permute-start | bytes 294920 | tf_op jit(solution)/shard_map/ppermute | solution.py:19
  201.9 8.3 %collective-permute-start.1 = (f32[4,16,384]{2,1,0:T(8,128)S(1)}, f32[4,16,384]{2,1,0:T(8,128)S(1)}, u32[]{:S(2)}, u32[]{:S(2)}) collective-permute-start(f32[4,16,384]{2,1,0:T(8,128)S(1)} %get-tuple-element.14), channel_id=1, source_target_pairs={{1,0},{2,1},{3,2},{4,3},{5,4},{6,5},{7,6},{8,7},{9,8},{10,9},{11,1... | collective-permute-start | bytes 294920 | tf_op jit(solution)/shard_map/ppermute | solution.py:22
  210.6 2.7 %copy-start.17 = (f32[4,64]{1,0:T(4,128)S(1)}, f32[4,64]{1,0:T(4,128)}, u32[]{:S(2)}) copy-start(f32[4,64]{1,0:T(4,128)} %param.14) | copy-start | bytes 3076
  213.3 2.9 %copy-start.12 = (f32[384,384]{1,0:T(8,128)S(1)}, f32[384,384]{1,0:T(8,128)}, u32[]{:S(2)}) copy-start(f32[384,384]{1,0:T(8,128)} %copy-done.11) | copy-start | bytes 1769476
  213.3 2.9 %copy-start.18 = (f32[64]{0:T(128)S(1)}, f32[64]{0:T(128)}, u32[]{:S(2)}) copy-start(f32[64]{0:T(128)} %param.13) | copy-start | bytes 772
  (1 other events, 0.8 us)
Sparse Core Ops, SparseCore 0:
  64.6 104.4 all-reduce.1
  197.4 9.2 reduce-scatter.1
where the time goes:
time: 231 us; the launch traced here: 227 us
  waiting for transfers between devices  99.7 us (43%)
  matrix products  55.2 us (24%)
  local copies, waits for them, and re-layouts  38.6 us (17%)
  between operations  13.9 us (6%)
  other arithmetic  13.1 us (6%)
  starting transfers between devices  6.29 us (3%)
    psum x1, waiting for transfers between devices, local(): predicted = lax.psum(flat, 'pts')  95.8 us
    slice x5, local copies, waits for them, and re-layouts, spectral(): right_x, right_y = (right[..., :half], right[..., half:])  13 us
    dot_general x2, matrix products, spectral(): prod_yy = jnp.einsum(form, left_y, right_y, precision=HIGHEST)  10.6 us
    slice x6, local copies, waits for them, and re-layouts, spectral(): left_x, left_y = (left[..., :half], left[..., half:])  10.3 us
    dot_general x2, matrix products, spectral(): prod_xx = jnp.einsum(form, left_x, right_x, precision=HIGHEST)  9.51 us
    dot_general x2, matrix products, spectral(): prod_yx = jnp.einsum(form, left_y, right_x, precision=HIGHEST)  7.87 us
    dot_general x2, matrix products, spectral(): prod_xy = jnp.einsum(form, left_x, right_y, precision=HIGHEST)  6.8 us
  transfers between devices with their start and end apart: 4, of which 2 were waited for; matrix products, arithmetic and copies ran while one was open for 8% of the time, Pallas kernels for 0%

commit v1 on v0

v1 whole, which is shorter than its diff:
```python
import functools
import math

import jax
import jax.numpy as jnp
import ml_dtypes
import numpy as np
from jax import lax
from jax.experimental import pallas as pl
from jax.experimental.pallas import tpu as pltpu
from jax.sharding import PartitionSpec as P

COLS = 16
LANES = 128
SUB = 8
F32 = jnp.float32
BF16 = jnp.bfloat16
NT_DIMS = (((1,), (1,)), ((), ()))


def dft_table(length):
    steps = np.arange(length, dtype=np.int64)
    phase = (steps[:, None] * (2 * steps[None, :] + 1)) % (4 * length)
    angle = phase.astype(np.float64) * (2.0 * math.pi / (4 * length))
    table = np.concatenate([np.cos(angle), -np.sin(angle)], axis=1)
    high = table.astype(ml_dtypes.bfloat16)
    low = (table - high.astype(np.float64)).astype(ml_dtypes.bfloat16)
    return np.concatenate([high, low], axis=0)


def split(x):
    high = x.astype(BF16)
    return high, (x - high.astype(F32)).astype(BF16)


def dot(a, b):
    return jnp.dot(a, b, preferred_element_type=F32)


def dot_nt(a, b):
    return lax.dot_general(a, b, NT_DIMS, preferred_element_type=F32)


def dft(high, low, table_ref, length):
    return dot(high, table_ref[:length]) + dot(high, table_ref[length:]) + dot(low, table_ref[:length])


def inverse_dft(high, low, table_ref, length):
    return (
        dot_nt(high, table_ref[:length])
        + dot_nt(high, table_ref[length:])
        + dot_nt(low, table_ref[:length])
    )


def forward_kernel(
    shift_ref, kern_ref, vec_ref, table_ref, pred_ref, khat_ref, vhat_ref, high_ref, low_ref, spec_ref
):
    sensors, points, length = kern_ref.shape
    count = vec_ref.shape[0]
    shift = shift_ref[0]
    cols = length // LANES

    def load_kern(s, _):
        rows = pl.ds(pl.multiple_of(s * points, points), points)
        high_ref[rows], low_ref[rows] = split(kern_ref[s])
        return 0

    def load_vec(k, _):
        rows = pl.ds(pl.multiple_of(k * points, points), points)
        high_ref[rows], low_ref[rows] = split(vec_ref[lax.rem(k + shift, count)])
        return 0

    lax.fori_loop(0, sensors, load_kern, 0)
    rows = sensors * points
    hat = dft(high_ref[:rows], low_ref[:rows], table_ref, length)
    real, imag = hat[:, :length], hat[:, length:]
    khat_ref[0] = real
    khat_ref[1] = imag - real
    khat_ref[2] = imag + real

    lax.fori_loop(0, count, load_vec, 0)
    rows = count * points
    hat = dft(high_ref[:rows], low_ref[:rows], table_ref, length)
    real, imag = hat[:, :length], hat[:, length:]
    vhat_ref[0] = real + imag
    vhat_ref[1] = real
    vhat_ref[2] = imag

    k_block, s_block = 2, sensors // 2
    sub_iota = lax.broadcasted_iota(jnp.int32, (sensors, LANES), 0)

    def product(step, _):
        k0 = step // cols * k_block
        lanes = pl.ds(pl.multiple_of(step % cols * LANES, LANES), LANES)
        out_re = [jnp.zeros((sensors, LANES), F32) for _ in range(k_block)]
        out_im = [jnp.zeros((sensors, LANES), F32) for _ in range(k_block)]
        for s0 in range(0, sensors, s_block):
            acc = [[[None] * 3 for _ in range(s_block)] for _ in range(k_block)]
            for g in range(points // SUB):
                left = [
                    [
                        vhat_ref[c, pl.ds(pl.multiple_of((k0 + i) * points + g * SUB, SUB), SUB), lanes]
                        for c in range(3)
                    ]
                    for i in range(k_block)
                ]
                for j in range(s_block):
                    right = [
                        khat_ref[c, pl.ds((s0 + j) * points + g * SUB, SUB), lanes] for c in range(3)
                    ]
                    for i in range(k_block):
                        for c in range(3):
                            term = left[i][c] * right[c]
                            acc[i][j][c] = term if acc[i][j][c] is None else acc[i][j][c] + term
            for i in range(k_block):
                for j in range(s_block):
                    one, two, three = acc[i][j]
                    re = jnp.sum(one - three, axis=0, keepdims=True)
                    im = jnp.sum(one + two, axis=0, keepdims=True)
                    out_re[i] = jnp.where(sub_iota == s0 + j, re, out_re[i])
                    out_im[i] = jnp.where(sub_iota == s0 + j, im, out_im[i])
        for i in range(k_block):
            at = pl.ds(pl.multiple_of((k0 + i) * sensors, sensors), sensors)
            spec_ref[at, lanes] = out_re[i]
            other = pl.ds(pl.multiple_of(step % cols * LANES + length, LANES), LANES)
            spec_ref[at, other] = out_im[i]
        return 0

    lax.fori_loop(0, count // k_block * cols, product, 0)
    high, low = split(spec_ref[...])
    pred_ref[...] = inverse_dft(high, low, table_ref, length) * (1.0 / length)


def forward(shift, kernel, vectors, table):
    sensors, points, length = kernel.shape
    count = vectors.shape[0]
    most = max(sensors, count) * points
    vmem = pl.BlockSpec(memory_space=pltpu.VMEM)
    smem = pl.BlockSpec(memory_space=pltpu.SMEM)
    return pl.pallas_call(
        forward_kernel,
        out_shape=(
            jax.ShapeDtypeStruct((count * sensors, length), F32),
            jax.ShapeDtypeStruct((3, sensors * points, length), F32),
        ),
        in_specs=[smem, vmem, vmem, vmem],
        out_specs=(vmem, vmem),
        scratch_shapes=[
            pltpu.VMEM((3, count * points, length), F32),
            pltpu.VMEM((most, length), BF16),
            pltpu.VMEM((most, length), BF16),
            pltpu.VMEM((count * sensors, 2 * length), F32),
        ],
        compiler_params=pltpu.CompilerParams(vmem_limit_bytes=40 * 1024 * 1024),
    )(shift, kernel, vectors, table)


def adjoint_kernel(
    own,
    pred_ref,
    more_ref,
    scale_ref,
    mask_ref,
    corr_ref,
    khat_ref,
    table_ref,
    prior_ref,
    out_ref,
    rest_ref,
    rhat_ref,
    high_ref,
    low_ref,
):
    groups, length, _ = corr_ref.shape
    rows = pred_ref.shape[0]
    count = high_ref.shape[0] // prior_ref.shape[1]
    points = prior_ref.shape[1]
    sensors = rows // count
    cols = length // LANES
    pred = pred_ref[...] + more_ref[...]
    high, low = split(pred)
    mixed = pred
    for g in range(groups):
        corr_high, corr_low = split(corr_ref[g])
        part = dot_nt(high, corr_high) + dot_nt(high, corr_low) + dot_nt(low, corr_high)
        mixed = mixed + mask_ref[:, g : g + 1] * part
    residual = mixed * scale_ref[:, 0:1]
    high, low = split(residual)
    hat = dft(high, low, table_ref, length)
    real, imag = hat[:, :length], hat[:, length:]
    rhat_ref[0] = jnp.broadcast_to((real + imag)[:, None, :], (rows, SUB, length))
    rhat_ref[1] = jnp.broadcast_to(imag[:, None, :], (rows, SUB, length))
    rhat_ref[2] = jnp.broadcast_to(real[:, None, :], (rows, SUB, length))

    k_block, g_block = 4, 2
    tall = g_block * SUB
    blocks = points // tall

    def product(step, _):
        col = step % cols
        g0 = step // cols % blocks
        k0 = step // (cols * blocks) * k_block
        lanes = pl.ds(pl.multiple_of(col * LANES, LANES), LANES)
        others = pl.ds(pl.multiple_of(col * LANES + length, LANES), LANES)
        acc = [[[None] * 3 for _ in range(g_block)] for _ in range(k_block)]
        for s in range(sensors):
            right = [
                [
                    khat_ref[c, pl.ds(pl.multiple_of(g0 * tall, tall) + s * points + b * SUB, SUB), lanes]
                    for c in range(3)
                ]
                for b in range(g_block)
            ]
            for i in range(k_block):
                left = [rhat_ref[c, (k0 + i) * sensors + s, :, lanes] for c in range(3)]
                for b in range(g_block):
                    for c in range(3):
                        term = left[c] * right[b][c]
                        acc[i][b][c] = term if acc[i][b][c] is None else acc[i][b][c] + term
        for i in range(k_block):
            re = jnp.concatenate([one + two for one, two, _ in acc[i]], axis=0)
            im = jnp.concatenate([one - three for one, _, three in acc[i]], axis=0)
            at = pl.ds(pl.multiple_of((k0 + i) * points + g0 * tall, tall), tall)
            high_ref[at, lanes], low_ref[at, lanes] = split(re)
            high_ref[at, others], low_ref[at, others] = split(im)
        return 0

    lax.fori_loop(0, count // k_block * blocks * cols, product, 0)
    data = inverse_dft(high_ref[...], low_ref[...], table_ref, length)
    data = data.reshape(count, points, length)
    out_ref[...] = data[:own] + prior_ref[...]
    rest_ref[...] = data[own:]


def adjoint(pred, more, scale, mask, correlation, khat, table, prior, count):
    rows, length = pred.shape
    own, points, _ = prior.shape
    vmem = pl.BlockSpec(memory_space=pltpu.VMEM)
    return pl.pallas_call(
        functools.partial(adjoint_kernel, own),
        out_shape=(
            jax.ShapeDtypeStruct((own, points, length), F32),
            jax.ShapeDtypeStruct((count - own, points, length), F32),
        ),
        in_specs=[vmem] * 8,
        out_specs=(vmem, vmem),
        scratch_shapes=[
            pltpu.VMEM((3, rows, SUB, length), F32),
            pltpu.VMEM((count * points, 2 * length), BF16),
            pltpu.VMEM((count * points, 2 * length), BF16),
        ],
        compiler_params=pltpu.CompilerParams(vmem_limit_bytes=40 * 1024 * 1024),
    )(pred, more, scale, mask, correlation, khat, table, prior)


def prior_kernel(shift_ref, base_ref, vec_ref, low_ref, high_ref, stiff_ref, coup_ref, near_ref, out_ref):
    own, points, _ = out_ref.shape
    halo = low_ref.shape[1]
    count = vec_ref.shape[0]
    span = points + 2 * halo
    place = lax.broadcasted_iota(jnp.int32, (span, points), 0)
    coup = coup_ref[...]
    here = lax.broadcasted_iota(jnp.int32, (span, points), 1) + halo
    diagonal = stiff_ref[...] + jnp.sum(coup, axis=0, keepdims=True)
    weight = jnp.where(place == here, diagonal, 0.0)
    near = near_ref[...] - base_ref[0]
    for j in range(coup.shape[0]):
        weight = weight - jnp.where(place == near[j : j + 1], coup[j : j + 1], 0.0)
    weight_high, weight_low = split(weight.T)
    for k in range(own):
        value = jnp.concatenate(
            [low_ref[k], vec_ref[lax.rem(shift_ref[0] + k, count)], high_ref[k]], axis=0
        )
        high, low = split(value)
        out_ref[k] = dot(weight_high, high) + dot(weight_high, low) + dot(weight_low, high)


def prior_term(shift, base, vectors, low, high, stiffness, couplings, neighbors):
    own = low.shape[0]
    _, points, length = vectors.shape
    vmem = pl.BlockSpec(memory_space=pltpu.VMEM)
    smem = pl.BlockSpec(memory_space=pltpu.SMEM)
    return pl.pallas_call(
        prior_kernel,
        out_shape=jax.ShapeDtypeStruct((own, points, length), F32),
        in_specs=[smem, smem] + [vmem] * 6,
        out_specs=vmem,
        compiler_params=pltpu.CompilerParams(vmem_limit_bytes=40 * 1024 * 1024),
    )(shift, base, vectors, low, high, stiffness[None], couplings, neighbors)


def butterfly_masks(size):
    masks = [1 << bit for bit in range(size.bit_length() - 1)]
    order = []
    while masks:
        order.append(masks.pop(0))
        if masks:
            order.append(masks.pop())
    swapped = list(order)
    for i in range(0, len(order) - 1, 2):
        swapped[i], swapped[i + 1] = order[i + 1], order[i]
    return order, swapped


def local(table, kernel, vectors, noise_scale, sensor_group, correlation, stiffness, couplings, neighbors):
    sensors, points, length = kernel.shape
    count = vectors.shape[0]
    n_sens, n_pts = lax.axis_size("sens"), lax.axis_size("pts")
    sens, pts = lax.axis_index("sens"), lax.axis_index("pts")
    own = count // n_sens
    shift = (sens * own).reshape(1)

    pred, khat = forward(shift, kernel, vectors, table)

    own_vectors = lax.dynamic_slice_in_dim(vectors, sens * own, own, 0)
    ahead = [(i, i + 1) for i in range(n_pts - 1)]
    behind = [(i + 1, i) for i in range(n_pts - 1)]
    low = lax.ppermute(own_vectors[:, points - COLS :], "pts", ahead)
    high = lax.ppermute(own_vectors[:, :COLS], "pts", behind)
    base = (pts * points - COLS).reshape(1)
    prior = prior_term(shift, base, vectors, low, high, stiffness, couplings, neighbors)

    more = jnp.zeros_like(pred)
    even, odd = butterfly_masks(n_pts)
    for step, (mask_even, mask_odd) in enumerate(zip(even, odd)):
        pairs = [
            (s * n_pts + p, s * n_pts + (p ^ (mask_odd if s % 2 else mask_even)))
            for s in range(n_sens)
            for p in range(n_pts)
        ]
        if step:
            pred = pred + more
        more = lax.ppermute(pred, ("sens", "pts"), pairs)

    row_scale = jnp.tile(noise_scale * (1.0 / length), count)[:, None]
    groups = correlation.shape[0]
    row_mask = (jnp.tile(sensor_group, count)[:, None] == jnp.arange(groups)[None, :]).astype(F32)
    total, rest = adjoint(pred, more, row_scale, row_mask, correlation, khat, table, prior, count)
    for j in range(1, n_sens):
        pairs = [(s, (s + j) % n_sens) for s in range(n_sens)]
        total = total + lax.ppermute(rest[(j - 1) * own : j * own], "sens", pairs)
    return total


def solution(mesh):
    in_specs = (
        P(),
        P("sens", "pts", None),
        P(None, "pts", None),
        P("sens"),
        P("sens"),
        P(),
        P("pts"),
        P(None, "pts"),
        P(None, "pts"),
    )
    out_specs = P("sens", "pts", None)
    mapped = jax.shard_map(local, mesh=mesh, in_specs=in_specs, out_specs=out_specs, check_vma=False)

    def run(kernel, *rest):
        return mapped(jnp.asarray(dft_table(kernel.shape[-1])), kernel, *rest)

    return run
```

time: 231 us -> 50.7 us (0.22)
  the two profiles are of different devices: /device:TPU:6 before, /device:TPU:3 now
where the time goes in v1:
time: 50.7 us; the launch traced here: 49.7 us
  starting transfers between devices  17.9 us (35%)
  Pallas kernels  13.9 us (27%)
  local copies, waits for them, and re-layouts  8.55 us (17%)
  waiting for transfers between devices  8.25 us (16%)
  other arithmetic  0.9 us (2%)
    unnamed x26, local copies, waits for them, and re-layouts  8.37 us
    pallas_call x1, Pallas kernels, forward(): pl.pallas_call(forward_kernel, out_shape=(jax.ShapeDtypeStruct((count * s...  7.98 us
    ppermute x4, waiting for transfers between devices, local(): more = lax.ppermute(pred, ('sens', 'pts'), pairs)  6.89 us
    ppermute x4, starting transfers between devices, local(): more = lax.ppermute(pred, ('sens', 'pts'), pairs)  6.62 us
    pallas_call x1, Pallas kernels, adjoint(): pl.pallas_call(functools.partial(adjoint_kernel, own), out_shape=(jax.Sha...  5.56 us
    ppermute x1, starting transfers between devices, local(): total = total + lax.ppermute(rest[(j - 1) * own:j * own], 'sens', pairs)  5.15 us
    ppermute x1, starting transfers between devices, local(): high = lax.ppermute(own_vectors[:, :COLS], 'pts', behind)  3.19 us
    ppermute x1, starting transfers between devices, local(): low = lax.ppermute(own_vectors[:, points - COLS:], 'pts', ahead)  2.99 us
  transfers between devices with their start and end apart: 7, of which 4 were waited for; matrix products, arithmetic and copies ran while one was open for 1% of the time, Pallas kernels for 1%

profile of v1, /device:TPU:3, one launch (start us, length us, event | category | flops | bytes accessed | tf_op | source)
XLA Modules:
  0.0 49.7 jit_solution(9593386579042236533)
XLA Ops:
  0.0 1.3 %copy-done = bf16[768,768]{1,0:T(8,128)(2,1)S(1)} copy-done((bf16[768,768]{1,0:T(8,128)(2,1)S(1)}, bf16[768,768]{1,0:T(8,128)(2,1)}, u32[]{:S(2)}) %copy-start) | copy-done | bytes 1179672
  1.4 1.1 %copy-done.2 = f32[8,64,384]{2,1,0:T(8,128)S(1)} copy-done((f32[8,64,384]{2,1,0:T(8,128)S(1)}, f32[8,64,384]{2,1,0:T(8,128)}, u32[]{:S(2)}) %copy-start.2) | copy-done | bytes 786456
  2.5 1.1 %copy-done.7 = f32[8,64,384]{2,1,0:T(8,128)S(1)} copy-done((f32[8,64,384]{2,1,0:T(8,128)S(1)}, f32[8,64,384]{2,1,0:T(8,128)}, u32[]{:S(2)}) %copy-start.7) | copy-done | bytes 786456
  3.6 8.0 %shard_map.91 = (f32[64,384]{1,0:T(8,128)S(1)}, f32[3,512,384]{2,1,0:T(8,128)S(1)}) custom-call(s32[1]{0:T(128)} %bitcast.shift_ref, f32[8,64,384]{2,1,0:T(8,128)S(1)} %copy-done.7, f32[8,64,384]{2,1,0:T(8,128)S(1)} %copy-done.2, bf16[768,768]{1,0:T(8,128)(2,1)S(1)} %copy-done), custom_call_target="tpu_custom_call" | custom-call | tf_op jit(solution)/shard_map/pallas_call | solution.py:141
  11.6 1.4 %copy-done.5 = f32[3,512,384]{2,1,0:T(8,128)} copy-done((f32[3,512,384]{2,1,0:T(8,128)}, f32[3,512,384]{2,1,0:T(8,128)S(1)}, u32[]{:S(2)}) %copy-start.5) | copy-done | bytes 2359320
  13.1 2.3 %collective-permute-start = (f32[64,384]{1,0:T(8,128)S(1)}, f32[64,384]{1,0:T(8,128)S(1)}, u32[]{:S(2)}, u32[]{:S(2)}) collective-permute-start(f32[64,384]{1,0:T(8,128)S(1)} %get-tuple-element.9), channel_id=1, source_target_pairs={{0,1},{1,0},{2,3},{3,2},{4,5},{5,4},{6,7},{7,6},{8,9},{9,8},{10,11... | collective-permute-start | bytes 294920 | tf_op jit(solution)/shard_map/ppermute | solution.py:334
  15.4 2.1 %collective-permute-done = f32[64,384]{1,0:T(8,128)S(1)} collective-permute-done((f32[64,384]{1,0:T(8,128)S(1)}, f32[64,384]{1,0:T(8,128)S(1)}, u32[]{:S(2)}, u32[]{:S(2)}) %collective-permute-start) | collective-permute-done | bytes 98336 | tf_op jit(solution)/shard_map/ppermute | solution.py:334
  17.4 0.3 collective-permute-start.1
  17.7 3.2 %collective-permute-start.5 = (f32[4,16,384]{2,1,0:T(8,128)S(1)}, f32[4,16,384]{2,1,0:T(8,128)S(1)}, u32[]{:S(2)}, u32[]{:S(2)}) collective-permute-start(f32[4,16,384]{2,1,0:T(8,128)S(1)} %get-tuple-element.13), channel_id=1, source_target_pairs={{1,0},{2,1},{3,2},{4,3},{5,4},{6,5},{7,6},{8,7},{9,8},{10,9},{11,1... | collective-permute-start | bytes 294920 | tf_op jit(solution)/shard_map/ppermute | solution.py:320
  20.9 3.0 %collective-permute-start.4 = (f32[4,16,384]{2,1,0:T(8,128)S(1)}, f32[4,16,384]{2,1,0:T(8,128)S(1)}, u32[]{:S(2)}, u32[]{:S(2)}) collective-permute-start(f32[4,16,384]{2,1,0:T(8,128)S(1)} %get-tuple-element.14), channel_id=1, source_target_pairs={{0,1},{1,2},{2,3},{3,4},{4,5},{5,6},{6,7},{7,8},{8,9},{9,10},{10,1... | collective-permute-start | bytes 294920 | tf_op jit(solution)/shard_map/ppermute | solution.py:319
  23.9 0.1 eq.15
  24.0 1.9 %collective-permute-start.2 = (f32[64,384]{1,0:T(8,128)S(1)}, f32[64,384]{1,0:T(8,128)S(1)}, u32[]{:S(2)}, u32[]{:S(2)}) collective-permute-start(f32[64,384]{1,0:T(8,128)S(1)} %add.17), channel_id=1, source_target_pairs={{0,2},{1,3},{2,0},{3,1},{4,6},{5,7},{6,4},{7,5},{8,10},{9,11},{10,... | collective-permute-start | bytes 294920 | tf_op jit(solution)/shard_map/ppermute | solution.py:334
  25.9 0.1 fusion.mask_ref
  26.0 2.2 %collective-permute-done.2 = f32[64,384]{1,0:T(8,128)S(1)} collective-permute-done((f32[64,384]{1,0:T(8,128)S(1)}, f32[64,384]{1,0:T(8,128)S(1)}, u32[]{:S(2)}, u32[]{:S(2)}) %collective-permute-start.2) | collective-permute-done | bytes 98336 | tf_op jit(solution)/shard_map/ppermute | solution.py:334
  28.2 2.2 %collective-permute-start.3 = (f32[64,384]{1,0:T(8,128)S(1)}, f32[64,384]{1,0:T(8,128)S(1)}, u32[]{:S(2)}, u32[]{:S(2)}) collective-permute-start(f32[64,384]{1,0:T(8,128)S(1)} %add.18.pred_ref), channel_id=1, source_target_pairs={{0,4},{1,5},{2,6},{3,7},{4,0},{5,1},{6,2},{7,3},{8,12},{9,13},{10,... | collective-permute-start | bytes 294920 | tf_op jit(solution)/shard_map/ppermute | solution.py:334
  30.4 0.1 broadcast_in_dim_tile.5.scale_ref
  30.6 0.4 shard_map.92.prior_ref
  31.0 2.6 %collective-permute-done.3.more_ref = f32[64,384]{1,0:T(8,128)S(1)} collective-permute-done((f32[64,384]{1,0:T(8,128)S(1)}, f32[64,384]{1,0:T(8,128)S(1)}, u32[]{:S(2)}, u32[]{:S(2)}) %collective-permute-start.3) | collective-permute-done | bytes 98336 | tf_op jit(solution)/shard_map/ppermute | solution.py:334
  33.5 1.7 %copy-done.4 = f32[4,384,384]{2,1,0:T(8,128)S(1)} copy-done((f32[4,384,384]{2,1,0:T(8,128)S(1)}, f32[4,384,384]{2,1,0:T(8,128)}, u32[]{:S(2)}) %copy-start.4) | copy-done | bytes 2359320
  35.2 1.7 %copy-done.6 = f32[3,512,384]{2,1,0:T(8,128)S(1)} copy-done((f32[3,512,384]{2,1,0:T(8,128)S(1)}, f32[3,512,384]{2,1,0:T(8,128)}, u32[]{:S(2)}) %copy-start.6) | copy-done | bytes 2359320
  36.9 5.6 %shard_map.93 = (f32[4,64,384]{2,1,0:T(8,128)S(1)}, f32[4,64,384]{2,1,0:T(8,128)S(1)}) custom-call(f32[64,384]{1,0:T(8,128)S(1)} %add.18.pred_ref, f32[64,384]{1,0:T(8,128)S(1)} %collective-permute-done.3.more_ref, f32[64,1]{1,0:T(8,128)S(1)} %broadcast_in_dim_tile.5.scale_ref, f32[64,4]{1,0:T(8,128)S(1)} %fusion.mask_ref, f32[4,384,384]{2,1,0:T(8,128)S(1)} %copy-done.4, ...), custom_call_target="tpu_custom_call" | custom-call | tf_op jit(solution)/shard_map/pallas_call | solution.py:240
  42.4 5.2 %collective-permute-start.6 = (f32[4,64,384]{2,1,0:T(8,128)S(1)}, f32[4,64,384]{2,1,0:T(8,128)S(1)}, u32[]{:S(2)}, u32[]{:S(2)}) collective-permute-start(f32[4,64,384]{2,1,0:T(8,128)S(1)} %get-tuple-element.12), channel_id=1, source_target_pairs={{0,16},{16,0},{1,17},{17,1},{2,18},{18,2},{3,19},{19,3},{4,20},{20... | collective-permute-start | bytes 1179656 | tf_op jit(solution)/shard_map/ppermute | solution.py:342
  47.6 1.3 %collective-permute-done.6 = f32[4,64,384]{2,1,0:T(8,128)S(1)} collective-permute-done((f32[4,64,384]{2,1,0:T(8,128)S(1)}, f32[4,64,384]{2,1,0:T(8,128)S(1)}, u32[]{:S(2)}, u32[]{:S(2)}) %collective-permute-start.6) | collective-permute-done | bytes 393248 | tf_op jit(solution)/shard_map/ppermute | solution.py:342
  48.9 0.8 %add.20 = f32[4,64,384]{2,1,0:T(8,128)} add(f32[4,64,384]{2,1,0:T(8,128)S(1)} %get-tuple-element.11, f32[4,64,384]{2,1,0:T(8,128)S(1)} %collective-permute-done.6) | non-fusion elementwise | flops 98304 | bytes 1179648 | tf_op jit(solution)/shard_map/add | solution.py:342
  (30 shorter events, 0.1 us)
Async XLA Ops:
  0.0 23.9 %copy-start.11 = (s32[8]{0:T(128)S(1)}, s32[8]{0:T(128)}, u32[]{:S(2)}) copy-start(s32[8]{0:T(128)} %param.12) | copy-start | bytes 100
  0.0 30.4 %copy-start.12 = (f32[8]{0:T(128)S(1)}, f32[8]{0:T(128)}, u32[]{:S(2)}) copy-start(f32[8]{0:T(128)} %param.11) | copy-start | bytes 100
  0.0 30.5 %copy-start.9 = (s32[4,64]{1,0:T(4,128)S(1)}, s32[4,64]{1,0:T(4,128)}, u32[]{:S(2)}) copy-start(s32[4,64]{1,0:T(4,128)} %near_ref.1) | copy-start | bytes 3076
  0.0 30.5 %copy-start.8 = (f32[4,64]{1,0:T(4,128)S(1)}, f32[4,64]{1,0:T(4,128)}, u32[]{:S(2)}) copy-start(f32[4,64]{1,0:T(4,128)} %coup_ref.1) | copy-start | bytes 3076
  0.0 30.5 %copy-start.10 = (f32[64]{0:T(128)S(1)}, f32[64]{0:T(128)}, u32[]{:S(2)}) copy-start(f32[64]{0:T(128)} %param.14) | copy-start | bytes 772
  0.0 1.3 %copy-start = (bf16[768,768]{1,0:T(8,128)(2,1)S(1)}, bf16[768,768]{1,0:T(8,128)(2,1)}, u32[]{:S(2)}) copy-start(bf16[768,768]{1,0:T(8,128)(2,1)} %constant.24.clone.table_ref) | copy-start | bytes 3538948
  1.4 1.1 %copy-start.2 = (f32[8,64,384]{2,1,0:T(8,128)S(1)}, f32[8,64,384]{2,1,0:T(8,128)}, u32[]{:S(2)}) copy-start(f32[8,64,384]{2,1,0:T(8,128)} %vec_ref.3) | copy-start | bytes 2359300
  2.5 1.1 %copy-start.7 = (f32[8,64,384]{2,1,0:T(8,128)S(1)}, f32[8,64,384]{2,1,0:T(8,128)}, u32[]{:S(2)}) copy-start(f32[8,64,384]{2,1,0:T(8,128)} %kern_ref.1) | copy-start | bytes 2359300
  3.6 14.1 %copy-start.3 = (f32[8,64,384]{2,1,0:T(8,128)S(1)}, f32[8,64,384]{2,1,0:T(8,128)}, u32[]{:S(2)}) copy-start(f32[8,64,384]{2,1,0:T(8,128)} %vec_ref.3) | copy-start | bytes 2359300
  3.6 29.9 %copy-start.1 = (bf16[768,768]{1,0:T(8,128)(2,1)S(1)}, bf16[768,768]{1,0:T(8,128)(2,1)}, u32[]{:S(2)}) copy-start(bf16[768,768]{1,0:T(8,128)(2,1)} %constant.24.clone.table_ref) | copy-start | bytes 3538948
  11.6 1.5 %copy-start.5 = (f32[3,512,384]{2,1,0:T(8,128)}, f32[3,512,384]{2,1,0:T(8,128)S(1)}, u32[]{:S(2)}) copy-start(f32[3,512,384]{2,1,0:T(8,128)S(1)} %get-tuple-element.10.khat_ref) | copy-start | bytes 7077892
  13.1 4.4 %collective-permute-start = (f32[64,384]{1,0:T(8,128)S(1)}, f32[64,384]{1,0:T(8,128)S(1)}, u32[]{:S(2)}, u32[]{:S(2)}) collective-permute-start(f32[64,384]{1,0:T(8,128)S(1)} %get-tuple-element.9), channel_id=1, source_target_pairs={{0,1},{1,0},{2,3},{3,2},{4,5},{5,4},{6,7},{7,6},{8,9},{9,8},{10,11... | collective-permute-start | bytes 294920 | tf_op jit(solution)/shard_map/ppermute | solution.py:334
  17.4 6.6 %collective-permute-start.1 = (f32[64,384]{1,0:T(8,128)S(1)}, f32[64,384]{1,0:T(8,128)S(1)}, u32[]{:S(2)}, u32[]{:S(2)}) collective-permute-start(f32[64,384]{1,0:T(8,128)S(1)} %add.16), channel_id=1, source_target_pairs={{0,8},{1,9},{2,10},{3,11},{4,12},{5,13},{6,14},{7,15},{8,0},{9,1},... | collective-permute-start | bytes 294920 | tf_op jit(solution)/shard_map/ppermute | solution.py:334
  17.7 12.8 %collective-permute-start.5 = (f32[4,16,384]{2,1,0:T(8,128)S(1)}, f32[4,16,384]{2,1,0:T(8,128)S(1)}, u32[]{:S(2)}, u32[]{:S(2)}) collective-permute-start(f32[4,16,384]{2,1,0:T(8,128)S(1)} %get-tuple-element.13), channel_id=1, source_target_pairs={{1,0},{2,1},{3,2},{4,3},{5,4},{6,5},{7,6},{8,7},{9,8},{10,9},{11,1... | collective-permute-start | bytes 294920 | tf_op jit(solution)/shard_map/ppermute | solution.py:320
  20.9 9.6 %collective-permute-start.4 = (f32[4,16,384]{2,1,0:T(8,128)S(1)}, f32[4,16,384]{2,1,0:T(8,128)S(1)}, u32[]{:S(2)}, u32[]{:S(2)}) collective-permute-start(f32[4,16,384]{2,1,0:T(8,128)S(1)} %get-tuple-element.14), channel_id=1, source_target_pairs={{0,1},{1,2},{2,3},{3,4},{4,5},{5,6},{6,7},{7,8},{8,9},{9,10},{10,1... | collective-permute-start | bytes 294920 | tf_op jit(solution)/shard_map/ppermute | solution.py:319
  24.0 4.2 %collective-permute-start.2 = (f32[64,384]{1,0:T(8,128)S(1)}, f32[64,384]{1,0:T(8,128)S(1)}, u32[]{:S(2)}, u32[]{:S(2)}) collective-permute-start(f32[64,384]{1,0:T(8,128)S(1)} %add.17), channel_id=1, source_target_pairs={{0,2},{1,3},{2,0},{3,1},{4,6},{5,7},{6,4},{7,5},{8,10},{9,11},{10,... | collective-permute-start | bytes 294920 | tf_op jit(solution)/shard_map/ppermute | solution.py:334
  28.2 5.3 %collective-permute-start.3 = (f32[64,384]{1,0:T(8,128)S(1)}, f32[64,384]{1,0:T(8,128)S(1)}, u32[]{:S(2)}, u32[]{:S(2)}) collective-permute-start(f32[64,384]{1,0:T(8,128)S(1)} %add.18.pred_ref), channel_id=1, source_target_pairs={{0,4},{1,5},{2,6},{3,7},{4,0},{5,1},{6,2},{7,3},{8,12},{9,13},{10,... | collective-permute-start | bytes 294920 | tf_op jit(solution)/shard_map/ppermute | solution.py:334
  33.5 1.7 %copy-start.4 = (f32[4,384,384]{2,1,0:T(8,128)S(1)}, f32[4,384,384]{2,1,0:T(8,128)}, u32[]{:S(2)}) copy-start(f32[4,384,384]{2,1,0:T(8,128)} %corr_ref.1) | copy-start | bytes 7077892
  35.2 1.7 %copy-start.6 = (f32[3,512,384]{2,1,0:T(8,128)S(1)}, f32[3,512,384]{2,1,0:T(8,128)}, u32[]{:S(2)}) copy-start(f32[3,512,384]{2,1,0:T(8,128)} %copy-done.5) | copy-start | bytes 7077892
  42.4 6.5 %collective-permute-start.6 = (f32[4,64,384]{2,1,0:T(8,128)S(1)}, f32[4,64,384]{2,1,0:T(8,128)S(1)}, u32[]{:S(2)}, u32[]{:S(2)}) collective-permute-start(f32[4,64,384]{2,1,0:T(8,128)S(1)} %get-tuple-element.12), channel_id=1, source_target_pairs={{0,16},{16,0},{1,17},{17,1},{2,18},{18,2},{3,19},{19,3},{4,20},{20... | collective-permute-start | bytes 1179656 | tf_op jit(solution)/shard_map/ppermute | solution.py:342

commit v2 on v0

v2 whole, which is shorter than its diff:
```python
import functools
import math

import jax
import jax.numpy as jnp
import ml_dtypes
import numpy as np
from jax import lax
from jax.experimental import pallas as pl
from jax.experimental.pallas import tpu as pltpu
from jax.sharding import PartitionSpec as P

COLS = 16
LANES = 128
SUB = 8
F32 = jnp.float32
BF16 = jnp.bfloat16
NT_DIMS = (((1,), (1,)), ((), ()))


def dft_table(length):
    steps = np.arange(length, dtype=np.int64)
    phase = (steps[:, None] * (2 * steps[None, :] + 1)) % (4 * length)
    angle = phase.astype(np.float64) * (2.0 * math.pi / (4 * length))
    pair = np.stack([np.cos(angle), -np.sin(angle)], axis=1)
    pair = pair.reshape(length, 2, length // LANES, LANES)
    table = pair.transpose(0, 2, 1, 3).reshape(length, 2 * length)
    high = table.astype(ml_dtypes.bfloat16)
    low = (table - high.astype(np.float64)).astype(ml_dtypes.bfloat16)
    return np.concatenate([high, low], axis=0)


def split(x):
    high = x.astype(BF16)
    return high, (x - high.astype(F32)).astype(BF16)


def dot(a, b):
    return jnp.dot(a, b, preferred_element_type=F32)


def dot_nt(a, b):
    return lax.dot_general(a, b, NT_DIMS, preferred_element_type=F32)


def inverse_dft(high, low, table_ref, length):
    return (
        dot_nt(high, table_ref[:length])
        + dot_nt(high, table_ref[length : 2 * length])
        + dot_nt(low, table_ref[:length])
    )


def in_vmem(x):
    return pltpu.with_memory_space_constraint(x, pltpu.VMEM)


def in_hbm(x):
    return pltpu.with_memory_space_constraint(x, pltpu.HBM)


def rows_at(start, size):
    return pl.ds(pl.multiple_of(start, size), size)


def forward_kernel(
    kern_hbm,
    vec_hbm,
    table_hbm,
    corr_hbm,
    pred_ref,
    khat_ref,
    table_ref,
    vec_ref,
    corr_ref,
    first_ref,
    second_ref,
    kern_ref,
    vhat_ref,
    lhs_ref,
    spec_ref,
    sems,
):
    sensors, points, length = kern_ref.shape
    count = vec_ref.shape[0]
    pitch = vhat_ref.shape[2] // count
    own, halo, _ = first_ref.shape
    shift = lax.axis_index("sens") * own
    odd_place = lax.axis_index("pts") % 2
    cols = length // LANES

    copies = [
        pltpu.make_async_copy(kern_hbm, kern_ref, sems.at[0]),
        pltpu.make_async_copy(table_hbm, table_ref.at[: 2 * length], sems.at[1]),
        pltpu.make_async_copy(table_hbm.at[:length], table_ref.at[2 * length :], sems.at[2]),
        pltpu.make_async_copy(vec_hbm, vec_ref, sems.at[3]),
        pltpu.make_async_copy(corr_hbm, corr_ref, sems.at[4]),
    ]
    for copy in copies:
        copy.start()

    def fill(source_ref, first):
        def step(i, _):
            rows = rows_at(i * points, points)
            high, low = split(source_ref[lax.rem(i + first, source_ref.shape[0])])
            lhs_ref[rows, :length] = high
            lhs_ref[rows, length : 2 * length] = high
            lhs_ref[rows, 2 * length :] = low
            return 0

        lax.fori_loop(0, source_ref.shape[0], step, 0)

    copies[0].wait()
    fill(kern_ref, 0)
    copies[1].wait()
    copies[2].wait()
    rows = sensors * points
    for col in range(cols):
        hat = dot(lhs_ref[:rows], table_ref[:, 2 * col * LANES : 2 * (col + 1) * LANES])
        real, imag = hat[:, :LANES], hat[:, LANES:]
        khat_ref[0, col] = real
        khat_ref[1, col] = imag - real
        khat_ref[2, col] = imag + real

    copies[3].wait()
    fill(vec_ref, shift)
    step_in = points - halo
    for k in range(own):
        at = lax.rem(k + shift, count)
        first_ref[k] = vec_ref[at, rows_at((1 - odd_place) * step_in, halo)]
        second_ref[k] = vec_ref[at, rows_at(odd_place * step_in, halo)]
    rows = count * points
    for col in range(cols):
        hat = dot(lhs_ref[:rows], table_ref[:, 2 * col * LANES : 2 * (col + 1) * LANES])
        for k in range(count):
            real = hat[k * points : (k + 1) * points, :LANES]
            imag = hat[k * points : (k + 1) * points, LANES:]
            vhat_ref[0, col, k * pitch : k * pitch + points] = real + imag
            vhat_ref[1, col, k * pitch : k * pitch + points] = real
            vhat_ref[2, col, k * pitch : k * pitch + points] = imag

    def product(col, _):
        acc = [[None] * 3 for _ in range(sensors)]
        for p in range(points):
            left = [vhat_ref[c, col, pl.ds(p, count, stride=pitch)] for c in range(3)]
            for s in range(sensors):
                for c in range(3):
                    row = khat_ref[c, col, s * points + p : s * points + p + 1]
                    term = left[c] * jnp.broadcast_to(row, left[c].shape)
                    acc[s][c] = term if acc[s][c] is None else acc[s][c] + term
        for s in range(sensors):
            one, two, three = acc[s]
            spec_ref[s * count : (s + 1) * count, rows_at(2 * col * LANES, LANES)] = one - three
            spec_ref[s * count : (s + 1) * count, rows_at((2 * col + 1) * LANES, LANES)] = one + two
        return 0

    lax.fori_loop(0, cols, product, 0)
    high, low = split(spec_ref[...])
    pred_ref[...] = inverse_dft(high, low, table_ref, length)
    copies[4].wait()


def forward(kernel, vectors, table, correlation, own):
    sensors, points, length = kernel.shape
    count = vectors.shape[0]
    cols = length // LANES
    most = max(sensors, count) * points
    hbm = pl.BlockSpec(memory_space=pltpu.HBM)
    return pl.pallas_call(
        forward_kernel,
        out_shape=(
            pltpu.VMEM((sensors * count, length), F32),
            pltpu.VMEM((3, cols, sensors * points, LANES), F32),
            pltpu.VMEM((3 * length, 2 * length), BF16),
            pltpu.VMEM(vectors.shape, F32),
            pltpu.VMEM(correlation.shape, F32),
            pltpu.VMEM((own, COLS, length), F32),
            pltpu.VMEM((own, COLS, length), F32),
        ),
        in_specs=[hbm] * 4,
        out_specs=[pl.BlockSpec(memory_space=pltpu.VMEM)] * 7,
        scratch_shapes=[
            pltpu.VMEM(kernel.shape, F32),
            pltpu.VMEM((3, cols, count * (points + SUB), LANES), F32),
            pltpu.VMEM((most, 3 * length), BF16),
            pltpu.VMEM((sensors * count, 2 * length), F32),
            pltpu.SemaphoreType.DMA((5,)),
        ],
        compiler_params=pltpu.CompilerParams(vmem_limit_bytes=12 * 1024 * 1024),
    )(*map(in_hbm, (kernel, vectors, table, correlation)))


def correlate(first, count, rhat_ref, khat_ref, table_ref, high_ref, low_ref):
    length = table_ref.shape[1] // 2
    sensors = rhat_ref.shape[2] // count
    points = khat_ref.shape[2] // sensors
    cols = length // LANES
    some = high_ref.shape[0] // points
    k_block, g_block = 4, 2
    tall = g_block * SUB
    blocks = points // tall

    def product(step, _):
        col, g0 = step // blocks, step % blocks
        for k0 in range(0, some, k_block):
            ks = range(k0, min(k0 + k_block, some))
            acc = {}
            for s in range(sensors):
                right = [
                    [
                        khat_ref[c, col, pl.ds(s * points + pl.multiple_of(g0 * tall, tall) + b * SUB, SUB)]
                        for c in range(3)
                    ]
                    for b in range(g_block)
                ]
                for k in ks:
                    for c in range(3):
                        at = s * count + first + k
                        left = jnp.broadcast_to(rhat_ref[c, col, at : at + 1], (SUB, LANES))
                        for b in range(g_block):
                            term = left * right[b][c]
                            acc[k, b, c] = term if s == 0 else acc[k, b, c] + term
            for k in ks:
                re = jnp.concatenate([acc[k, b, 0] + acc[k, b, 1] for b in range(g_block)], axis=0)
                im = jnp.concatenate([acc[k, b, 0] - acc[k, b, 2] for b in range(g_block)], axis=0)
                at = pl.ds(k * points + pl.multiple_of(g0 * tall, tall), tall)
                lanes = rows_at(2 * col * LANES, LANES)
                others = rows_at((2 * col + 1) * LANES, LANES)
                high_ref[at, lanes], low_ref[at, lanes] = split(re)
                high_ref[at, others], low_ref[at, others] = split(im)
        return 0

    lax.fori_loop(0, cols * blocks, product, 0)
    data = inverse_dft(high_ref[...], low_ref[...], table_ref, length)
    return data.reshape(some, points, length)


def others_kernel(
    own,
    count,
    scale_ref,
    group_ref,
    pred_ref,
    corr_ref,
    khat_ref,
    table_ref,
    rest_ref,
    rhat_ref,
    high_ref,
    low_ref,
):
    sensors = scale_ref.shape[0]
    rows, length = pred_ref.shape
    groups = corr_ref.shape[0] // length
    pred = pred_ref[...]
    high, low = split(pred)
    turned = jnp.concatenate([high.astype(F32), low.astype(F32)], axis=0).T
    lane = lax.broadcasted_iota(jnp.int32, turned.shape, 1)
    halves = jnp.concatenate([turned, jnp.where(lane < rows, turned, 0.0)], axis=0).astype(BF16)
    mixed = dot(corr_ref[...], halves)
    sensor = lax.rem(lane, rows) // count
    group = jnp.zeros_like(sensor)
    for s in range(sensors):
        group = jnp.where(sensor == s, group_ref[s], group)
    chosen = jnp.zeros_like(turned)
    for g in range(groups):
        chosen = jnp.where(group == g, mixed[g * length : (g + 1) * length], chosen)
    chosen = chosen.T
    whole = pred + chosen[:rows] + chosen[rows:]
    whole = jnp.concatenate(
        [whole[s * count : (s + 1) * count] * scale_ref[s] for s in range(sensors)], axis=0
    ) * (1.0 / (length * length))
    high, low = split(whole)
    hat = dot(jnp.concatenate([high, high, low], axis=1), table_ref[...])
    for col in range(length // LANES):
        real = hat[:, 2 * col * LANES : (2 * col + 1) * LANES]
        imag = hat[:, (2 * col + 1) * LANES : (2 * col + 2) * LANES]
        rhat_ref[0, col] = real + imag
        rhat_ref[1, col] = imag
        rhat_ref[2, col] = real
    rest_ref[...] = correlate(own, count, rhat_ref, khat_ref, table_ref, high_ref, low_ref)


def own_kernel(count, rhat_ref, khat_ref, table_ref, prior_ref, out_ref, high_ref, low_ref):
    data = correlate(0, count, rhat_ref, khat_ref, table_ref, high_ref, low_ref)
    out_ref[...] = data + prior_ref[...]


def adjoint_others(pred, scale, group, correlation, khat, table, own, count):
    rows, length = pred.shape
    points = khat.shape[2] // (rows // count)
    vmem = pl.BlockSpec(memory_space=pltpu.VMEM)
    smem = pl.BlockSpec(memory_space=pltpu.SMEM)
    some = count - own
    return pl.pallas_call(
        functools.partial(others_kernel, own, count),
        out_shape=(
            pltpu.VMEM((some, points, length), F32),
            pltpu.VMEM((3, length // LANES, rows, LANES), F32),
        ),
        in_specs=[smem] * 2 + [vmem] * 4,
        out_specs=[vmem, vmem],
        scratch_shapes=[pltpu.VMEM((some * points, 2 * length), BF16)] * 2,
        compiler_params=pltpu.CompilerParams(vmem_limit_bytes=12 * 1024 * 1024),
    )(scale, group, *map(in_vmem, (pred, correlation, khat, table)))


def adjoint_own(rhat, khat, table, prior, count):
    own, points, length = prior.shape
    vmem = pl.BlockSpec(memory_space=pltpu.VMEM)
    return pl.pallas_call(
        functools.partial(own_kernel, count),
        out_shape=pltpu.VMEM((own, points, length), F32),
        in_specs=[vmem] * 4,
        out_specs=vmem,
        scratch_shapes=[pltpu.VMEM((own * points, 2 * length), BF16)] * 2,
        compiler_params=pltpu.CompilerParams(vmem_limit_bytes=12 * 1024 * 1024),
        cost_estimate=pl.CostEstimate(
            flops=6 * own * points * length * length * 2, bytes_accessed=4 * khat.size, transcendentals=0
        ),
    )(*map(in_vmem, (rhat, khat, table, prior)))


def halves_kernel(corr_ref, out_ref):
    length = corr_ref.shape[1]

    def step(g, _):
        rows = rows_at(g * length, length)
        out_ref[rows, :length], out_ref[rows, length:] = split(corr_ref[g])
        return 0

    lax.fori_loop(0, corr_ref.shape[0], step, 0)


def halves_of(correlation):
    groups, length, _ = correlation.shape
    vmem = pl.BlockSpec(memory_space=pltpu.VMEM)
    return pl.pallas_call(
        halves_kernel,
        out_shape=pltpu.VMEM((groups * length, 2 * length), BF16),
        in_specs=[vmem],
        out_specs=vmem,
        compiler_params=pltpu.CompilerParams(vmem_limit_bytes=4 * 1024 * 1024),
    )(in_vmem(correlation))


def add_kernel(*refs):
    total = refs[0][...]
    for ref in refs[1:-1]:
        total = total + ref[...]
    refs[-1][...] = total


def add(*parts):
    vmem = pl.BlockSpec(memory_space=pltpu.VMEM)
    return pl.pallas_call(
        add_kernel,
        out_shape=jax.ShapeDtypeStruct(parts[0].shape, F32),
        in_specs=[vmem] * len(parts),
        out_specs=vmem,
        compiler_params=pltpu.CompilerParams(vmem_limit_bytes=4 * 1024 * 1024),
    )(*map(in_vmem, parts))


def prior_kernel(vec_ref, first_ref, second_ref, stiff_ref, coup_ref, near_ref, out_ref):
    own, points, _ = out_ref.shape
    place_here = lax.axis_index("pts")
    shift = lax.axis_index("sens") * own
    halo = first_ref.shape[1]
    count = vec_ref.shape[0]
    span = points + 2 * halo
    place = lax.broadcasted_iota(jnp.int32, (span, points), 0)
    coup = coup_ref[...]
    here = lax.broadcasted_iota(jnp.int32, (span, points), 1) + halo
    diagonal = stiff_ref[...] + jnp.sum(coup, axis=0, keepdims=True)
    weight = jnp.where(place == here, diagonal, 0.0)
    near = near_ref[...] - (place_here * points - halo)
    swap = (1 - place_here % 2) * (points + halo)
    near = near + jnp.where(near < halo, swap, 0) - jnp.where(near >= points + halo, swap, 0)
    for j in range(coup.shape[0]):
        weight = weight - jnp.where(place == near[j : j + 1], coup[j : j + 1], 0.0)
    weight_high, weight_low = split(weight.T)
    for k in range(own):
        value = jnp.concatenate(
            [first_ref[k], vec_ref[lax.rem(shift + k, count)], second_ref[k]], axis=0
        )
        high, low = split(value)
        out_ref[k] = dot(weight_high, high) + dot(weight_high, low) + dot(weight_low, high)


def prior_term(vectors, first, second, stiffness, couplings, neighbors):
    own = first.shape[0]
    _, points, length = vectors.shape
    vmem = pl.BlockSpec(memory_space=pltpu.VMEM)
    return pl.pallas_call(
        prior_kernel,
        out_shape=pltpu.VMEM((own, points, length), F32),
        in_specs=[vmem] * 6,
        out_specs=vmem,
        compiler_params=pltpu.CompilerParams(vmem_limit_bytes=8 * 1024 * 1024),
    )(
        *map(in_vmem, (vectors, first, second, stiffness[None], couplings, neighbors))
    )


def stages(size):
    bits = [1 << bit for bit in range(size.bit_length() - 1)]
    masks = []
    while bits:
        low, *bits = bits
        masks.append([low])
        if bits:
            high, *bits = bits
            masks[-1] += [high, low + high]
    turned = list(masks)
    if len(masks) > 1 and len(masks[0]) == len(masks[1]):
        turned[0], turned[1] = masks[1], masks[0]
    return masks, turned


def local(table, kernel, vectors, noise_scale, sensor_group, correlation, stiffness, couplings, neighbors):
    sensors, points, length = kernel.shape
    count = vectors.shape[0]
    n_sens, n_pts = lax.axis_size("sens"), lax.axis_size("pts")
    own = count // n_sens

    pred, khat, table, vectors, correlation, *edges = forward(
        kernel, vectors, table, correlation, own
    )
    correlation = halves_of(correlation)

    links = [[], []]
    for p in range(n_pts - 1):
        links[p % 2] += [(p, p + 1), (p + 1, p)]
    halos = []
    for step, (even, odd) in enumerate(zip(*stages(n_pts))):
        if step == 1:
            pred, edges[1] = lax.optimization_barrier((pred, edges[1]))
        more = []
        for mask_even, mask_odd in zip(even, odd):
            pairs = [
                (s * n_pts + p, s * n_pts + (p ^ (mask_odd if s % 2 else mask_even)))
                for s in range(n_sens)
                for p in range(n_pts)
            ]
            more.append(lax.ppermute(pred, ("sens", "pts"), pairs))
        if step < 2:
            halos.append(lax.ppermute(edges[step], "pts", links[step]))
        for part in more:
            pred = pred + part
        if step == 0:
            pred, halos[0], correlation = lax.optimization_barrier((pred, halos[0], correlation))

    prior = prior_term(vectors, halos[0], halos[1], stiffness, couplings, neighbors)
    pred, prior = lax.optimization_barrier((pred, prior))
    rest, rhat = adjoint_others(pred, noise_scale, sensor_group, correlation, khat, table, own, count)
    received = []
    for j in range(1, n_sens):
        pairs = [(s, (s + j) % n_sens) for s in range(n_sens)]
        received.append(lax.ppermute(rest[(j - 1) * own : j * own], "sens", pairs))
    total = adjoint_own(rhat, khat, table, prior, count)
    return add(total, *received)


def solution(mesh):
    in_specs = (
        P(),
        P("sens", "pts", None),
        P(None, "pts", None),
        P("sens"),
        P("sens"),
        P(),
        P("pts"),
        P(None, "pts"),
        P(None, "pts"),
    )
    out_specs = P("sens", "pts", None)
    mapped = jax.shard_map(local, mesh=mesh, in_specs=in_specs, out_specs=out_specs, check_vma=False)

    def run(kernel, *rest):
        return mapped(jnp.asarray(dft_table(kernel.shape[-1])), kernel, *rest)

    return run
```

time: 231 us -> 38.6 us (0.17)
  the two profiles are of different devices: /device:TPU:6 before, /device:TPU:25 now
where the time goes in v2:
time: 38.6 us; the launch traced here: 38.4 us
  Pallas kernels  16.1 us (42%)
  starting transfers between devices  14.8 us (38%)
  waiting for transfers between devices  7.26 us (19%)
    pallas_call x1, Pallas kernels, forward(): pl.pallas_call(forward_kernel, out_shape=(pltpu.VMEM((sensors * count, le...  8.12 us
    ppermute x6, starting transfers between devices, local(): more.append(lax.ppermute(pred, ('sens', 'pts'), pairs))  6.52 us
    ppermute x2, waiting for transfers between devices, local(): halos.append(lax.ppermute(edges[step], 'pts', links[step]))  5.79 us
    ppermute x2, starting transfers between devices, local(): halos.append(lax.ppermute(edges[step], 'pts', links[step]))  5.19 us
    pallas_call x1, Pallas kernels, adjoint_others(): pl.pallas_call(functools.partial(others_kernel, own, count), out_shape=(p...  4.66 us
    ppermute x1, starting transfers between devices, local(): received.append(lax.ppermute(rest[(j - 1) * own:j * own], 'sens', pairs))  3.09 us
    pallas_call x1, Pallas kernels, adjoint_own(): pl.pallas_call(functools.partial(own_kernel, count), out_shape=pltpu.VMEM...  1.72 us
    ppermute x6, waiting for transfers between devices, local(): more.append(lax.ppermute(pred, ('sens', 'pts'), pairs))  1.47 us
  transfers between devices with their start and end apart: 9, of which 5 were waited for; matrix products, arithmetic and copies ran while one was open for 0% of the time, Pallas kernels for 6%

profile of v2, /device:TPU:25, one launch (start us, length us, event | category | flops | bytes accessed | tf_op | source)
XLA Modules:
  0.0 38.4 jit_solution(14794102586897568838)
XLA Ops:
  0.0 8.1 %shard_map.91 = (f32[64,384]{1,0:T(8,128)S(1)}, f32[3,3,512,128]{3,2,1,0:T(8,128)S(1)}, bf16[1152,768]{1,0:T(8,128)(2,1)S(1)}, f32[8,64,384]{2,1,0:T(8,128)S(1)}...) custom-call(f32[8,64,384]{2,1,0:T(8,128)} %kern_hbm.1, f32[8,64,384]{2,1,0:T(8,128)} %vec_hbm.1, ...), custom_call_target="tpu_custom_call" | custom-call | tf_op jit(solution)/shard_map/pallas_call | solution.py:169
  8.1 0.1 collective-permute-start.2
  8.2 1.3 %collective-permute-start.1 = (f32[64,384]{1,0:T(8,128)S(1)}, f32[64,384]{1,0:T(8,128)S(1)}, u32[]{:S(2)}, u32[]{:S(2)}) collective-permute-start(f32[64,384]{1,0:T(8,128)S(1)} %get-tuple-element.21), channel_id=1, source_target_pairs={{0,2},{1,3},{2,0},{3,1},{4,6},{5,7},{6,4},{7,5},{8,10},{9,11},{10,... | collective-permute-start | bytes 294920 | tf_op jit(solution)/shard_map/ppermute | solution.py:446
  9.6 2.2 %collective-permute-start = (f32[64,384]{1,0:T(8,128)S(1)}, f32[64,384]{1,0:T(8,128)S(1)}, u32[]{:S(2)}, u32[]{:S(2)}) collective-permute-start(f32[64,384]{1,0:T(8,128)S(1)} %get-tuple-element.21), channel_id=1, source_target_pairs={{0,1},{1,0},{2,3},{3,2},{4,5},{5,4},{6,7},{7,6},{8,9},{9,8},{10,11... | collective-permute-start | bytes 294920 | tf_op jit(solution)/shard_map/ppermute | solution.py:446
  11.7 1.2 %collective-permute-start.3 = (f32[4,16,384]{2,1,0:T(8,128)S(1)}, f32[4,16,384]{2,1,0:T(8,128)S(1)}, u32[]{:S(2)}, u32[]{:S(2)}) collective-permute-start(f32[4,16,384]{2,1,0:T(8,128)S(1)} %get-tuple-element.22), channel_id=1, source_target_pairs={{0,1},{1,0},{2,3},{3,2},{4,5},{5,4},{6,7},{7,6},{8,9},{9,8},{10,11... | collective-permute-start | bytes 294920 | tf_op jit(solution)/shard_map/ppermute | solution.py:448
  13.0 0.4 %shard_map.92.corr_ref = bf16[1536,768]{1,0:T(8,128)(2,1)S(1)} custom-call(f32[4,384,384]{2,1,0:T(8,128)S(1)} %get-tuple-element.23.corr_ref), custom_call_target="tpu_custom_call" | custom-call | tf_op jit(solution)/shard_map/pallas_call | solution.py:338
  13.4 0.0 copy-start.3
  13.4 0.0 copy-start.4
  13.4 0.2 collective-permute-done.2
  13.7 1.1 %collective-permute-done.1 = f32[64,384]{1,0:T(8,128)S(1)} collective-permute-done((f32[64,384]{1,0:T(8,128)S(1)}, f32[64,384]{1,0:T(8,128)S(1)}, u32[]{:S(2)}, u32[]{:S(2)}) %collective-permute-start.1) | collective-permute-done | bytes 98336 | tf_op jit(solution)/shard_map/ppermute | solution.py:446
  14.8 0.2 collective-permute-done
  14.9 1.2 %collective-permute-done.3.first_ref = f32[4,16,384]{2,1,0:T(8,128)S(1)} collective-permute-done((f32[4,16,384]{2,1,0:T(8,128)S(1)}, f32[4,16,384]{2,1,0:T(8,128)S(1)}, u32[]{:S(2)}, u32[]{:S(2)}) %collective-permute-start.3) | collective-permute-done | bytes 98336 | tf_op jit(solution)/shard_map/ppermute | solution.py:448
  16.1 2.5 %collective-permute-start.6 = (f32[64,384]{1,0:T(8,128)S(1)}, f32[64,384]{1,0:T(8,128)S(1)}, u32[]{:S(2)}, u32[]{:S(2)}) collective-permute-start(f32[64,384]{1,0:T(8,128)S(1)} %add_add_fusion.1), channel_id=1, source_target_pairs={{0,12},{1,13},{2,14},{3,15},{4,8},{5,9},{6,10},{7,11},{8,4},{9,5},... | collective-permute-start | bytes 294920 | tf_op jit(solution)/shard_map/ppermute | solution.py:446
  18.6 0.4 collective-permute-start.5
  19.0 0.0 collective-permute-start.4
  19.0 4.0 %collective-permute-start.7 = (f32[4,16,384]{2,1,0:T(8,128)S(1)}, f32[4,16,384]{2,1,0:T(8,128)S(1)}, u32[]{:S(2)}, u32[]{:S(2)}) collective-permute-start(f32[4,16,384]{2,1,0:T(8,128)S(1)} %get-tuple-element.29), channel_id=1, source_target_pairs={{1,2},{2,1},{3,4},{4,3},{5,6},{6,5},{7,8},{8,7},{9,10},{10,9},{11,... | collective-permute-start | bytes 294920 | tf_op jit(solution)/shard_map/ppermute | solution.py:448
  23.0 0.0 collective-permute-done.6
  23.0 0.0 collective-permute-done.5
  23.1 4.6 %collective-permute-done.7.second_ref = f32[4,16,384]{2,1,0:T(8,128)S(1)} collective-permute-done((f32[4,16,384]{2,1,0:T(8,128)S(1)}, f32[4,16,384]{2,1,0:T(8,128)S(1)}, u32[]{:S(2)}, u32[]{:S(2)}) %collective-permute-start.7) | collective-permute-done | bytes 98336 | tf_op jit(solution)/shard_map/ppermute | solution.py:448
  27.7 0.4 %shard_map.93.prior_ref = f32[4,64,384]{2,1,0:T(8,128)S(1)} custom-call(f32[8,64,384]{2,1,0:T(8,128)S(1)} %get-tuple-element.27.vec_ref, f32[4,16,384]{2,1,0:T(8,128)S(1)} %collective-permute-done.3.first_ref, f32[4,16,384]{2,1,0:T(8,128)S(1)} %collective-permute-done.7.second_ref, f32[1,64]{1,0:T(1,128)S(1)} %bitcast.1, f32[4,64]{1,0:T(4,128)S(1)} %copy-done, ...), custom_call_target="tpu_custom_call" | custom-call | tf_op jit(solution)/shard_map/pallas_call | solution.py:395
  28.1 4.7 %shard_map.94 = (f32[4,64,384]{2,1,0:T(8,128)S(1)}, f32[3,3,64,128]{3,2,1,0:T(8,128)S(1)}) custom-call(f32[8]{0:T(128)S(1)} %copy-done.3, s32[8]{0:T(128)S(1)} %copy-done.4, f32[64,384]{1,0:T(8,128)S(1)} %add_add_fusion.pred_ref, bf16[1536,768]{1,0:T(8,128)(2,1)S(1)} %shard_map.92.corr_ref, f32[3,3,512,128]{3,2,1,0:T(8,128)S(1)} %get-tuple-element.32.khat_ref, ...), custom_call_target="tpu_custom_call" | custom-call | tf_op jit(solution)/shard_map/pallas_call | solution.py:295
  32.8 3.1 %collective-permute-start.8 = (f32[4,64,384]{2,1,0:T(8,128)S(1)}, f32[4,64,384]{2,1,0:T(8,128)S(1)}, u32[]{:S(2)}, u32[]{:S(2)}) collective-permute-start(f32[4,64,384]{2,1,0:T(8,128)S(1)} %get-tuple-element.36), channel_id=1, source_target_pairs={{0,16},{16,0},{1,17},{17,1},{2,18},{18,2},{3,19},{19,3},{4,20},{20... | collective-permute-start | bytes 1179656 | tf_op jit(solution)/shard_map/ppermute | solution.py:460
  35.9 1.7 %shard_map.95.refs_0_ = f32[4,64,384]{2,1,0:T(8,128)S(1)} custom-call(f32[3,3,64,128]{3,2,1,0:T(8,128)S(1)} %get-tuple-element.34.rhat_ref, f32[3,3,512,128]{3,2,1,0:T(8,128)S(1)} %get-tuple-element.32.khat_ref, bf16[1152,768]{1,0:T(8,128)(2,1)S(1)} %get-tuple-element.33.table_ref, f32[4,64,384]{2,1,0:T(8,128)S(1)} %shard_map.93.prior_ref), custom_call_target="tpu_custom_call" | custom-call | flops 452984832 | bytes 2359296 | tf_op jit(solution)/shard_map/pallas_call | solution.py:311
  37.6 0.8 %shard_map.96 = f32[4,64,384]{2,1,0:T(8,128)} custom-call(f32[4,64,384]{2,1,0:T(8,128)S(1)} %shard_map.95.refs_0_, f32[4,64,384]{2,1,0:T(8,128)S(1)} %collective-permute-done.8.refs_1_), custom_call_target="tpu_custom_call" | custom-call | tf_op jit(solution)/shard_map/pallas_call | solution.py:356
  (12 shorter events, 0.1 us)
Async XLA Ops:
  8.1 5.5 %collective-permute-start.2 = (f32[64,384]{1,0:T(8,128)S(1)}, f32[64,384]{1,0:T(8,128)S(1)}, u32[]{:S(2)}, u32[]{:S(2)}) collective-permute-start(f32[64,384]{1,0:T(8,128)S(1)} %get-tuple-element.21), channel_id=1, source_target_pairs={{0,3},{1,2},{2,1},{3,0},{4,7},{5,6},{6,5},{7,4},{8,11},{9,10},{10,... | collective-permute-start | bytes 294920 | tf_op jit(solution)/shard_map/ppermute | solution.py:446
  8.2 6.5 %collective-permute-start.1 = (f32[64,384]{1,0:T(8,128)S(1)}, f32[64,384]{1,0:T(8,128)S(1)}, u32[]{:S(2)}, u32[]{:S(2)}) collective-permute-start(f32[64,384]{1,0:T(8,128)S(1)} %get-tuple-element.21), channel_id=1, source_target_pairs={{0,2},{1,3},{2,0},{3,1},{4,6},{5,7},{6,4},{7,5},{8,10},{9,11},{10,... | collective-permute-start | bytes 294920 | tf_op jit(solution)/shard_map/ppermute | solution.py:446
  9.6 5.4 %collective-permute-start = (f32[64,384]{1,0:T(8,128)S(1)}, f32[64,384]{1,0:T(8,128)S(1)}, u32[]{:S(2)}, u32[]{:S(2)}) collective-permute-start(f32[64,384]{1,0:T(8,128)S(1)} %get-tuple-element.21), channel_id=1, source_target_pairs={{0,1},{1,0},{2,3},{3,2},{4,5},{5,4},{6,7},{7,6},{8,9},{9,8},{10,11... | collective-permute-start | bytes 294920 | tf_op jit(solution)/shard_map/ppermute | solution.py:446
  11.7 4.4 %collective-permute-start.3 = (f32[4,16,384]{2,1,0:T(8,128)S(1)}, f32[4,16,384]{2,1,0:T(8,128)S(1)}, u32[]{:S(2)}, u32[]{:S(2)}) collective-permute-start(f32[4,16,384]{2,1,0:T(8,128)S(1)} %get-tuple-element.22), channel_id=1, source_target_pairs={{0,1},{1,0},{2,3},{3,2},{4,5},{5,4},{6,7},{7,6},{8,9},{9,8},{10,11... | collective-permute-start | bytes 294920 | tf_op jit(solution)/shard_map/ppermute | solution.py:448
  13.0 14.7 %copy-start = (f32[4,64]{1,0:T(4,128)S(1)}, f32[4,64]{1,0:T(4,128)}, u32[]{:S(2)}) copy-start(f32[4,64]{1,0:T(4,128)} %coup_ref.1) | copy-start | bytes 3076
  13.0 14.7 %copy-start.1 = (s32[4,64]{1,0:T(4,128)S(1)}, s32[4,64]{1,0:T(4,128)}, u32[]{:S(2)}) copy-start(s32[4,64]{1,0:T(4,128)} %near_ref.1) | copy-start | bytes 3076
  13.0 14.7 %copy-start.2 = (f32[64]{0:T(128)S(1)}, f32[64]{0:T(128)}, u32[]{:S(2)}) copy-start(f32[64]{0:T(128)} %param.14) | copy-start | bytes 772
  13.4 14.7 %copy-start.3 = (f32[8]{0:T(128)S(1)}, f32[8]{0:T(128)}, u32[]{:S(2)}) copy-start(f32[8]{0:T(128)} %scale_ref.1) | copy-start | bytes 100
  13.4 14.7 %copy-start.4 = (s32[8]{0:T(128)S(1)}, s32[8]{0:T(128)}, u32[]{:S(2)}) copy-start(s32[8]{0:T(128)} %group_ref.1) | copy-start | bytes 100
  16.1 6.9 %collective-permute-start.6 = (f32[64,384]{1,0:T(8,128)S(1)}, f32[64,384]{1,0:T(8,128)S(1)}, u32[]{:S(2)}, u32[]{:S(2)}) collective-permute-start(f32[64,384]{1,0:T(8,128)S(1)} %add_add_fusion.1), channel_id=1, source_target_pairs={{0,12},{1,13},{2,14},{3,15},{4,8},{5,9},{6,10},{7,11},{8,4},{9,5},... | collective-permute-start | bytes 294920 | tf_op jit(solution)/shard_map/ppermute | solution.py:446
  18.6 4.4 %collective-permute-start.5 = (f32[64,384]{1,0:T(8,128)S(1)}, f32[64,384]{1,0:T(8,128)S(1)}, u32[]{:S(2)}, u32[]{:S(2)}) collective-permute-start(f32[64,384]{1,0:T(8,128)S(1)} %add_add_fusion.1), channel_id=1, source_target_pairs={{0,8},{1,9},{2,10},{3,11},{4,12},{5,13},{6,14},{7,15},{8,0},{9,1},... | collective-permute-start | bytes 294920 | tf_op jit(solution)/shard_map/ppermute | solution.py:446
  19.0 4.0 %collective-permute-start.4 = (f32[64,384]{1,0:T(8,128)S(1)}, f32[64,384]{1,0:T(8,128)S(1)}, u32[]{:S(2)}, u32[]{:S(2)}) collective-permute-start(f32[64,384]{1,0:T(8,128)S(1)} %add_add_fusion.1), channel_id=1, source_target_pairs={{0,4},{1,5},{2,6},{3,7},{4,0},{5,1},{6,2},{7,3},{8,12},{9,13},{10,... | collective-permute-start | bytes 294920 | tf_op jit(solution)/shard_map/ppermute | solution.py:446
  19.0 8.7 %collective-permute-start.7 = (f32[4,16,384]{2,1,0:T(8,128)S(1)}, f32[4,16,384]{2,1,0:T(8,128)S(1)}, u32[]{:S(2)}, u32[]{:S(2)}) collective-permute-start(f32[4,16,384]{2,1,0:T(8,128)S(1)} %get-tuple-element.29), channel_id=1, source_target_pairs={{1,2},{2,1},{3,4},{4,3},{5,6},{6,5},{7,8},{8,7},{9,10},{10,9},{11,... | collective-permute-start | bytes 294920 | tf_op jit(solution)/shard_map/ppermute | solution.py:448
  32.8 4.8 %collective-permute-start.8 = (f32[4,64,384]{2,1,0:T(8,128)S(1)}, f32[4,64,384]{2,1,0:T(8,128)S(1)}, u32[]{:S(2)}, u32[]{:S(2)}) collective-permute-start(f32[4,64,384]{2,1,0:T(8,128)S(1)} %get-tuple-element.36), channel_id=1, source_target_pairs={{0,16},{16,0},{1,17},{17,1},{2,18},{18,2},{3,19},{19,3},{4,20},{20... | collective-permute-start | bytes 1179656 | tf_op jit(solution)/shard_map/ppermute | solution.py:460

commit v3 on v2

v3 whole, which is shorter than its diff:
```python
import functools
import math

import jax
import jax.numpy as jnp
import ml_dtypes
import numpy as np
from jax import lax
from jax.experimental import pallas as pl
from jax.experimental.pallas import tpu as pltpu
from jax.sharding import PartitionSpec as P

COLS = 16
LANES = 128
SUB = 8
F32 = jnp.float32
BF16 = jnp.bfloat16


def halves_table(table):
    high = table.astype(ml_dtypes.bfloat16)
    low = (table - high.astype(np.float64)).astype(ml_dtypes.bfloat16)
    return np.concatenate([high, low], axis=0)


def dft_tables(length):
    steps = np.arange(length, dtype=np.int64)
    phase = (steps[:, None] * (2 * steps[None, :] + 1)) % (4 * length)
    angle = phase.astype(np.float64) * (2.0 * math.pi / (4 * length))
    pair = np.stack([np.cos(angle), -np.sin(angle)], axis=1)
    pair = pair.reshape(length, 2, length // LANES, LANES)
    table = pair.transpose(0, 2, 1, 3).reshape(length, 2 * length)
    return halves_table(table), halves_table(table.T)


def split(x):
    high = x.astype(BF16)
    return high, (x - high.astype(F32)).astype(BF16)


def dot(a, b):
    return jnp.dot(a, b, preferred_element_type=F32)


def in_vmem(x):
    return pltpu.with_memory_space_constraint(x, pltpu.VMEM)


def in_hbm(x):
    return pltpu.with_memory_space_constraint(x, pltpu.HBM)


def rows_at(start, size):
    return pl.ds(pl.multiple_of(start, size), size)


def back_column(high, low, inverse_ref, col):
    half = inverse_ref.shape[0] // 2
    upper = inverse_ref[2 * col * LANES : 2 * (col + 1) * LANES]
    lower = inverse_ref[half + 2 * col * LANES : half + 2 * (col + 1) * LANES]
    return dot(high, upper) + dot(high, lower) + dot(low, upper)


def forward_kernel(
    kern_hbm,
    vec_hbm,
    table_hbm,
    inverse_hbm,
    corr_hbm,
    pred_ref,
    khat_ref,
    table_ref,
    inverse_ref,
    vec_ref,
    corr_ref,
    first_ref,
    second_ref,
    kern_ref,
    vhat_ref,
    kern_lhs_ref,
    vec_lhs_ref,
    sems,
):
    sensors, points, length = kern_ref.shape
    count = vec_ref.shape[0]
    own, halo, _ = first_ref.shape
    shift = lax.axis_index("sens") * own
    odd_place = lax.axis_index("pts") % 2
    cols = length // LANES

    pairs = [(kern_hbm, kern_ref), (vec_hbm, vec_ref)]
    for col in range(cols):
        lanes = slice(2 * col * LANES, 2 * (col + 1) * LANES)
        pairs.append((table_hbm.at[:, lanes], table_ref.at[: 2 * length, lanes]))
        pairs.append((table_hbm.at[:length, lanes], table_ref.at[2 * length :, lanes]))
    pairs.append((inverse_hbm, inverse_ref))
    pairs.append((corr_hbm, corr_ref))
    copies = [
        pltpu.make_async_copy(source, target, sems.at[i]) for i, (source, target) in enumerate(pairs)
    ]
    for i in (0, 2, 3, 1, *range(4, len(copies))):
        copies[i].start()

    def fill(source_ref, lhs_ref, first):
        def step(i, _):
            rows = rows_at(i * points, points)
            high, low = split(source_ref[lax.rem(i + first, source_ref.shape[0])])
            lhs_ref[rows, :length] = high
            lhs_ref[rows, length : 2 * length] = high
            lhs_ref[rows, 2 * length :] = low
            return 0

        lax.fori_loop(0, source_ref.shape[0], step, 0)

    def transform(lhs_ref, col):
        hat = dot(lhs_ref[...], table_ref[:, 2 * col * LANES : 2 * (col + 1) * LANES])
        return hat[:, :LANES], hat[:, LANES:]

    def kern_column(col):
        real, imag = transform(kern_lhs_ref, col)
        khat_ref[0, col] = real
        khat_ref[1, col] = imag - real
        khat_ref[2, col] = imag + real

    def vec_column(col):
        real, imag = transform(vec_lhs_ref, col)
        for k in range(count):
            re, im = real[k * points : (k + 1) * points], imag[k * points : (k + 1) * points]
            at = pl.ds(k, points, stride=count)
            vhat_ref[0, col, at] = re + im
            vhat_ref[1, col, at] = re
            vhat_ref[2, col, at] = im

    def product(col):
        acc = [[None] * 3 for _ in range(sensors)]
        for p in range(points):
            left = [vhat_ref[c, col, p * count : (p + 1) * count] for c in range(3)]
            for s in range(sensors):
                for c in range(3):
                    row = khat_ref[c, col, s * points + p : s * points + p + 1]
                    term = left[c] * jnp.broadcast_to(row, left[c].shape)
                    acc[s][c] = term if acc[s][c] is None else acc[s][c] + term
        real = jnp.concatenate([one - three for one, _, three in acc], axis=0)
        imag = jnp.concatenate([one + two for one, two, _ in acc], axis=0)
        high, low = split(jnp.concatenate([real, imag], axis=1))
        return back_column(high, low, inverse_ref, col)

    copies[0].wait()
    fill(kern_ref, kern_lhs_ref, 0)
    copies[2].wait()
    copies[3].wait()
    kern_column(0)
    copies[1].wait()
    fill(vec_ref, vec_lhs_ref, shift)
    step_in = points - halo
    for k in range(own):
        at = lax.rem(k + shift, count)
        first_ref[k] = vec_ref[at, rows_at((1 - odd_place) * step_in, halo)]
        second_ref[k] = vec_ref[at, rows_at(odd_place * step_in, halo)]
    for copy in copies[4:-1]:
        copy.wait()
    pred = None
    for col in range(cols):
        if col:
            kern_column(col)
        vec_column(col)
        part = product(col)
        pred = part if pred is None else pred + part
    pred_ref[...] = pred
    copies[-1].wait()


def forward(kernel, vectors, table, inverse, correlation, own):
    sensors, points, length = kernel.shape
    count = vectors.shape[0]
    cols = length // LANES
    hbm = pl.BlockSpec(memory_space=pltpu.HBM)
    return pl.pallas_call(
        forward_kernel,
        out_shape=(
            pltpu.VMEM((sensors * count, length), F32),
            pltpu.VMEM((3, cols, sensors * points, LANES), F32),
            pltpu.VMEM((3 * length, 2 * length), BF16),
            pltpu.VMEM((4 * length, length), BF16),
            pltpu.VMEM(vectors.shape, F32),
            pltpu.VMEM(correlation.shape, F32),
            pltpu.VMEM((own, COLS, length), F32),
            pltpu.VMEM((own, COLS, length), F32),
        ),
        in_specs=[hbm] * 5,
        out_specs=[pl.BlockSpec(memory_space=pltpu.VMEM)] * 8,
        scratch_shapes=[
            pltpu.VMEM(kernel.shape, F32),
            pltpu.VMEM((3, cols, count * points, LANES), F32),
            pltpu.VMEM((sensors * points, 3 * length), BF16),
            pltpu.VMEM((count * points, 3 * length), BF16),
            pltpu.SemaphoreType.DMA((4 + 2 * cols,)),
        ],
        compiler_params=pltpu.CompilerParams(vmem_limit_bytes=14 * 1024 * 1024),
    )(*map(in_hbm, (kernel, vectors, table, inverse, correlation)))


def correlate(first, count, rhat_ref, khat_ref, inverse_ref, high_ref, low_ref):
    length = inverse_ref.shape[1]
    sensors = rhat_ref.shape[2] // count
    points = khat_ref.shape[2] // sensors
    cols = length // LANES
    some = high_ref.shape[0] // points
    k_block, g_block = 4, 2
    tall = g_block * SUB
    blocks = points // tall

    def product(step, _):
        col, g0 = step // blocks, step % blocks
        for k0 in range(0, some, k_block):
            ks = range(k0, min(k0 + k_block, some))
            acc = {}
            for s in range(sensors):
                right = [
                    [
                        khat_ref[c, col, pl.ds(s * points + pl.multiple_of(g0 * tall, tall) + b * SUB, SUB)]
                        for c in range(3)
                    ]
                    for b in range(g_block)
                ]
                for k in ks:
                    for c in range(3):
                        at = s * count + first + k
                        left = jnp.broadcast_to(rhat_ref[c, col, at : at + 1], (SUB, LANES))
                        for b in range(g_block):
                            term = left * right[b][c]
                            acc[k, b, c] = term if s == 0 else acc[k, b, c] + term
            for k in ks:
                re = jnp.concatenate([acc[k, b, 0] + acc[k, b, 1] for b in range(g_block)], axis=0)
                im = jnp.concatenate([acc[k, b, 0] - acc[k, b, 2] for b in range(g_block)], axis=0)
                at = pl.ds(k * points + pl.multiple_of(g0 * tall, tall), tall)
                lanes = rows_at(2 * col * LANES, LANES)
                others = rows_at((2 * col + 1) * LANES, LANES)
                high_ref[at, lanes], low_ref[at, lanes] = split(re)
                high_ref[at, others], low_ref[at, others] = split(im)
        return 0

    lax.fori_loop(0, cols * blocks, product, 0)
    high, low = high_ref[...], low_ref[...]
    upper, lower = inverse_ref[: 2 * length], inverse_ref[2 * length :]
    data = dot(high, upper) + dot(high, lower) + dot(low, upper)
    return data.reshape(some, points, length)


def others_kernel(
    own,
    count,
    scale_ref,
    group_ref,
    pred_ref,
    corr_ref,
    khat_ref,
    table_ref,
    inverse_ref,
    rest_ref,
    rhat_ref,
    high_ref,
    low_ref,
):
    sensors = scale_ref.shape[0]
    length = pred_ref.shape[1]
    groups = corr_ref.shape[1] // length
    pred = pred_ref[...]
    high, low = split(pred)
    mixed = dot(jnp.concatenate([high, high], axis=1), corr_ref[...]) + dot(low, corr_ref[:length])
    whole = []
    for s in range(sensors):
        at = slice(s * count, (s + 1) * count)
        value = pred[at]
        for g in range(groups):
            weight = jnp.where(group_ref[s] == g, 1.0, 0.0)
            value = value + weight * mixed[at, g * length : (g + 1) * length]
        whole.append(value * (scale_ref[s] * (1.0 / (length * length))))
    high, low = split(jnp.concatenate(whole, axis=0))
    hat = dot(jnp.concatenate([high, high, low], axis=1), table_ref[...])
    for col in range(length // LANES):
        real = hat[:, 2 * col * LANES : (2 * col + 1) * LANES]
        imag = hat[:, (2 * col + 1) * LANES : (2 * col + 2) * LANES]
        rhat_ref[0, col] = real + imag
        rhat_ref[1, col] = imag
        rhat_ref[2, col] = real
    rest_ref[...] = correlate(own, count, rhat_ref, khat_ref, inverse_ref, high_ref, low_ref)


def own_kernel(count, rhat_ref, khat_ref, inverse_ref, prior_ref, out_ref, high_ref, low_ref):
    data = correlate(0, count, rhat_ref, khat_ref, inverse_ref, high_ref, low_ref)
    out_ref[...] = data + prior_ref[...]


def adjoint_others(pred, scale, group, correlation, khat, table, inverse, own, count):
    rows, length = pred.shape
    points = khat.shape[2] // (rows // count)
    vmem = pl.BlockSpec(memory_space=pltpu.VMEM)
    smem = pl.BlockSpec(memory_space=pltpu.SMEM)
    some = count - own
    return pl.pallas_call(
        functools.partial(others_kernel, own, count),
        out_shape=(
            pltpu.VMEM((some, points, length), F32),
            pltpu.VMEM((3, length // LANES, rows, LANES), F32),
        ),
        in_specs=[smem] * 2 + [vmem] * 5,
        out_specs=[vmem, vmem],
        scratch_shapes=[pltpu.VMEM((some * points, 2 * length), BF16)] * 2,
        compiler_params=pltpu.CompilerParams(vmem_limit_bytes=12 * 1024 * 1024),
        cost_estimate=pl.CostEstimate(flops=1, bytes_accessed=1, transcendentals=0),
    )(scale, group, *map(in_vmem, (pred, correlation, khat, table, inverse)))


def adjoint_own(rhat, khat, inverse, prior, count):
    own, points, length = prior.shape
    vmem = pl.BlockSpec(memory_space=pltpu.VMEM)
    return pl.pallas_call(
        functools.partial(own_kernel, count),
        out_shape=pltpu.VMEM((own, points, length), F32),
        in_specs=[vmem] * 4,
        out_specs=vmem,
        scratch_shapes=[pltpu.VMEM((own * points, 2 * length), BF16)] * 2,
        compiler_params=pltpu.CompilerParams(vmem_limit_bytes=12 * 1024 * 1024),
        cost_estimate=pl.CostEstimate(
            flops=6 * own * points * length * length * 2, bytes_accessed=4 * khat.size, transcendentals=0
        ),
    )(*map(in_vmem, (rhat, khat, inverse, prior)))


def turned_kernel(corr_ref, out_ref):
    groups, length, _ = corr_ref.shape
    for g in range(groups):
        lanes = slice(g * length, (g + 1) * length)
        out_ref[:length, lanes], out_ref[length:, lanes] = split(corr_ref[g].T)


def turned(correlation):
    groups, length, _ = correlation.shape
    vmem = pl.BlockSpec(memory_space=pltpu.VMEM)
    return pl.pallas_call(
        turned_kernel,
        out_shape=pltpu.VMEM((2 * length, groups * length), BF16),
        in_specs=[vmem],
        out_specs=vmem,
        compiler_params=pltpu.CompilerParams(vmem_limit_bytes=8 * 1024 * 1024),
    )(in_vmem(correlation))


def add_kernel(*refs):
    total = refs[0][...]
    for ref in refs[1:-1]:
        total = total + ref[...]
    refs[-1][...] = total


def add(*parts):
    vmem = pl.BlockSpec(memory_space=pltpu.VMEM)
    return pl.pallas_call(
        add_kernel,
        out_shape=jax.ShapeDtypeStruct(parts[0].shape, F32),
        in_specs=[vmem] * len(parts),
        out_specs=vmem,
        compiler_params=pltpu.CompilerParams(vmem_limit_bytes=4 * 1024 * 1024),
    )(*map(in_vmem, parts))


def prior_kernel(vec_ref, first_ref, second_ref, stiff_ref, coup_ref, near_ref, out_ref):
    own, points, _ = out_ref.shape
    place_here = lax.axis_index("pts")
    shift = lax.axis_index("sens") * own
    halo = first_ref.shape[1]
    count = vec_ref.shape[0]
    span = points + 2 * halo
    place = lax.broadcasted_iota(jnp.int32, (span, points), 0)
    coup = coup_ref[...]
    here = lax.broadcasted_iota(jnp.int32, (span, points), 1) + halo
    diagonal = stiff_ref[...] + jnp.sum(coup, axis=0, keepdims=True)
    weight = jnp.where(place == here, diagonal, 0.0)
    near = near_ref[...] - (place_here * points - halo)
    swap = (1 - place_here % 2) * (points + halo)
    near = near + jnp.where(near < halo, swap, 0) - jnp.where(near >= points + halo, swap, 0)
    for j in range(coup.shape[0]):
        weight = weight - jnp.where(place == near[j : j + 1], coup[j : j + 1], 0.0)
    weight_high, weight_low = split(weight.T)
    for k in range(own):
        value = jnp.concatenate(
            [first_ref[k], vec_ref[lax.rem(shift + k, count)], second_ref[k]], axis=0
        )
        high, low = split(value)
        out_ref[k] = dot(weight_high, high) + dot(weight_high, low) + dot(weight_low, high)


def prior_term(vectors, first, second, stiffness, couplings, neighbors):
    own = first.shape[0]
    _, points, length = vectors.shape
    vmem = pl.BlockSpec(memory_space=pltpu.VMEM)
    return pl.pallas_call(
        prior_kernel,
        out_shape=pltpu.VMEM((own, points, length), F32),
        in_specs=[vmem] * 6,
        out_specs=vmem,
        compiler_params=pltpu.CompilerParams(vmem_limit_bytes=8 * 1024 * 1024),
    )(
        *map(in_vmem, (vectors, first, second, stiffness[None], couplings, neighbors))
    )


def stages(size):
    bits = [1 << bit for bit in range(size.bit_length() - 1)]
    masks = []
    while bits:
        low, *bits = bits
        masks.append([low])
        if bits:
            high, *bits = bits
            masks[-1] += [high, low + high]
    turned = list(masks)
    if len(masks) > 1 and len(masks[0]) == len(masks[1]):
        turned[0], turned[1] = masks[1], masks[0]
    return masks, turned


def local(table, inverse, kernel, vectors, noise_scale, sensor_group, correlation, stiffness, couplings, neighbors):
    sensors, points, length = kernel.shape
    count = vectors.shape[0]
    n_sens, n_pts = lax.axis_size("sens"), lax.axis_size("pts")
    own = count // n_sens

    pred, khat, table, inverse, vectors, correlation, *edges = forward(
        kernel, vectors, table, inverse, correlation, own
    )
    correlation = turned(correlation)

    links = [[], []]
    for s in range(n_sens):
        for p in range(n_pts - 1):
            here = s * n_pts + p
            links[p % 2] += [(here, here + 1), (here + 1, here)]
        if n_sens % 2 == 0:
            for p in (0, n_pts - 1):
                links[1].append((s * n_pts + p, (s ^ 1) * n_pts + p))
    halos = []
    for step, (even, odd) in enumerate(zip(*stages(n_pts))):
        if step == 1:
            pred, edges[1] = lax.optimization_barrier((pred, edges[1]))
        more = []
        for mask_even, mask_odd in zip(even, odd):
            pairs = [
                (s * n_pts + p, s * n_pts + (p ^ (mask_odd if s % 2 else mask_even)))
                for s in range(n_sens)
                for p in range(n_pts)
            ]
            more.append(lax.ppermute(pred, ("sens", "pts"), pairs))
        if step < 2:
            halos.append(lax.ppermute(edges[step], ("sens", "pts"), links[step]))
        for part in more:
            pred = pred + part
        if step == 0:
            pred, halos[0], correlation = lax.optimization_barrier((pred, halos[0], correlation))

    rest, rhat = adjoint_others(pred, noise_scale, sensor_group, correlation, khat, table, inverse, own, count)
    rest, halos[1] = lax.optimization_barrier((rest, halos[1]))
    received = []
    for j in range(1, n_sens):
        pairs = [(s, (s + j) % n_sens) for s in range(n_sens)]
        received.append(lax.ppermute(rest[(j - 1) * own : j * own], "sens", pairs))
    prior = prior_term(vectors, halos[0], halos[1], stiffness, couplings, neighbors)
    total = adjoint_own(rhat, khat, inverse, prior, count)
    return add(total, *received)


def solution(mesh):
    in_specs = (
        P(),
        P(),
        P("sens", "pts", None),
        P(None, "pts", None),
        P("sens"),
        P("sens"),
        P(),
        P("pts"),
        P(None, "pts"),
        P(None, "pts"),
    )
    out_specs = P("sens", "pts", None)
    mapped = jax.shard_map(local, mesh=mesh, in_specs=in_specs, out_specs=out_specs, check_vma=False)

    def run(kernel, *rest):
        tables = map(jnp.asarray, dft_tables(kernel.shape[-1]))
        return mapped(*tables, kernel, *rest)

    return run
```

time: 38.6 us -> 34.5 us (0.89)
  the two profiles are of different devices: /device:TPU:25 before, /device:TPU:1 now
where the time goes in v3:
time: 34.5 us; the launch traced here: 34.3 us
  starting transfers between devices  17.5 us (51%)
  Pallas kernels  13.9 us (40%)
  waiting for transfers between devices  2.67 us (8%)
    ppermute x6, starting transfers between devices, local(): more.append(lax.ppermute(pred, ('sens', 'pts'), pairs))  7.33 us
    pallas_call x1, Pallas kernels, forward(): pl.pallas_call(forward_kernel, out_shape=(pltpu.VMEM((sensors * count, le...  6.86 us
    ppermute x1, starting transfers between devices, local(): received.append(lax.ppermute(rest[(j - 1) * own:j * own], 'sens', pairs))  5.6 us
    ppermute x2, starting transfers between devices, local(): halos.append(lax.ppermute(edges[step], ('sens', 'pts'), links[step]))  4.6 us
    pallas_call x1, Pallas kernels, adjoint_others(): pl.pallas_call(functools.partial(others_kernel, own, count), out_shape=(p...  3.48 us
    ppermute x6, waiting for transfers between devices, local(): more.append(lax.ppermute(pred, ('sens', 'pts'), pairs))  2.63 us
    pallas_call x1, Pallas kernels, adjoint_own(): pl.pallas_call(functools.partial(own_kernel, count), out_shape=pltpu.VMEM...  1.72 us
    pallas_call x1, Pallas kernels, add(): pl.pallas_call(add_kernel, out_shape=jax.ShapeDtypeStruct(parts[0].shape,...  0.79 us
  transfers between devices with their start and end apart: 9, of which 3 were waited for; matrix products, arithmetic and copies ran while one was open for 0% of the time, Pallas kernels for 18%

profile of v3, /device:TPU:1, one launch (start us, length us, event | category | flops | bytes accessed | tf_op | source)
XLA Modules:
  0.0 34.3 jit_solution(16998994125288578406)
XLA Ops:
  0.0 6.9 %shard_map.100 = (f32[64,384]{1,0:T(8,128)S(1)}, f32[3,3,512,128]{3,2,1,0:T(8,128)S(1)}, bf16[1152,768]{1,0:T(8,128)(2,1)S(1)}, bf16[1536,384]{1,0:T(8,128)(2,1)...) custom-call(f32[8,64,384]{2,1,0:T(8,128)} %kern_hbm.1, ...), custom_call_target="tpu_custom_call" | custom-call | tf_op jit(solution)/shard_map/pallas_call | solution.py:178
  6.9 4.2 %collective-permute-start.2 = (f32[64,384]{1,0:T(8,128)S(1)}, f32[64,384]{1,0:T(8,128)S(1)}, u32[]{:S(2)}, u32[]{:S(2)}) collective-permute-start(f32[64,384]{1,0:T(8,128)S(1)} %get-tuple-element.22), channel_id=1, source_target_pairs={{0,3},{1,2},{2,1},{3,0},{4,7},{5,6},{6,5},{7,4},{8,11},{9,10},{10,... | collective-permute-start | bytes 294920 | tf_op jit(solution)/shard_map/ppermute | solution.py:454
  11.1 0.0 collective-permute-start.1
  11.1 0.4 %collective-permute-start = (f32[64,384]{1,0:T(8,128)S(1)}, f32[64,384]{1,0:T(8,128)S(1)}, u32[]{:S(2)}, u32[]{:S(2)}) collective-permute-start(f32[64,384]{1,0:T(8,128)S(1)} %get-tuple-element.22), channel_id=1, source_target_pairs={{0,1},{1,0},{2,3},{3,2},{4,5},{5,4},{6,7},{7,6},{8,9},{9,8},{10,11... | collective-permute-start | bytes 294920 | tf_op jit(solution)/shard_map/ppermute | solution.py:454
  11.4 1.2 %collective-permute-start.3 = (f32[4,16,384]{2,1,0:T(8,128)S(1)}, f32[4,16,384]{2,1,0:T(8,128)S(1)}, u32[]{:S(2)}, u32[]{:S(2)}) collective-permute-start(f32[4,16,384]{2,1,0:T(8,128)S(1)} %get-tuple-element.23), channel_id=1, source_target_pairs={{0,1},{1,0},{2,3},{3,2},{4,5},{5,4},{6,7},{7,6},{8,9},{9,8},{10,11... | collective-permute-start | bytes 294920 | tf_op jit(solution)/shard_map/ppermute | solution.py:456
  12.7 0.7 %shard_map.101.corr_ref = bf16[768,1536]{1,0:T(8,128)(2,1)S(1)} custom-call(f32[4,384,384]{2,1,0:T(8,128)S(1)} %get-tuple-element.24.corr_ref), custom_call_target="tpu_custom_call" | custom-call | tf_op jit(solution)/shard_map/pallas_call | solution.py:341
  13.4 2.2 %collective-permute-done.1 = f32[64,384]{1,0:T(8,128)S(1)} collective-permute-done((f32[64,384]{1,0:T(8,128)S(1)}, f32[64,384]{1,0:T(8,128)S(1)}, u32[]{:S(2)}, u32[]{:S(2)}) %collective-permute-start.1) | collective-permute-done | bytes 98336 | tf_op jit(solution)/shard_map/ppermute | solution.py:454
  15.6 0.3 collective-permute-done
  15.9 0.0 collective-permute-done.3.first_ref
  16.0 2.4 %collective-permute-start.6 = (f32[64,384]{1,0:T(8,128)S(1)}, f32[64,384]{1,0:T(8,128)S(1)}, u32[]{:S(2)}, u32[]{:S(2)}) collective-permute-start(f32[64,384]{1,0:T(8,128)S(1)} %add_add_fusion.1), channel_id=1, source_target_pairs={{0,12},{1,13},{2,14},{3,15},{4,8},{5,9},{6,10},{7,11},{8,4},{9,5},... | collective-permute-start | bytes 294920 | tf_op jit(solution)/shard_map/ppermute | solution.py:454
  18.4 0.4 %collective-permute-start.5 = (f32[64,384]{1,0:T(8,128)S(1)}, f32[64,384]{1,0:T(8,128)S(1)}, u32[]{:S(2)}, u32[]{:S(2)}) collective-permute-start(f32[64,384]{1,0:T(8,128)S(1)} %add_add_fusion.1), channel_id=1, source_target_pairs={{0,8},{1,9},{2,10},{3,11},{4,12},{5,13},{6,14},{7,15},{8,0},{9,1},... | collective-permute-start | bytes 294920 | tf_op jit(solution)/shard_map/ppermute | solution.py:454
  18.7 3.4 %collective-permute-start.7 = (f32[4,16,384]{2,1,0:T(8,128)S(1)}, f32[4,16,384]{2,1,0:T(8,128)S(1)}, u32[]{:S(2)}, u32[]{:S(2)}) collective-permute-start(f32[4,16,384]{2,1,0:T(8,128)S(1)} %get-tuple-element.36), channel_id=1, source_target_pairs={{1,2},{2,1},{3,4},{4,3},{5,6},{6,5},{7,8},{8,7},{9,10},{10,9},{11,... | collective-permute-start | bytes 294920 | tf_op jit(solution)/shard_map/ppermute | solution.py:456
  22.1 0.0 collective-permute-done.6
  22.1 0.0 collective-permute-done.5
  22.1 0.1 collective-permute-done.4
  22.2 0.0 copy-start
  22.2 0.0 copy-start.1
  22.3 0.0 copy-start.2
  22.3 3.5 %shard_map.102 = (f32[4,64,384]{2,1,0:T(8,128)S(1)}, f32[3,3,64,128]{3,2,1,0:T(8,128)S(1)}) custom-call(f32[8]{0:T(128)S(1)} %copy-done.3, s32[8]{0:T(128)S(1)} %copy-done.4, f32[64,384]{1,0:T(8,128)S(1)} %add_add_fusion.pred_ref, bf16[768,1536]{1,0:T(8,128)(2,1)S(1)} %shard_map.101.corr_ref, f32[3,3,512,128]{3,2,1,0:T(8,128)S(1)} %get-tuple-element.29.khat_ref, ...), custom_call_target="tpu_custom_call" | custom-call | flops 1 | bytes 1 | tf_op jit(solution)/shard_map/pallas_call | solution.py:301
  25.8 5.6 %collective-permute-start.8 = (f32[4,64,384]{2,1,0:T(8,128)S(1)}, f32[4,64,384]{2,1,0:T(8,128)S(1)}, u32[]{:S(2)}, u32[]{:S(2)}) collective-permute-start(f32[4,64,384]{2,1,0:T(8,128)S(1)} %get-tuple-element.38), channel_id=1, source_target_pairs={{0,16},{16,0},{1,17},{17,1},{2,18},{18,2},{3,19},{19,3},{4,20},{20... | collective-permute-start | bytes 1179656 | tf_op jit(solution)/shard_map/ppermute | solution.py:467
  31.4 0.4 %shard_map.103.prior_ref = f32[4,64,384]{2,1,0:T(8,128)S(1)} custom-call(f32[8,64,384]{2,1,0:T(8,128)S(1)} %get-tuple-element.33.vec_ref, f32[4,16,384]{2,1,0:T(8,128)S(1)} %collective-permute-done.3.first_ref, f32[4,16,384]{2,1,0:T(8,128)S(1)} %collective-permute-done.7.second_ref, f32[1,64]{1,0:T(1,128)S(1)} %bitcast.1, f32[4,64]{1,0:T(4,128)S(1)} %copy-done, ...), custom_call_target="tpu_custom_call" | custom-call | tf_op jit(solution)/shard_map/pallas_call | solution.py:398
  31.8 1.7 %shard_map.104.refs_0_ = f32[4,64,384]{2,1,0:T(8,128)S(1)} custom-call(f32[3,3,64,128]{3,2,1,0:T(8,128)S(1)} %get-tuple-element.32.rhat_ref, f32[3,3,512,128]{3,2,1,0:T(8,128)S(1)} %get-tuple-element.29.khat_ref, bf16[1536,384]{1,0:T(8,128)(2,1)S(1)} %get-tuple-element.31.inverse_ref, f32[4,64,384]{2,1,0:T(8,128)S(1)} %shard_map.103.prior_ref), custom_call_target="tpu_custom_call" | custom-call | flops 452984832 | bytes 2359296 | tf_op jit(solution)/shard_map/pallas_call | solution.py:318
  33.5 0.0 collective-permute-done.8.refs_1_
  33.5 0.8 %shard_map.105 = f32[4,64,384]{2,1,0:T(8,128)} custom-call(f32[4,64,384]{2,1,0:T(8,128)S(1)} %shard_map.104.refs_0_, f32[4,64,384]{2,1,0:T(8,128)S(1)} %collective-permute-done.8.refs_1_), custom_call_target="tpu_custom_call" | custom-call | tf_op jit(solution)/shard_map/pallas_call | solution.py:359
  (12 shorter events, 0.1 us)
Async XLA Ops:
  6.9 6.5 %collective-permute-start.2 = (f32[64,384]{1,0:T(8,128)S(1)}, f32[64,384]{1,0:T(8,128)S(1)}, u32[]{:S(2)}, u32[]{:S(2)}) collective-permute-start(f32[64,384]{1,0:T(8,128)S(1)} %get-tuple-element.22), channel_id=1, source_target_pairs={{0,3},{1,2},{2,1},{3,0},{4,7},{5,6},{6,5},{7,4},{8,11},{9,10},{10,... | collective-permute-start | bytes 294920 | tf_op jit(solution)/shard_map/ppermute | solution.py:454
  11.1 4.5 %collective-permute-start.1 = (f32[64,384]{1,0:T(8,128)S(1)}, f32[64,384]{1,0:T(8,128)S(1)}, u32[]{:S(2)}, u32[]{:S(2)}) collective-permute-start(f32[64,384]{1,0:T(8,128)S(1)} %get-tuple-element.22), channel_id=1, source_target_pairs={{0,2},{1,3},{2,0},{3,1},{4,6},{5,7},{6,4},{7,5},{8,10},{9,11},{10,... | collective-permute-start | bytes 294920 | tf_op jit(solution)/shard_map/ppermute | solution.py:454
  11.1 4.8 %collective-permute-start = (f32[64,384]{1,0:T(8,128)S(1)}, f32[64,384]{1,0:T(8,128)S(1)}, u32[]{:S(2)}, u32[]{:S(2)}) collective-permute-start(f32[64,384]{1,0:T(8,128)S(1)} %get-tuple-element.22), channel_id=1, source_target_pairs={{0,1},{1,0},{2,3},{3,2},{4,5},{5,4},{6,7},{7,6},{8,9},{9,8},{10,11... | collective-permute-start | bytes 294920 | tf_op jit(solution)/shard_map/ppermute | solution.py:454
  11.4 4.5 %collective-permute-start.3 = (f32[4,16,384]{2,1,0:T(8,128)S(1)}, f32[4,16,384]{2,1,0:T(8,128)S(1)}, u32[]{:S(2)}, u32[]{:S(2)}) collective-permute-start(f32[4,16,384]{2,1,0:T(8,128)S(1)} %get-tuple-element.23), channel_id=1, source_target_pairs={{0,1},{1,0},{2,3},{3,2},{4,5},{5,4},{6,7},{7,6},{8,9},{9,8},{10,11... | collective-permute-start | bytes 294920 | tf_op jit(solution)/shard_map/ppermute | solution.py:456
  12.7 9.6 %copy-start.3 = (f32[8]{0:T(128)S(1)}, f32[8]{0:T(128)}, u32[]{:S(2)}) copy-start(f32[8]{0:T(128)} %scale_ref.1) | copy-start | bytes 100
  12.7 9.6 %copy-start.4 = (s32[8]{0:T(128)S(1)}, s32[8]{0:T(128)}, u32[]{:S(2)}) copy-start(s32[8]{0:T(128)} %group_ref.1) | copy-start | bytes 100
  16.0 6.1 %collective-permute-start.6 = (f32[64,384]{1,0:T(8,128)S(1)}, f32[64,384]{1,0:T(8,128)S(1)}, u32[]{:S(2)}, u32[]{:S(2)}) collective-permute-start(f32[64,384]{1,0:T(8,128)S(1)} %add_add_fusion.1), channel_id=1, source_target_pairs={{0,12},{1,13},{2,14},{3,15},{4,8},{5,9},{6,10},{7,11},{8,4},{9,5},... | collective-permute-start | bytes 294920 | tf_op jit(solution)/shard_map/ppermute | solution.py:454
  18.4 3.8 %collective-permute-start.5 = (f32[64,384]{1,0:T(8,128)S(1)}, f32[64,384]{1,0:T(8,128)S(1)}, u32[]{:S(2)}, u32[]{:S(2)}) collective-permute-start(f32[64,384]{1,0:T(8,128)S(1)} %add_add_fusion.1), channel_id=1, source_target_pairs={{0,8},{1,9},{2,10},{3,11},{4,12},{5,13},{6,14},{7,15},{8,0},{9,1},... | collective-permute-start | bytes 294920 | tf_op jit(solution)/shard_map/ppermute | solution.py:454
  18.7 3.5 %collective-permute-start.4 = (f32[64,384]{1,0:T(8,128)S(1)}, f32[64,384]{1,0:T(8,128)S(1)}, u32[]{:S(2)}, u32[]{:S(2)}) collective-permute-start(f32[64,384]{1,0:T(8,128)S(1)} %add_add_fusion.1), channel_id=1, source_target_pairs={{0,4},{1,5},{2,6},{3,7},{4,0},{5,1},{6,2},{7,3},{8,12},{9,13},{10,... | collective-permute-start | bytes 294920 | tf_op jit(solution)/shard_map/ppermute | solution.py:454
  18.7 7.0 %collective-permute-start.7 = (f32[4,16,384]{2,1,0:T(8,128)S(1)}, f32[4,16,384]{2,1,0:T(8,128)S(1)}, u32[]{:S(2)}, u32[]{:S(2)}) collective-permute-start(f32[4,16,384]{2,1,0:T(8,128)S(1)} %get-tuple-element.36), channel_id=1, source_target_pairs={{1,2},{2,1},{3,4},{4,3},{5,6},{6,5},{7,8},{8,7},{9,10},{10,9},{11,... | collective-permute-start | bytes 294920 | tf_op jit(solution)/shard_map/ppermute | solution.py:456
  22.2 9.1 %copy-start = (f32[4,64]{1,0:T(4,128)S(1)}, f32[4,64]{1,0:T(4,128)}, u32[]{:S(2)}) copy-start(f32[4,64]{1,0:T(4,128)} %coup_ref.1) | copy-start | bytes 3076
  22.2 9.1 %copy-start.1 = (s32[4,64]{1,0:T(4,128)S(1)}, s32[4,64]{1,0:T(4,128)}, u32[]{:S(2)}) copy-start(s32[4,64]{1,0:T(4,128)} %near_ref.1) | copy-start | bytes 3076
  22.3 9.1 %copy-start.2 = (f32[64]{0:T(128)S(1)}, f32[64]{0:T(128)}, u32[]{:S(2)}) copy-start(f32[64]{0:T(128)} %param.15) | copy-start | bytes 772
  25.8 7.7 %collective-permute-start.8 = (f32[4,64,384]{2,1,0:T(8,128)S(1)}, f32[4,64,384]{2,1,0:T(8,128)S(1)}, u32[]{:S(2)}, u32[]{:S(2)}) collective-permute-start(f32[4,64,384]{2,1,0:T(8,128)S(1)} %get-tuple-element.38), channel_id=1, source_target_pairs={{0,16},{16,0},{1,17},{17,1},{2,18},{18,2},{3,19},{19,3},{4,20},{20... | collective-permute-start | bytes 1179656 | tf_op jit(solution)/shard_map/ppermute | solution.py:467

commit v4 on v3

--- a/solution.py
+++ b/solution.py
@@ -54,10 +54,23 @@
     return pl.ds(pl.multiple_of(start, size), size)
 
 
-def back_column(high, low, inverse_ref, col):
+def sums(parts):
+    row = lax.broadcasted_iota(jnp.int32, parts[0].shape, 0)
+    width = 1
+    while len(parts) > 1:
+        first = row // width % 2 == 0
+        parts = [
+            jnp.where(first, a, b) + pltpu.roll(jnp.where(first, b, a), width, 0)
+            for a, b in zip(parts[::2], parts[1::2])
+        ]
+        width *= 2
+    return parts[0]
+
+
+def back(high_ref, low_ref, inverse_ref):
     half = inverse_ref.shape[0] // 2
-    upper = inverse_ref[2 * col * LANES : 2 * (col + 1) * LANES]
-    lower = inverse_ref[half + 2 * col * LANES : half + 2 * (col + 1) * LANES]
+    high, low = high_ref[...], low_ref[...]
+    upper, lower = inverse_ref[:half], inverse_ref[half:]
     return dot(high, upper) + dot(high, lower) + dot(low, upper)
 
 
@@ -79,6 +92,8 @@
     vhat_ref,
     kern_lhs_ref,
     vec_lhs_ref,
+    high_ref,
+    low_ref,
     sems,
 ):
     sensors, points, length = kern_ref.shape
@@ -124,26 +139,27 @@
 
     def vec_column(col):
         real, imag = transform(vec_lhs_ref, col)
-        for k in range(count):
-            re, im = real[k * points : (k + 1) * points], imag[k * points : (k + 1) * points]
-            at = pl.ds(k, points, stride=count)
-            vhat_ref[0, col, at] = re + im
-            vhat_ref[1, col, at] = re
-            vhat_ref[2, col, at] = im
+        vhat_ref[0, col] = real + imag
+        vhat_ref[1, col] = real
+        vhat_ref[2, col] = imag
 
     def product(col):
-        acc = [[None] * 3 for _ in range(sensors)]
-        for p in range(points):
-            left = [vhat_ref[c, col, p * count : (p + 1) * count] for c in range(3)]
-            for s in range(sensors):
-                for c in range(3):
-                    row = khat_ref[c, col, s * points + p : s * points + p + 1]
-                    term = left[c] * jnp.broadcast_to(row, left[c].shape)
-                    acc[s][c] = term if acc[s][c] is None else acc[s][c] + term
-        real = jnp.concatenate([one - three for one, _, three in acc], axis=0)
-        imag = jnp.concatenate([one + two for one, two, _ in acc], axis=0)
-        high, low = split(jnp.concatenate([real, imag], axis=1))
-        return back_column(high, low, inverse_ref, col)
+        rows = []
+        for s in range(sensors):
+            acc = [[None] * 3 for _ in range(count)]
+            for g in range(points // SUB):
+                at = s * points + g * SUB
+                right = [khat_ref[c, col, at : at + SUB] for c in range(3)]
+                for k in range(count):
+                    for c in range(3):
+                        at = k * points + g * SUB
+                        term = vhat_ref[c, col, at : at + SUB] * right[c]
+                        acc[k][c] = term if acc[k][c] is None else acc[k][c] + term
+            real = sums([one - three for one, _, three in acc])
+            imag = sums([one + two for one, two, _ in acc])
+            rows.append(jnp.concatenate([real, imag], axis=1))
+        lanes = slice(2 * col * LANES, 2 * (col + 1) * LANES)
+        high_ref[:, lanes], low_ref[:, lanes] = split(jnp.concatenate(rows, axis=0))
 
     copies[0].wait()
     fill(kern_ref, kern_lhs_ref, 0)
@@ -159,14 +175,13 @@
         second_ref[k] = vec_ref[at, rows_at(odd_place * step_in, halo)]
     for copy in copies[4:-1]:
         copy.wait()
-    pred = None
+    vec_column(0)
     for col in range(cols):
-        if col:
-            kern_column(col)
-        vec_column(col)
-        part = product(col)
-        pred = part if pred is None else pred + part
-    pred_ref[...] = pred
+        if col + 1 < cols:
+            kern_column(col + 1)
+            vec_column(col + 1)
+        product(col)
+    pred_ref[...] = back(high_ref, low_ref, inverse_ref)
     copies[-1].wait()
 
 
@@ -194,57 +209,58 @@
             pltpu.VMEM((3, cols, count * points, LANES), F32),
             pltpu.VMEM((sensors * points, 3 * length), BF16),
             pltpu.VMEM((count * points, 3 * length), BF16),
+            pltpu.VMEM((sensors * count, 2 * length), BF16),
+            pltpu.VMEM((sensors * count, 2 * length), BF16),
             pltpu.SemaphoreType.DMA((4 + 2 * cols,)),
         ],
         compiler_params=pltpu.CompilerParams(vmem_limit_bytes=14 * 1024 * 1024),
     )(*map(in_hbm, (kernel, vectors, table, inverse, correlation)))
 
 
-def correlate(first, count, rhat_ref, khat_ref, inverse_ref, high_ref, low_ref):
-    length = inverse_ref.shape[1]
+def correlate(first, count, rhat_ref, khat_ref, inverse_ref, high_ref, low_ref, data_ref):
+    some, points, length = data_ref.shape
     sensors = rhat_ref.shape[2] // count
-    points = khat_ref.shape[2] // sensors
     cols = length // LANES
-    some = high_ref.shape[0] // points
     k_block, g_block = 4, 2
     tall = g_block * SUB
-    blocks = points // tall
-
-    def product(step, _):
-        col, g0 = step // blocks, step % blocks
-        for k0 in range(0, some, k_block):
-            ks = range(k0, min(k0 + k_block, some))
-            acc = {}
-            for s in range(sensors):
-                right = [
-                    [
-                        khat_ref[c, col, pl.ds(s * points + pl.multiple_of(g0 * tall, tall) + b * SUB, SUB)]
-                        for c in range(3)
-                    ]
-                    for b in range(g_block)
+
+    def product(col, g0, ks):
+        acc = {}
+        for s in range(sensors):
+            right = [
+                [
+                    khat_ref[c, col, pl.ds(s * points + g0 * tall + b * SUB, SUB)]
+                    for c in range(3)
                 ]
-                for k in ks:
-                    for c in range(3):
-                        at = s * count + first + k
-                        left = jnp.broadcast_to(rhat_ref[c, col, at : at + 1], (SUB, LANES))
-                        for b in range(g_block):
-                            term = left * right[b][c]
-                            acc[k, b, c] = term if s == 0 else acc[k, b, c] + term
+                for b in range(g_block)
+            ]
             for k in ks:
-                re = jnp.concatenate([acc[k, b, 0] + acc[k, b, 1] for b in range(g_block)], axis=0)
-                im = jnp.concatenate([acc[k, b, 0] - acc[k, b, 2] for b in range(g_block)], axis=0)
-                at = pl.ds(k * points + pl.multiple_of(g0 * tall, tall), tall)
-                lanes = rows_at(2 * col * LANES, LANES)
-                others = rows_at((2 * col + 1) * LANES, LANES)
-                high_ref[at, lanes], low_ref[at, lanes] = split(re)
-                high_ref[at, others], low_ref[at, others] = split(im)
-        return 0
-
-    lax.fori_loop(0, cols * blocks, product, 0)
-    high, low = high_ref[...], low_ref[...]
-    upper, lower = inverse_ref[: 2 * length], inverse_ref[2 * length :]
-    data = dot(high, upper) + dot(high, lower) + dot(low, upper)
-    return data.reshape(some, points, length)
+                for c in range(3):
+                    at = s * count + first + k
+                    left = jnp.broadcast_to(rhat_ref[c, col, at : at + 1], (SUB, LANES))
+                    for b in range(g_block):
+                        term = left * right[b][c]
+                        acc[k, b, c] = term if s == 0 else acc[k, b, c] + term
+        for k in ks:
+            re = jnp.concatenate([acc[k, b, 0] + acc[k, b, 1] for b in range(g_block)], axis=0)
+            im = jnp.concatenate([acc[k, b, 0] - acc[k, b, 2] for b in range(g_block)], axis=0)
+            at = slice(k * points + g0 * tall, k * points + (g0 + 1) * tall)
+            lanes = slice(2 * col * LANES, (2 * col + 1) * LANES)
+            others = slice((2 * col + 1) * LANES, (2 * col + 2) * LANES)
+            high_ref[at, lanes], low_ref[at, lanes] = split(re)
+            high_ref[at, others], low_ref[at, others] = split(im)
+
+    for col in range(cols):
+        for g0 in range(points // tall):
+            for k0 in range(0, some, k_block):
+                product(col, g0, range(k0, min(k0 + k_block, some)))
+        lanes = slice(2 * col * LANES, 2 * (col + 1) * LANES)
+        upper = inverse_ref[lanes]
+        lower = inverse_ref[lanes.start + 2 * length : lanes.stop + 2 * length]
+        high, low = high_ref[:, lanes], low_ref[:, lanes]
+        part = dot(high, upper) + dot(high, lower) + dot(low, upper)
+        part = part.reshape(some, points, length)
+        data_ref[...] = data_ref[...] + part if col else part
 
 
 def others_kernel(
@@ -284,12 +300,31 @@
         rhat_ref[0, col] = real + imag
         rhat_ref[1, col] = imag
         rhat_ref[2, col] = real
-    rest_ref[...] = correlate(own, count, rhat_ref, khat_ref, inverse_ref, high_ref, low_ref)
-
-
-def own_kernel(count, rhat_ref, khat_ref, inverse_ref, prior_ref, out_ref, high_ref, low_ref):
-    data = correlate(0, count, rhat_ref, khat_ref, inverse_ref, high_ref, low_ref)
-    out_ref[...] = data + prior_ref[...]
+    correlate(own, count, rhat_ref, khat_ref, inverse_ref, high_ref, low_ref, rest_ref)
+
+
+def own_kernel(
+    count,
+    rhat_ref,
+    khat_ref,
+    inverse_ref,
+    vec_ref,
+    weight_ref,
+    first_ref,
+    second_ref,
+    out_ref,
+    high_ref,
+    low_ref,
+):
+    correlate(0, count, rhat_ref, khat_ref, inverse_ref, high_ref, low_ref, out_ref)
+    own = out_ref.shape[0]
+    sens = lax.axis_index("sens")
+    upper, lower = weight_ref[0], weight_ref[1]
+    for k in range(own):
+        here = vec_ref[lax.rem(sens * own + k, count)]
+        value = jnp.concatenate([first_ref[k], here, second_ref[k]], axis=0)
+        high, low = split(value)
+        out_ref[k] = out_ref[k] + dot(upper, high) + dot(upper, low) + dot(lower, high)
 
 
 def adjoint_others(pred, scale, group, correlation, khat, table, inverse, own, count):
@@ -312,39 +347,59 @@
     )(scale, group, *map(in_vmem, (pred, correlation, khat, table, inverse)))
 
 
-def adjoint_own(rhat, khat, inverse, prior, count):
-    own, points, length = prior.shape
+def adjoint_own(rhat, khat, inverse, vectors, weight, halos, own):
+    count, points, length = vectors.shape
     vmem = pl.BlockSpec(memory_space=pltpu.VMEM)
+    operands = (rhat, khat, inverse, vectors, weight, *halos)
     return pl.pallas_call(
         functools.partial(own_kernel, count),
         out_shape=pltpu.VMEM((own, points, length), F32),
-        in_specs=[vmem] * 4,
+        in_specs=[vmem] * len(operands),
         out_specs=vmem,
         scratch_shapes=[pltpu.VMEM((own * points, 2 * length), BF16)] * 2,
         compiler_params=pltpu.CompilerParams(vmem_limit_bytes=12 * 1024 * 1024),
         cost_estimate=pl.CostEstimate(
             flops=6 * own * points * length * length * 2, bytes_accessed=4 * khat.size, transcendentals=0
         ),
-    )(*map(in_vmem, (rhat, khat, inverse, prior)))
-
-
-def turned_kernel(corr_ref, out_ref):
+    )(*map(in_vmem, operands))
+
+
+def ready_kernel(halo, corr_ref, stiff_ref, coup_ref, near_ref, out_ref, weight_ref):
     groups, length, _ = corr_ref.shape
     for g in range(groups):
         lanes = slice(g * length, (g + 1) * length)
         out_ref[:length, lanes], out_ref[length:, lanes] = split(corr_ref[g].T)
 
-
-def turned(correlation):
+    place_here = lax.axis_index("pts")
+    points = weight_ref.shape[1]
+    span = weight_ref.shape[2]
+    place = lax.broadcasted_iota(jnp.int32, (span, points), 0)
+    here = lax.broadcasted_iota(jnp.int32, (span, points), 1) + halo
+    coup = coup_ref[...]
+    diagonal = stiff_ref[...] + jnp.sum(coup, axis=0, keepdims=True)
+    weight = jnp.where(place == here, diagonal, 0.0)
+    near = near_ref[...] - (place_here * points - halo)
+    swap = (1 - place_here % 2) * (points + halo)
+    near = near + jnp.where(near < halo, swap, 0) - jnp.where(near >= points + halo, swap, 0)
+    for j in range(coup.shape[0]):
+        weight = weight - jnp.where(place == near[j : j + 1], coup[j : j + 1], 0.0)
+    weight_ref[0], weight_ref[1] = split(weight.T)
+
+
+def ready(correlation, stiffness, couplings, neighbors):
     groups, length, _ = correlation.shape
+    points = stiffness.shape[0]
     vmem = pl.BlockSpec(memory_space=pltpu.VMEM)
     return pl.pallas_call(
-        turned_kernel,
-        out_shape=pltpu.VMEM((2 * length, groups * length), BF16),
-        in_specs=[vmem],
-        out_specs=vmem,
+        functools.partial(ready_kernel, COLS),
+        out_shape=(
+            pltpu.VMEM((2 * length, groups * length), BF16),
+            pltpu.VMEM((2, points, points + 2 * COLS), BF16),
+        ),
+        in_specs=[vmem] * 4,
+        out_specs=[vmem] * 2,
         compiler_params=pltpu.CompilerParams(vmem_limit_bytes=8 * 1024 * 1024),
-    )(in_vmem(correlation))
+    )(*map(in_vmem, (correlation, stiffness[None], couplings, neighbors)))
 
 
 def add_kernel(*refs):
@@ -363,47 +418,6 @@
         out_specs=vmem,
         compiler_params=pltpu.CompilerParams(vmem_limit_bytes=4 * 1024 * 1024),
     )(*map(in_vmem, parts))
-
-
-def prior_kernel(vec_ref, first_ref, second_ref, stiff_ref, coup_ref, near_ref, out_ref):
-    own, points, _ = out_ref.shape
-    place_here = lax.axis_index("pts")
-    shift = lax.axis_index("sens") * own
-    halo = first_ref.shape[1]
-    count = vec_ref.shape[0]
-    span = points + 2 * halo
-    place = lax.broadcasted_iota(jnp.int32, (span, points), 0)
-    coup = coup_ref[...]
-    here = lax.broadcasted_iota(jnp.int32, (span, points), 1) + halo
-    diagonal = stiff_ref[...] + jnp.sum(coup, axis=0, keepdims=True)
-    weight = jnp.where(place == here, diagonal, 0.0)
-    near = near_ref[...] - (place_here * points - halo)
-    swap = (1 - place_here % 2) * (points + halo)
-    near = near + jnp.where(near < halo, swap, 0) - jnp.where(near >= points + halo, swap, 0)
-    for j in range(coup.shape[0]):
-        weight = weight - jnp.where(place == near[j : j + 1], coup[j : j + 1], 0.0)
-    weight_high, weight_low = split(weight.T)
-    for k in range(own):
-        value = jnp.concatenate(
-            [first_ref[k], vec_ref[lax.rem(shift + k, count)], second_ref[k]], axis=0
-        )
-        high, low = split(value)
-        out_ref[k] = dot(weight_high, high) + dot(weight_high, low) + dot(weight_low, high)
-
-
-def prior_term(vectors, first, second, stiffness, couplings, neighbors):
-    own = first.shape[0]
-    _, points, length = vectors.shape
-    vmem = pl.BlockSpec(memory_space=pltpu.VMEM)
-    return pl.pallas_call(
-        prior_kernel,
-        out_shape=pltpu.VMEM((own, points, length), F32),
-        in_specs=[vmem] * 6,
-        out_specs=vmem,
-        compiler_params=pltpu.CompilerParams(vmem_limit_bytes=8 * 1024 * 1024),
-    )(
-        *map(in_vmem, (vectors, first, second, stiffness[None], couplings, neighbors))
-    )
 
 
 def stages(size):
@@ -430,7 +444,7 @@
     pred, khat, table, inverse, vectors, correlation, *edges = forward(
         kernel, vectors, table, inverse, correlation, own
     )
-    correlation = turned(correlation)
+    correlation, weight = ready(correlation, stiffness, couplings, neighbors)
 
     links = [[], []]
     for s in range(n_sens):
@@ -442,8 +456,6 @@
                 links[1].append((s * n_pts + p, (s ^ 1) * n_pts + p))
     halos = []
     for step, (even, odd) in enumerate(zip(*stages(n_pts))):
-        if step == 1:
-            pred, edges[1] = lax.optimization_barrier((pred, edges[1]))
         more = []
         for mask_even, mask_odd in zip(even, odd):
             pairs = [
@@ -457,7 +469,9 @@
         for part in more:
             pred = pred + part
         if step == 0:
-            pred, halos[0], correlation = lax.optimization_barrier((pred, halos[0], correlation))
+            pred, halos[0], correlation, edges[1] = lax.optimization_barrier(
+                (pred, halos[0], correlation, edges[1])
+            )
 
     rest, rhat = adjoint_others(pred, noise_scale, sensor_group, correlation, khat, table, inverse, own, count)
     rest, halos[1] = lax.optimization_barrier((rest, halos[1]))
@@ -465,8 +479,7 @@
     for j in range(1, n_sens):
         pairs = [(s, (s + j) % n_sens) for s in range(n_sens)]
         received.append(lax.ppermute(rest[(j - 1) * own : j * own], "sens", pairs))
-    prior = prior_term(vectors, halos[0], halos[1], stiffness, couplings, neighbors)
-    total = adjoint_own(rhat, khat, inverse, prior, count)
+    total = adjoint_own(rhat, khat, inverse, vectors, weight, halos, own)
     return add(total, *received)
 
 

time: 34.5 us -> 32.4 us (0.939)
  the two profiles are of different devices: /device:TPU:1 before, /device:TPU:0 now
where the time goes in v4:
time: 32.4 us; the launch traced here: 32.3 us
  Pallas kernels  11.9 us (37%)
  starting transfers between devices  11 us (34%)
  waiting for transfers between devices  9.22 us (28%)
    ppermute x6, starting transfers between devices, local(): more.append(lax.ppermute(pred, ('sens', 'pts'), pairs))  8.99 us
    ppermute x6, waiting for transfers between devices, local(): more.append(lax.ppermute(pred, ('sens', 'pts'), pairs))  8.14 us
    pallas_call x1, Pallas kernels, forward(): pl.pallas_call(forward_kernel, out_shape=(pltpu.VMEM((sensors * count, le...  5.77 us
    pallas_call x1, Pallas kernels, adjoint_others(): pl.pallas_call(functools.partial(others_kernel, own, count), out_shape=(p...  3.05 us
    ppermute x2, starting transfers between devices, local(): halos.append(lax.ppermute(edges[step], ('sens', 'pts'), links[step]))  1.89 us
    pallas_call x1, Pallas kernels, adjoint_own(): pl.pallas_call(functools.partial(own_kernel, count), out_shape=pltpu.VMEM...  1.64 us
    ppermute x2, waiting for transfers between devices, local(): halos.append(lax.ppermute(edges[step], ('sens', 'pts'), links[step]))  1.03 us
    pallas_call x1, Pallas kernels, add(): pl.pallas_call(add_kernel, out_shape=jax.ShapeDtypeStruct(parts[0].shape,...  0.79 us
  transfers between devices with their start and end apart: 9, of which 6 were waited for; matrix products, arithmetic and copies ran while one was open for 0% of the time, Pallas kernels for 17%

profile of v4, /device:TPU:0, one launch (start us, length us, event | category | flops | bytes accessed | tf_op | source)
XLA Modules:
  0.0 32.3 jit_solution(2639458480351164562)
XLA Ops:
  0.0 5.8 %shard_map.100 = (f32[64,384]{1,0:T(8,128)S(1)}, f32[3,3,512,128]{3,2,1,0:T(8,128)S(1)}, bf16[1152,768]{1,0:T(8,128)(2,1)S(1)}, bf16[1536,384]{1,0:T(8,128)(2,1)...) custom-call(f32[8,64,384]{2,1,0:T(8,128)} %kern_hbm.1, ...), custom_call_target="tpu_custom_call" | custom-call | tf_op jit(solution)/shard_map/pallas_call | solution.py:193
  5.8 0.0 copy-start.2
  5.8 0.0 copy-start.3
  5.8 4.0 %collective-permute-start.2 = (f32[64,384]{1,0:T(8,128)S(1)}, f32[64,384]{1,0:T(8,128)S(1)}, u32[]{:S(2)}, u32[]{:S(2)}) collective-permute-start(f32[64,384]{1,0:T(8,128)S(1)} %get-tuple-element.23), channel_id=1, source_target_pairs={{0,3},{1,2},{2,1},{3,0},{4,7},{5,6},{6,5},{7,4},{8,11},{9,10},{10,... | collective-permute-start | bytes 294920 | tf_op jit(solution)/shard_map/ppermute | solution.py:466
  9.8 0.5 %collective-permute-start.1 = (f32[64,384]{1,0:T(8,128)S(1)}, f32[64,384]{1,0:T(8,128)S(1)}, u32[]{:S(2)}, u32[]{:S(2)}) collective-permute-start(f32[64,384]{1,0:T(8,128)S(1)} %get-tuple-element.23), channel_id=1, source_target_pairs={{0,2},{1,3},{2,0},{3,1},{4,6},{5,7},{6,4},{7,5},{8,10},{9,11},{10,... | collective-permute-start | bytes 294920 | tf_op jit(solution)/shard_map/ppermute | solution.py:466
  10.3 0.1 collective-permute-start
  10.4 1.9 %collective-permute-start.3 = (f32[4,16,384]{2,1,0:T(8,128)S(1)}, f32[4,16,384]{2,1,0:T(8,128)S(1)}, u32[]{:S(2)}, u32[]{:S(2)}) collective-permute-start(f32[4,16,384]{2,1,0:T(8,128)S(1)} %get-tuple-element.24), channel_id=1, source_target_pairs={{0,1},{1,0},{2,3},{3,2},{4,5},{5,4},{6,7},{7,6},{8,9},{9,8},{10,11... | collective-permute-start | bytes 294920 | tf_op jit(solution)/shard_map/ppermute | solution.py:468
  12.3 0.7 %shard_map.101 = (bf16[768,1536]{1,0:T(8,128)(2,1)S(1)}, bf16[2,64,96]{2,1,0:T(8,128)(2,1)S(1)}) custom-call(f32[4,384,384]{2,1,0:T(8,128)S(1)} %get-tuple-element.25.corr_ref, f32[1,64]{1,0:T(1,128)S(1)} %bitcast.1, f32[4,64]{1,0:T(4,128)S(1)} %copy-done, s32[4,64]{1,0:T(4,128)S(1)} %copy-done.1), custom_call_target="tpu_custom_call" | custom-call | tf_op jit(solution)/shard_map/pallas_call | solution.py:393
  13.0 0.0 collective-permute-done.2
  13.0 1.4 %collective-permute-done.1 = f32[64,384]{1,0:T(8,128)S(1)} collective-permute-done((f32[64,384]{1,0:T(8,128)S(1)}, f32[64,384]{1,0:T(8,128)S(1)}, u32[]{:S(2)}, u32[]{:S(2)}) %collective-permute-start.1) | collective-permute-done | bytes 98336 | tf_op jit(solution)/shard_map/ppermute | solution.py:466
  14.4 1.2 %collective-permute-done = f32[64,384]{1,0:T(8,128)S(1)} collective-permute-done((f32[64,384]{1,0:T(8,128)S(1)}, f32[64,384]{1,0:T(8,128)S(1)}, u32[]{:S(2)}, u32[]{:S(2)}) %collective-permute-start) | collective-permute-done | bytes 98336 | tf_op jit(solution)/shard_map/ppermute | solution.py:466
  15.6 1.0 %collective-permute-done.3.first_ref = f32[4,16,384]{2,1,0:T(8,128)S(1)} collective-permute-done((f32[4,16,384]{2,1,0:T(8,128)S(1)}, f32[4,16,384]{2,1,0:T(8,128)S(1)}, u32[]{:S(2)}, u32[]{:S(2)}) %collective-permute-start.3) | collective-permute-done | bytes 98336 | tf_op jit(solution)/shard_map/ppermute | solution.py:468
  16.6 3.5 %collective-permute-start.6 = (f32[64,384]{1,0:T(8,128)S(1)}, f32[64,384]{1,0:T(8,128)S(1)}, u32[]{:S(2)}, u32[]{:S(2)}) collective-permute-start(f32[64,384]{1,0:T(8,128)S(1)} %add_add_fusion.1), channel_id=1, source_target_pairs={{0,12},{1,13},{2,14},{3,15},{4,8},{5,9},{6,10},{7,11},{8,4},{9,5},... | collective-permute-start | bytes 294920 | tf_op jit(solution)/shard_map/ppermute | solution.py:466
  20.1 0.0 collective-permute-start.5
  20.1 0.9 %collective-permute-start.4 = (f32[64,384]{1,0:T(8,128)S(1)}, f32[64,384]{1,0:T(8,128)S(1)}, u32[]{:S(2)}, u32[]{:S(2)}) collective-permute-start(f32[64,384]{1,0:T(8,128)S(1)} %add_add_fusion.1), channel_id=1, source_target_pairs={{0,4},{1,5},{2,6},{3,7},{4,0},{5,1},{6,2},{7,3},{8,12},{9,13},{10,... | collective-permute-start | bytes 294920 | tf_op jit(solution)/shard_map/ppermute | solution.py:466
  21.0 0.0 collective-permute-start.7
  21.0 2.1 %collective-permute-done.6 = f32[64,384]{1,0:T(8,128)S(1)} collective-permute-done((f32[64,384]{1,0:T(8,128)S(1)}, f32[64,384]{1,0:T(8,128)S(1)}, u32[]{:S(2)}, u32[]{:S(2)}) %collective-permute-start.6) | collective-permute-done | bytes 98336 | tf_op jit(solution)/shard_map/ppermute | solution.py:466
  23.1 3.5 %collective-permute-done.5 = f32[64,384]{1,0:T(8,128)S(1)} collective-permute-done((f32[64,384]{1,0:T(8,128)S(1)}, f32[64,384]{1,0:T(8,128)S(1)}, u32[]{:S(2)}, u32[]{:S(2)}) %collective-permute-start.5) | collective-permute-done | bytes 98336 | tf_op jit(solution)/shard_map/ppermute | solution.py:466
  26.6 0.0 collective-permute-done.4
  26.7 3.0 %shard_map.102 = (f32[4,64,384]{2,1,0:T(8,128)S(1)}, f32[3,3,64,128]{3,2,1,0:T(8,128)S(1)}) custom-call(f32[8]{0:T(128)S(1)} %copy-done.2, s32[8]{0:T(128)S(1)} %copy-done.3, f32[64,384]{1,0:T(8,128)S(1)} %add_add_fusion.pred_ref, bf16[768,1536]{1,0:T(8,128)(2,1)S(1)} %get-tuple-element.29.corr_ref, f32[3,3,512,128]{3,2,1,0:T(8,128)S(1)} %get-tuple-element.30.khat_ref, ...), custom_call_target="tpu_custom_call" | custom-call | flops 1 | bytes 1 | tf_op jit(solution)/shard_map/pallas_call | solution.py:336
  29.7 0.1 collective-permute-start.8
  29.8 1.6 %shard_map.103.refs_0_ = f32[4,64,384]{2,1,0:T(8,128)S(1)} custom-call(f32[3,3,64,128]{3,2,1,0:T(8,128)S(1)} %get-tuple-element.33.rhat_ref, f32[3,3,512,128]{3,2,1,0:T(8,128)S(1)} %get-tuple-element.30.khat_ref, bf16[1536,384]{1,0:T(8,128)(2,1)S(1)} %get-tuple-element.32.inverse_ref, f32[8,64,384]{2,1,0:T(8,128)S(1)} %get-tuple-element.34.vec_ref, ...), custom_call_target="tpu_custom_call" | custom-call | flops 452984832 | bytes 2359296 | tf_op jit(solution)/shard_map/pallas_call | solution.py:354
  31.4 0.1 collective-permute-done.8.refs_1_
  31.5 0.8 %shard_map.104 = f32[4,64,384]{2,1,0:T(8,128)} custom-call(f32[4,64,384]{2,1,0:T(8,128)S(1)} %shard_map.103.refs_0_, f32[4,64,384]{2,1,0:T(8,128)S(1)} %collective-permute-done.8.refs_1_), custom_call_target="tpu_custom_call" | custom-call | tf_op jit(solution)/shard_map/pallas_call | solution.py:414
  (11 shorter events, 0.1 us)
Async XLA Ops:
  0.0 12.3 %copy-start.1 = (s32[4,64]{1,0:T(4,128)S(1)}, s32[4,64]{1,0:T(4,128)}, u32[]{:S(2)}) copy-start(s32[4,64]{1,0:T(4,128)} %near_ref.1) | copy-start | bytes 3076
  0.0 12.3 %copy-start = (f32[4,64]{1,0:T(4,128)S(1)}, f32[4,64]{1,0:T(4,128)}, u32[]{:S(2)}) copy-start(f32[4,64]{1,0:T(4,128)} %coup_ref.1) | copy-start | bytes 3076
  0.0 12.3 %copy-start.4 = (f32[64]{0:T(128)S(1)}, f32[64]{0:T(128)}, u32[]{:S(2)}) copy-start(f32[64]{0:T(128)} %param.15) | copy-start | bytes 772
  5.8 20.9 %copy-start.2 = (f32[8]{0:T(128)S(1)}, f32[8]{0:T(128)}, u32[]{:S(2)}) copy-start(f32[8]{0:T(128)} %scale_ref.1) | copy-start | bytes 100
  5.8 20.9 %copy-start.3 = (s32[8]{0:T(128)S(1)}, s32[8]{0:T(128)}, u32[]{:S(2)}) copy-start(s32[8]{0:T(128)} %group_ref.1) | copy-start | bytes 100
  5.8 7.2 %collective-permute-start.2 = (f32[64,384]{1,0:T(8,128)S(1)}, f32[64,384]{1,0:T(8,128)S(1)}, u32[]{:S(2)}, u32[]{:S(2)}) collective-permute-start(f32[64,384]{1,0:T(8,128)S(1)} %get-tuple-element.23), channel_id=1, source_target_pairs={{0,3},{1,2},{2,1},{3,0},{4,7},{5,6},{6,5},{7,4},{8,11},{9,10},{10,... | collective-permute-start | bytes 294920 | tf_op jit(solution)/shard_map/ppermute | solution.py:466
  9.8 4.6 %collective-permute-start.1 = (f32[64,384]{1,0:T(8,128)S(1)}, f32[64,384]{1,0:T(8,128)S(1)}, u32[]{:S(2)}, u32[]{:S(2)}) collective-permute-start(f32[64,384]{1,0:T(8,128)S(1)} %get-tuple-element.23), channel_id=1, source_target_pairs={{0,2},{1,3},{2,0},{3,1},{4,6},{5,7},{6,4},{7,5},{8,10},{9,11},{10,... | collective-permute-start | bytes 294920 | tf_op jit(solution)/shard_map/ppermute | solution.py:466
  10.3 5.3 %collective-permute-start = (f32[64,384]{1,0:T(8,128)S(1)}, f32[64,384]{1,0:T(8,128)S(1)}, u32[]{:S(2)}, u32[]{:S(2)}) collective-permute-start(f32[64,384]{1,0:T(8,128)S(1)} %get-tuple-element.23), channel_id=1, source_target_pairs={{0,1},{1,0},{2,3},{3,2},{4,5},{5,4},{6,7},{7,6},{8,9},{9,8},{10,11... | collective-permute-start | bytes 294920 | tf_op jit(solution)/shard_map/ppermute | solution.py:466
  10.4 6.2 %collective-permute-start.3 = (f32[4,16,384]{2,1,0:T(8,128)S(1)}, f32[4,16,384]{2,1,0:T(8,128)S(1)}, u32[]{:S(2)}, u32[]{:S(2)}) collective-permute-start(f32[4,16,384]{2,1,0:T(8,128)S(1)} %get-tuple-element.24), channel_id=1, source_target_pairs={{0,1},{1,0},{2,3},{3,2},{4,5},{5,4},{6,7},{7,6},{8,9},{9,8},{10,11... | collective-permute-start | bytes 294920 | tf_op jit(solution)/shard_map/ppermute | solution.py:468
  16.6 6.5 %collective-permute-start.6 = (f32[64,384]{1,0:T(8,128)S(1)}, f32[64,384]{1,0:T(8,128)S(1)}, u32[]{:S(2)}, u32[]{:S(2)}) collective-permute-start(f32[64,384]{1,0:T(8,128)S(1)} %add_add_fusion.1), channel_id=1, source_target_pairs={{0,12},{1,13},{2,14},{3,15},{4,8},{5,9},{6,10},{7,11},{8,4},{9,5},... | collective-permute-start | bytes 294920 | tf_op jit(solution)/shard_map/ppermute | solution.py:466
  20.1 6.5 %collective-permute-start.5 = (f32[64,384]{1,0:T(8,128)S(1)}, f32[64,384]{1,0:T(8,128)S(1)}, u32[]{:S(2)}, u32[]{:S(2)}) collective-permute-start(f32[64,384]{1,0:T(8,128)S(1)} %add_add_fusion.1), channel_id=1, source_target_pairs={{0,8},{1,9},{2,10},{3,11},{4,12},{5,13},{6,14},{7,15},{8,0},{9,1},... | collective-permute-start | bytes 294920 | tf_op jit(solution)/shard_map/ppermute | solution.py:466
  20.1 6.5 %collective-permute-start.4 = (f32[64,384]{1,0:T(8,128)S(1)}, f32[64,384]{1,0:T(8,128)S(1)}, u32[]{:S(2)}, u32[]{:S(2)}) collective-permute-start(f32[64,384]{1,0:T(8,128)S(1)} %add_add_fusion.1), channel_id=1, source_target_pairs={{0,4},{1,5},{2,6},{3,7},{4,0},{5,1},{6,2},{7,3},{8,12},{9,13},{10,... | collective-permute-start | bytes 294920 | tf_op jit(solution)/shard_map/ppermute | solution.py:466
  21.0 8.7 %collective-permute-start.7 = (f32[4,16,384]{2,1,0:T(8,128)S(1)}, f32[4,16,384]{2,1,0:T(8,128)S(1)}, u32[]{:S(2)}, u32[]{:S(2)}) collective-permute-start(f32[4,16,384]{2,1,0:T(8,128)S(1)} %get-tuple-element.38), channel_id=1, source_target_pairs={{1,2},{2,1},{3,4},{4,3},{5,6},{6,5},{7,8},{8,7},{9,10},{10,9},{11,... | collective-permute-start | bytes 294920 | tf_op jit(solution)/shard_map/ppermute | solution.py:468
  29.7 1.8 %collective-permute-start.8 = (f32[4,64,384]{2,1,0:T(8,128)S(1)}, f32[4,64,384]{2,1,0:T(8,128)S(1)}, u32[]{:S(2)}, u32[]{:S(2)}) collective-permute-start(f32[4,64,384]{2,1,0:T(8,128)S(1)} %get-tuple-element.40), channel_id=1, source_target_pairs={{0,16},{16,0},{1,17},{17,1},{2,18},{18,2},{3,19},{19,3},{4,20},{20... | collective-permute-start | bytes 1179656 | tf_op jit(solution)/shard_map/ppermute | solution.py:481

commit v5 on v4

--- a/solution.py
+++ b/solution.py
@@ -11,6 +11,7 @@
 from jax.sharding import PartitionSpec as P
 
 COLS = 16
+ORDER = ((1, 2, 0), (1, 0, 2))
 LANES = 128
 SUB = 8
 F32 = jnp.float32
@@ -86,59 +87,61 @@
     inverse_ref,
     vec_ref,
     corr_ref,
-    first_ref,
-    second_ref,
+    edge_ref,
     kern_ref,
     vhat_ref,
-    kern_lhs_ref,
-    vec_lhs_ref,
+    kern_high_ref,
+    kern_low_ref,
+    vec_high_ref,
+    vec_low_ref,
     high_ref,
     low_ref,
     sems,
 ):
     sensors, points, length = kern_ref.shape
     count = vec_ref.shape[0]
-    own, halo, _ = first_ref.shape
-    shift = lax.axis_index("sens") * own
-    odd_place = lax.axis_index("pts") % 2
+    both, halo, _ = edge_ref.shape
+    sens = lax.axis_index("sens")
+    shift = sens * (both // 2)
+    upper_edge = (lax.axis_index("pts") + sens + 1) % 2
     cols = length // LANES
+    kern_halves, vec_halves = (kern_high_ref, kern_low_ref), (vec_high_ref, vec_low_ref)
 
     pairs = [(kern_hbm, kern_ref), (vec_hbm, vec_ref)]
     for col in range(cols):
         lanes = slice(2 * col * LANES, 2 * (col + 1) * LANES)
-        pairs.append((table_hbm.at[:, lanes], table_ref.at[: 2 * length, lanes]))
-        pairs.append((table_hbm.at[:length, lanes], table_ref.at[2 * length :, lanes]))
+        pairs.append((table_hbm.at[:, lanes], table_ref.at[:, lanes]))
     pairs.append((inverse_hbm, inverse_ref))
     pairs.append((corr_hbm, corr_ref))
     copies = [
         pltpu.make_async_copy(source, target, sems.at[i]) for i, (source, target) in enumerate(pairs)
     ]
-    for i in (0, 2, 3, 1, *range(4, len(copies))):
+    for i in (0, 2, 1, *range(3, len(copies))):
         copies[i].start()
 
-    def fill(source_ref, lhs_ref, first):
-        def step(i, _):
-            rows = rows_at(i * points, points)
-            high, low = split(source_ref[lax.rem(i + first, source_ref.shape[0])])
-            lhs_ref[rows, :length] = high
-            lhs_ref[rows, length : 2 * length] = high
-            lhs_ref[rows, 2 * length :] = low
-            return 0
-
-        lax.fori_loop(0, source_ref.shape[0], step, 0)
-
-    def transform(lhs_ref, col):
-        hat = dot(lhs_ref[...], table_ref[:, 2 * col * LANES : 2 * (col + 1) * LANES])
+    def fill(source_ref, halves, first):
+        for i in range(source_ref.shape[0]):
+            rows = slice(i * points, (i + 1) * points)
+            value = source_ref[i if first is None else lax.rem(i + first, source_ref.shape[0])]
+            halves[0][rows], halves[1][rows] = split(value)
+
+    def transform(halves, col):
+        high, low = halves[0][...], halves[1][...]
+        lanes = slice(2 * col * LANES, 2 * (col + 1) * LANES)
+        upper, lower = table_ref[:length, lanes], table_ref[length:, lanes]
+        hat = dot(
+            jnp.concatenate([high, high, low], axis=1), jnp.concatenate([upper, lower, upper], axis=0)
+        )
         return hat[:, :LANES], hat[:, LANES:]
 
     def kern_column(col):
-        real, imag = transform(kern_lhs_ref, col)
+        real, imag = transform(kern_halves, col)
         khat_ref[0, col] = real
         khat_ref[1, col] = imag - real
         khat_ref[2, col] = imag + real
 
     def vec_column(col):
-        real, imag = transform(vec_lhs_ref, col)
+        real, imag = transform(vec_halves, col)
         vhat_ref[0, col] = real + imag
         vhat_ref[1, col] = real
         vhat_ref[2, col] = imag
@@ -162,18 +165,15 @@
         high_ref[:, lanes], low_ref[:, lanes] = split(jnp.concatenate(rows, axis=0))
 
     copies[0].wait()
-    fill(kern_ref, kern_lhs_ref, 0)
+    fill(kern_ref, kern_halves, None)
     copies[2].wait()
-    copies[3].wait()
     kern_column(0)
     copies[1].wait()
-    fill(vec_ref, vec_lhs_ref, shift)
-    step_in = points - halo
-    for k in range(own):
-        at = lax.rem(k + shift, count)
-        first_ref[k] = vec_ref[at, rows_at((1 - odd_place) * step_in, halo)]
-        second_ref[k] = vec_ref[at, rows_at(odd_place * step_in, halo)]
-    for copy in copies[4:-1]:
+    fill(vec_ref, vec_halves, shift)
+    edge = rows_at(upper_edge * (points - halo), halo)
+    for k in range(both):
+        edge_ref[k] = vec_ref[sens // 2 * both + k, edge]
+    for copy in copies[3:-1]:
         copy.wait()
     vec_column(0)
     for col in range(cols):
@@ -195,23 +195,24 @@
         out_shape=(
             pltpu.VMEM((sensors * count, length), F32),
             pltpu.VMEM((3, cols, sensors * points, LANES), F32),
-            pltpu.VMEM((3 * length, 2 * length), BF16),
+            pltpu.VMEM((2 * length, 2 * length), BF16),
             pltpu.VMEM((4 * length, length), BF16),
             pltpu.VMEM(vectors.shape, F32),
             pltpu.VMEM(correlation.shape, F32),
-            pltpu.VMEM((own, COLS, length), F32),
-            pltpu.VMEM((own, COLS, length), F32),
+            pltpu.VMEM((2 * own, COLS, length), F32),
         ),
         in_specs=[hbm] * 5,
-        out_specs=[pl.BlockSpec(memory_space=pltpu.VMEM)] * 8,
+        out_specs=[pl.BlockSpec(memory_space=pltpu.VMEM)] * 7,
         scratch_shapes=[
             pltpu.VMEM(kernel.shape, F32),
             pltpu.VMEM((3, cols, count * points, LANES), F32),
-            pltpu.VMEM((sensors * points, 3 * length), BF16),
-            pltpu.VMEM((count * points, 3 * length), BF16),
+            pltpu.VMEM((sensors * points, length), BF16),
+            pltpu.VMEM((sensors * points, length), BF16),
+            pltpu.VMEM((count * points, length), BF16),
+            pltpu.VMEM((count * points, length), BF16),
             pltpu.VMEM((sensors * count, 2 * length), BF16),
             pltpu.VMEM((sensors * count, 2 * length), BF16),
-            pltpu.SemaphoreType.DMA((4 + 2 * cols,)),
+            pltpu.SemaphoreType.DMA((4 + cols,)),
         ],
         compiler_params=pltpu.CompilerParams(vmem_limit_bytes=14 * 1024 * 1024),
     )(*map(in_hbm, (kernel, vectors, table, inverse, correlation)))
@@ -283,7 +284,10 @@
     groups = corr_ref.shape[1] // length
     pred = pred_ref[...]
     high, low = split(pred)
-    mixed = dot(jnp.concatenate([high, high], axis=1), corr_ref[...]) + dot(low, corr_ref[:length])
+    upper, lower = corr_ref[:length], corr_ref[length:]
+    mixed = dot(
+        jnp.concatenate([high, high, low], axis=1), jnp.concatenate([upper, lower, upper], axis=0)
+    )
     whole = []
     for s in range(sensors):
         at = slice(s * count, (s + 1) * count)
@@ -293,7 +297,10 @@
             value = value + weight * mixed[at, g * length : (g + 1) * length]
         whole.append(value * (scale_ref[s] * (1.0 / (length * length))))
     high, low = split(jnp.concatenate(whole, axis=0))
-    hat = dot(jnp.concatenate([high, high, low], axis=1), table_ref[...])
+    upper, lower = table_ref[:length], table_ref[length:]
+    hat = dot(
+        jnp.concatenate([high, high, low], axis=1), jnp.concatenate([upper, lower, upper], axis=0)
+    )
     for col in range(length // LANES):
         real = hat[:, 2 * col * LANES : (2 * col + 1) * LANES]
         imag = hat[:, (2 * col + 1) * LANES : (2 * col + 2) * LANES]
@@ -310,8 +317,8 @@
     inverse_ref,
     vec_ref,
     weight_ref,
-    first_ref,
-    second_ref,
+    mine_ref,
+    other_ref,
     out_ref,
     high_ref,
     low_ref,
@@ -322,7 +329,10 @@
     upper, lower = weight_ref[0], weight_ref[1]
     for k in range(own):
         here = vec_ref[lax.rem(sens * own + k, count)]
-        value = jnp.concatenate([first_ref[k], here, second_ref[k]], axis=0)
+        mine, other = mine_ref[sens % 2 * own + k], other_ref[sens % 2 * own + k]
+        first = jnp.where(sens % 2 == 0, mine, other)
+        second = jnp.where(sens % 2 == 0, other, mine)
+        value = jnp.concatenate([first, here, second], axis=0)
         high, low = split(value)
         out_ref[k] = out_ref[k] + dot(upper, high) + dot(upper, low) + dot(lower, high)
 
@@ -428,7 +438,8 @@
         masks.append([low])
         if bits:
             high, *bits = bits
-            masks[-1] += [high, low + high]
+            both = [low, high, low + high]
+            masks[-1] = [both[i] for i in (ORDER[1] if len(masks) > 1 else ORDER[0])]
     turned = list(masks)
     if len(masks) > 1 and len(masks[0]) == len(masks[1]):
         turned[0], turned[1] = masks[1], masks[0]
@@ -441,19 +452,17 @@
     n_sens, n_pts = lax.axis_size("sens"), lax.axis_size("pts")
     own = count // n_sens
 
-    pred, khat, table, inverse, vectors, correlation, *edges = forward(
+    pred, khat, table, inverse, vectors, correlation, edge = forward(
         kernel, vectors, table, inverse, correlation, own
     )
     correlation, weight = ready(correlation, stiffness, couplings, neighbors)
 
-    links = [[], []]
+    links = []
     for s in range(n_sens):
-        for p in range(n_pts - 1):
-            here = s * n_pts + p
-            links[p % 2] += [(here, here + 1), (here + 1, here)]
-        if n_sens % 2 == 0:
-            for p in (0, n_pts - 1):
-                links[1].append((s * n_pts + p, (s ^ 1) * n_pts + p))
+        for p in range(n_pts):
+            partner = p ^ 1 if s % 2 == 0 else ((p - 1) ^ 1) + 1
+            links.append((s * n_pts + p, s * n_pts + partner % n_pts))
+    across = [(s, s ^ 1) for s in range(n_sens)]
     halos = []
     for step, (even, odd) in enumerate(zip(*stages(n_pts))):
         more = []
@@ -464,17 +473,16 @@
                 for p in range(n_pts)
             ]
             more.append(lax.ppermute(pred, ("sens", "pts"), pairs))
-        if step < 2:
-            halos.append(lax.ppermute(edges[step], ("sens", "pts"), links[step]))
+        if step == 0:
+            halos.append(lax.ppermute(edge, ("sens", "pts"), links))
         for part in more:
             pred = pred + part
         if step == 0:
-            pred, halos[0], correlation, edges[1] = lax.optimization_barrier(
-                (pred, halos[0], correlation, edges[1])
-            )
+            pred, correlation = lax.optimization_barrier((pred, correlation))
+            halos.append(lax.ppermute(halos[0], "sens", across))
+    pred, halos[1] = lax.optimization_barrier((pred, halos[1]))
 
     rest, rhat = adjoint_others(pred, noise_scale, sensor_group, correlation, khat, table, inverse, own, count)
-    rest, halos[1] = lax.optimization_barrier((rest, halos[1]))
     received = []
     for j in range(1, n_sens):
         pairs = [(s, (s + j) % n_sens) for s in range(n_sens)]

time: 32.4 us -> 31.4 us (0.969)
  the two profiles are of different devices: /device:TPU:0 before, /device:TPU:3 now
where the time goes in v5:
time: 31.4 us; the launch traced here: 31 us
  starting transfers between devices  15.5 us (49%)
  Pallas kernels  11.7 us (37%)
  waiting for transfers between devices  3.57 us (11%)
    ppermute x6, starting transfers between devices, local(): more.append(lax.ppermute(pred, ('sens', 'pts'), pairs))  6.68 us
    pallas_call x1, Pallas kernels, forward(): pl.pallas_call(forward_kernel, out_shape=(pltpu.VMEM((sensors * count, le...  5.55 us
    ppermute x1, starting transfers between devices, local(): received.append(lax.ppermute(rest[(j - 1) * own:j * own], 'sens', pairs))  4.08 us
    ppermute x1, starting transfers between devices, local(): halos.append(lax.ppermute(halos[0], 'sens', across))  3.54 us
    ppermute x6, waiting for transfers between devices, local(): more.append(lax.ppermute(pred, ('sens', 'pts'), pairs))  3.36 us
    pallas_call x1, Pallas kernels, adjoint_others(): pl.pallas_call(functools.partial(others_kernel, own, count), out_shape=(p...  3.07 us
    pallas_call x1, Pallas kernels, adjoint_own(): pl.pallas_call(functools.partial(own_kernel, count), out_shape=pltpu.VMEM...  1.63 us
    ppermute x1, starting transfers between devices, local(): halos.append(lax.ppermute(edge, ('sens', 'pts'), links))  1.21 us
  transfers between devices with their start and end apart: 9, of which 3 were waited for; matrix products, arithmetic and copies ran while one was open for 0% of the time, Pallas kernels for 8%

profile of v5, /device:TPU:3, one launch (start us, length us, event | category | flops | bytes accessed | tf_op | source)
XLA Modules:
  0.0 31.0 jit_solution(17576700076010282055)
XLA Ops:
  0.0 5.5 %shard_map.100 = (f32[64,384]{1,0:T(8,128)S(1)}, f32[3,3,512,128]{3,2,1,0:T(8,128)S(1)}, bf16[768,768]{1,0:T(8,128)(2,1)S(1)}, bf16[1536,384]{1,0:T(8,128)(2,1)S...) custom-call(f32[8,64,384]{2,1,0:T(8,128)} %kern_hbm.1, ...), custom_call_target="tpu_custom_call" | custom-call | tf_op jit(solution)/shard_map/pallas_call | solution.py:193
  5.6 0.0 copy-start.3
  5.6 0.0 copy-start.4
  5.6 3.4 %collective-permute-start.2 = (f32[64,384]{1,0:T(8,128)S(1)}, f32[64,384]{1,0:T(8,128)S(1)}, u32[]{:S(2)}, u32[]{:S(2)}) collective-permute-start(f32[64,384]{1,0:T(8,128)S(1)} %get-tuple-element.20), channel_id=1, source_target_pairs={{0,1},{1,0},{2,3},{3,2},{4,5},{5,4},{6,7},{7,6},{8,9},{9,8},{10,11... | collective-permute-start | bytes 294920 | tf_op jit(solution)/shard_map/ppermute | solution.py:475
  9.0 0.0 collective-permute-start.1
  9.0 0.4 %collective-permute-start = (f32[64,384]{1,0:T(8,128)S(1)}, f32[64,384]{1,0:T(8,128)S(1)}, u32[]{:S(2)}, u32[]{:S(2)}) collective-permute-start(f32[64,384]{1,0:T(8,128)S(1)} %get-tuple-element.20), channel_id=1, source_target_pairs={{0,2},{1,3},{2,0},{3,1},{4,6},{5,7},{6,4},{7,5},{8,10},{9,11},{10,... | collective-permute-start | bytes 294920 | tf_op jit(solution)/shard_map/ppermute | solution.py:475
  9.3 1.2 %collective-permute-start.6 = (f32[8,16,384]{2,1,0:T(8,128)S(1)}, f32[8,16,384]{2,1,0:T(8,128)S(1)}, u32[]{:S(2)}, u32[]{:S(2)}) collective-permute-start(f32[8,16,384]{2,1,0:T(8,128)S(1)} %get-tuple-element.24), channel_id=1, source_target_pairs={{0,1},{1,0},{2,3},{3,2},{4,5},{5,4},{6,7},{7,6},{8,9},{9,8},{10,11... | collective-permute-start | bytes 589832 | tf_op jit(solution)/shard_map/ppermute | solution.py:477
  10.6 0.7 %shard_map.101 = (bf16[768,1536]{1,0:T(8,128)(2,1)S(1)}, bf16[2,64,96]{2,1,0:T(8,128)(2,1)S(1)}) custom-call(f32[4,384,384]{2,1,0:T(8,128)S(1)} %get-tuple-element.21.corr_ref, f32[1,64]{1,0:T(1,128)S(1)} %bitcast.1, f32[4,64]{1,0:T(4,128)S(1)} %copy-done, s32[4,64]{1,0:T(4,128)S(1)} %copy-done.1), custom_call_target="tpu_custom_call" | custom-call | tf_op jit(solution)/shard_map/pallas_call | solution.py:403
  11.3 0.0 collective-permute-done.2
  11.3 2.5 %collective-permute-done.1 = f32[64,384]{1,0:T(8,128)S(1)} collective-permute-done((f32[64,384]{1,0:T(8,128)S(1)}, f32[64,384]{1,0:T(8,128)S(1)}, u32[]{:S(2)}, u32[]{:S(2)}) %collective-permute-start.1) | collective-permute-done | bytes 98336 | tf_op jit(solution)/shard_map/ppermute | solution.py:475
  13.8 0.0 collective-permute-done
  13.8 1.7 %collective-permute-start.5 = (f32[64,384]{1,0:T(8,128)S(1)}, f32[64,384]{1,0:T(8,128)S(1)}, u32[]{:S(2)}, u32[]{:S(2)}) collective-permute-start(f32[64,384]{1,0:T(8,128)S(1)} %add_add_fusion.1), channel_id=1, source_target_pairs={{0,12},{1,13},{2,14},{3,15},{4,8},{5,9},{6,10},{7,11},{8,4},{9,5},... | collective-permute-start | bytes 294920 | tf_op jit(solution)/shard_map/ppermute | solution.py:475
  15.5 0.8 %collective-permute-start.4 = (f32[64,384]{1,0:T(8,128)S(1)}, f32[64,384]{1,0:T(8,128)S(1)}, u32[]{:S(2)}, u32[]{:S(2)}) collective-permute-start(f32[64,384]{1,0:T(8,128)S(1)} %add_add_fusion.1), channel_id=1, source_target_pairs={{0,4},{1,5},{2,6},{3,7},{4,0},{5,1},{6,2},{7,3},{8,12},{9,13},{10,... | collective-permute-start | bytes 294920 | tf_op jit(solution)/shard_map/ppermute | solution.py:475
  16.3 0.4 %collective-permute-start.3 = (f32[64,384]{1,0:T(8,128)S(1)}, f32[64,384]{1,0:T(8,128)S(1)}, u32[]{:S(2)}, u32[]{:S(2)}) collective-permute-start(f32[64,384]{1,0:T(8,128)S(1)} %add_add_fusion.1), channel_id=1, source_target_pairs={{0,8},{1,9},{2,10},{3,11},{4,12},{5,13},{6,14},{7,15},{8,0},{9,1},... | collective-permute-start | bytes 294920 | tf_op jit(solution)/shard_map/ppermute | solution.py:475
  16.8 0.0 collective-permute-done.6.mine_ref
  16.8 3.5 %collective-permute-start.7 = (f32[8,16,384]{2,1,0:T(8,128)S(1)}, f32[8,16,384]{2,1,0:T(8,128)S(1)}, u32[]{:S(2)}, u32[]{:S(2)}) collective-permute-start(f32[8,16,384]{2,1,0:T(8,128)S(1)} %collective-permute-done.6.mine_ref), channel_id=1, source_target_pairs={{0,16},{16,0},{1,17},{17,1},{2,18},{18,2},{3,19},{19,3},{4,20},{20... | collective-permute-start | bytes 589832 | tf_op jit(solution)/shard_map/ppermute | solution.py:482
  20.3 0.0 collective-permute-done.5
  20.3 0.0 collective-permute-done.4
  20.3 0.8 %collective-permute-done.3 = f32[64,384]{1,0:T(8,128)S(1)} collective-permute-done((f32[64,384]{1,0:T(8,128)S(1)}, f32[64,384]{1,0:T(8,128)S(1)}, u32[]{:S(2)}, u32[]{:S(2)}) %collective-permute-start.3) | collective-permute-done | bytes 98336 | tf_op jit(solution)/shard_map/ppermute | solution.py:475
  21.2 0.2 collective-permute-done.7.other_ref
  21.4 3.1 %shard_map.102 = (f32[4,64,384]{2,1,0:T(8,128)S(1)}, f32[3,3,64,128]{3,2,1,0:T(8,128)S(1)}) custom-call(f32[8]{0:T(128)S(1)} %copy-done.3, s32[8]{0:T(128)S(1)} %copy-done.4, f32[64,384]{1,0:T(8,128)S(1)} %add_add_fusion.pred_ref, bf16[768,1536]{1,0:T(8,128)(2,1)S(1)} %get-tuple-element.26.corr_ref, f32[3,3,512,128]{3,2,1,0:T(8,128)S(1)} %get-tuple-element.27.khat_ref, ...), custom_call_target="tpu_custom_call" | custom-call | flops 1 | bytes 1 | tf_op jit(solution)/shard_map/pallas_call | solution.py:346
  24.5 4.1 %collective-permute-start.8 = (f32[4,64,384]{2,1,0:T(8,128)S(1)}, f32[4,64,384]{2,1,0:T(8,128)S(1)}, u32[]{:S(2)}, u32[]{:S(2)}) collective-permute-start(f32[4,64,384]{2,1,0:T(8,128)S(1)} %get-tuple-element.34), channel_id=1, source_target_pairs={{0,16},{16,0},{1,17},{17,1},{2,18},{18,2},{3,19},{19,3},{4,20},{20... | collective-permute-start | bytes 1179656 | tf_op jit(solution)/shard_map/ppermute | solution.py:489
  28.5 1.6 %shard_map.103.refs_0_ = f32[4,64,384]{2,1,0:T(8,128)S(1)} custom-call(f32[3,3,64,128]{3,2,1,0:T(8,128)S(1)} %get-tuple-element.30.rhat_ref, f32[3,3,512,128]{3,2,1,0:T(8,128)S(1)} %get-tuple-element.27.khat_ref, bf16[1536,384]{1,0:T(8,128)(2,1)S(1)} %get-tuple-element.29.inverse_ref, f32[8,64,384]{2,1,0:T(8,128)S(1)} %get-tuple-element.31.vec_ref, ...), custom_call_target="tpu_custom_call" | custom-call | flops 452984832 | bytes 2359296 | tf_op jit(solution)/shard_map/pallas_call | solution.py:364
  30.2 0.8 %shard_map.104 = f32[4,64,384]{2,1,0:T(8,128)} custom-call(f32[4,64,384]{2,1,0:T(8,128)S(1)} %shard_map.103.refs_0_, f32[4,64,384]{2,1,0:T(8,128)S(1)} %collective-permute-done.8.refs_1_), custom_call_target="tpu_custom_call" | custom-call | tf_op jit(solution)/shard_map/pallas_call | solution.py:424
  (11 shorter events, 0.1 us)
Async XLA Ops:
  0.0 10.6 %copy-start.1 = (s32[4,64]{1,0:T(4,128)S(1)}, s32[4,64]{1,0:T(4,128)}, u32[]{:S(2)}) copy-start(s32[4,64]{1,0:T(4,128)} %near_ref.1) | copy-start | bytes 3076
  0.0 10.6 %copy-start = (f32[4,64]{1,0:T(4,128)S(1)}, f32[4,64]{1,0:T(4,128)}, u32[]{:S(2)}) copy-start(f32[4,64]{1,0:T(4,128)} %coup_ref.1) | copy-start | bytes 3076
  0.0 10.6 %copy-start.2 = (f32[64]{0:T(128)S(1)}, f32[64]{0:T(128)}, u32[]{:S(2)}) copy-start(f32[64]{0:T(128)} %param.15) | copy-start | bytes 772
  5.6 15.8 %copy-start.3 = (f32[8]{0:T(128)S(1)}, f32[8]{0:T(128)}, u32[]{:S(2)}) copy-start(f32[8]{0:T(128)} %scale_ref.1) | copy-start | bytes 100
  5.6 15.8 %copy-start.4 = (s32[8]{0:T(128)S(1)}, s32[8]{0:T(128)}, u32[]{:S(2)}) copy-start(s32[8]{0:T(128)} %group_ref.1) | copy-start | bytes 100
  5.6 5.7 %collective-permute-start.2 = (f32[64,384]{1,0:T(8,128)S(1)}, f32[64,384]{1,0:T(8,128)S(1)}, u32[]{:S(2)}, u32[]{:S(2)}) collective-permute-start(f32[64,384]{1,0:T(8,128)S(1)} %get-tuple-element.20), channel_id=1, source_target_pairs={{0,1},{1,0},{2,3},{3,2},{4,5},{5,4},{6,7},{7,6},{8,9},{9,8},{10,11... | collective-permute-start | bytes 294920 | tf_op jit(solution)/shard_map/ppermute | solution.py:475
  9.0 4.8 %collective-permute-start.1 = (f32[64,384]{1,0:T(8,128)S(1)}, f32[64,384]{1,0:T(8,128)S(1)}, u32[]{:S(2)}, u32[]{:S(2)}) collective-permute-start(f32[64,384]{1,0:T(8,128)S(1)} %get-tuple-element.20), channel_id=1, source_target_pairs={{0,3},{1,2},{2,1},{3,0},{4,7},{5,6},{6,5},{7,4},{8,11},{9,10},{10,... | collective-permute-start | bytes 294920 | tf_op jit(solution)/shard_map/ppermute | solution.py:475
  9.0 4.8 %collective-permute-start = (f32[64,384]{1,0:T(8,128)S(1)}, f32[64,384]{1,0:T(8,128)S(1)}, u32[]{:S(2)}, u32[]{:S(2)}) collective-permute-start(f32[64,384]{1,0:T(8,128)S(1)} %get-tuple-element.20), channel_id=1, source_target_pairs={{0,2},{1,3},{2,0},{3,1},{4,6},{5,7},{6,4},{7,5},{8,10},{9,11},{10,... | collective-permute-start | bytes 294920 | tf_op jit(solution)/shard_map/ppermute | solution.py:475
  9.3 7.4 %collective-permute-start.6 = (f32[8,16,384]{2,1,0:T(8,128)S(1)}, f32[8,16,384]{2,1,0:T(8,128)S(1)}, u32[]{:S(2)}, u32[]{:S(2)}) collective-permute-start(f32[8,16,384]{2,1,0:T(8,128)S(1)} %get-tuple-element.24), channel_id=1, source_target_pairs={{0,1},{1,0},{2,3},{3,2},{4,5},{5,4},{6,7},{7,6},{8,9},{9,8},{10,11... | collective-permute-start | bytes 589832 | tf_op jit(solution)/shard_map/ppermute | solution.py:477
  13.8 6.5 %collective-permute-start.5 = (f32[64,384]{1,0:T(8,128)S(1)}, f32[64,384]{1,0:T(8,128)S(1)}, u32[]{:S(2)}, u32[]{:S(2)}) collective-permute-start(f32[64,384]{1,0:T(8,128)S(1)} %add_add_fusion.1), channel_id=1, source_target_pairs={{0,12},{1,13},{2,14},{3,15},{4,8},{5,9},{6,10},{7,11},{8,4},{9,5},... | collective-permute-start | bytes 294920 | tf_op jit(solution)/shard_map/ppermute | solution.py:475
  15.5 4.8 %collective-permute-start.4 = (f32[64,384]{1,0:T(8,128)S(1)}, f32[64,384]{1,0:T(8,128)S(1)}, u32[]{:S(2)}, u32[]{:S(2)}) collective-permute-start(f32[64,384]{1,0:T(8,128)S(1)} %add_add_fusion.1), channel_id=1, source_target_pairs={{0,4},{1,5},{2,6},{3,7},{4,0},{5,1},{6,2},{7,3},{8,12},{9,13},{10,... | collective-permute-start | bytes 294920 | tf_op jit(solution)/shard_map/ppermute | solution.py:475
  16.3 4.8 %collective-permute-start.3 = (f32[64,384]{1,0:T(8,128)S(1)}, f32[64,384]{1,0:T(8,128)S(1)}, u32[]{:S(2)}, u32[]{:S(2)}) collective-permute-start(f32[64,384]{1,0:T(8,128)S(1)} %add_add_fusion.1), channel_id=1, source_target_pairs={{0,8},{1,9},{2,10},{3,11},{4,12},{5,13},{6,14},{7,15},{8,0},{9,1},... | collective-permute-start | bytes 294920 | tf_op jit(solution)/shard_map/ppermute | solution.py:475
  16.8 4.6 %collective-permute-start.7 = (f32[8,16,384]{2,1,0:T(8,128)S(1)}, f32[8,16,384]{2,1,0:T(8,128)S(1)}, u32[]{:S(2)}, u32[]{:S(2)}) collective-permute-start(f32[8,16,384]{2,1,0:T(8,128)S(1)} %collective-permute-done.6.mine_ref), channel_id=1, source_target_pairs={{0,16},{16,0},{1,17},{17,1},{2,18},{18,2},{3,19},{19,3},{4,20},{20... | collective-permute-start | bytes 589832 | tf_op jit(solution)/shard_map/ppermute | solution.py:482
  24.5 5.7 %collective-permute-start.8 = (f32[4,64,384]{2,1,0:T(8,128)S(1)}, f32[4,64,384]{2,1,0:T(8,128)S(1)}, u32[]{:S(2)}, u32[]{:S(2)}) collective-permute-start(f32[4,64,384]{2,1,0:T(8,128)S(1)} %get-tuple-element.34), channel_id=1, source_target_pairs={{0,16},{16,0},{1,17},{17,1},{2,18},{18,2},{3,19},{19,3},{4,20},{20... | collective-permute-start | bytes 1179656 | tf_op jit(solution)/shard_map/ppermute | solution.py:489

commit v6 on v5

--- a/solution.py
+++ b/solution.py
@@ -11,7 +11,7 @@
 from jax.sharding import PartitionSpec as P
 
 COLS = 16
-ORDER = ((1, 2, 0), (1, 0, 2))
+ORDER = ((1, 0, 2), (0, 1, 2))
 LANES = 128
 SUB = 8
 F32 = jnp.float32
@@ -326,7 +326,7 @@
     correlate(0, count, rhat_ref, khat_ref, inverse_ref, high_ref, low_ref, out_ref)
     own = out_ref.shape[0]
     sens = lax.axis_index("sens")
-    upper, lower = weight_ref[0], weight_ref[1]
+    weight = weight_ref[...]
     for k in range(own):
         here = vec_ref[lax.rem(sens * own + k, count)]
         mine, other = mine_ref[sens % 2 * own + k], other_ref[sens % 2 * own + k]
@@ -334,7 +334,7 @@
         second = jnp.where(sens % 2 == 0, other, mine)
         value = jnp.concatenate([first, here, second], axis=0)
         high, low = split(value)
-        out_ref[k] = out_ref[k] + dot(upper, high) + dot(upper, low) + dot(lower, high)
+        out_ref[k] = out_ref[k] + dot(weight, jnp.concatenate([high, low, high], axis=0))
 
 
 def adjoint_others(pred, scale, group, correlation, khat, table, inverse, own, count):
@@ -381,8 +381,8 @@
         out_ref[:length, lanes], out_ref[length:, lanes] = split(corr_ref[g].T)
 
     place_here = lax.axis_index("pts")
-    points = weight_ref.shape[1]
-    span = weight_ref.shape[2]
+    points = weight_ref.shape[0]
+    span = points + 2 * halo
     place = lax.broadcasted_iota(jnp.int32, (span, points), 0)
     here = lax.broadcasted_iota(jnp.int32, (span, points), 1) + halo
     coup = coup_ref[...]
@@ -393,7 +393,9 @@
     near = near + jnp.where(near < halo, swap, 0) - jnp.where(near >= points + halo, swap, 0)
     for j in range(coup.shape[0]):
         weight = weight - jnp.where(place == near[j : j + 1], coup[j : j + 1], 0.0)
-    weight_ref[0], weight_ref[1] = split(weight.T)
+    high, low = split(weight.T)
+    for i, part in enumerate((high, high, low)):
+        weight_ref[:, i * span : (i + 1) * span] = part
 
 
 def ready(correlation, stiffness, couplings, neighbors):
@@ -404,7 +406,7 @@
         functools.partial(ready_kernel, COLS),
         out_shape=(
             pltpu.VMEM((2 * length, groups * length), BF16),
-            pltpu.VMEM((2, points, points + 2 * COLS), BF16),
+            pltpu.VMEM((points, 3 * (points + 2 * COLS)), BF16),
         ),
         in_specs=[vmem] * 4,
         out_specs=[vmem] * 2,

time: 31.4 us -> 31.1 us (level)
    ppermute x6, waiting for transfers between devices: 3.36 us -> 2.49 us  [local(): more.append(lax.ppermute(pred, ('sens', 'pts'), pairs))]
    ppermute x1, waiting for transfers between devices: 0.21 us -> 1.03 us  [local(): halos.append(lax.ppermute(halos[0], 'sens', across))]
where the time goes in v6:
time: 31.1 us; the launch traced here: 30.9 us
  starting transfers between devices  15.5 us (50%)
  Pallas kernels  11.8 us (38%)
  waiting for transfers between devices  3.52 us (11%)
    ppermute x6, starting transfers between devices, local(): more.append(lax.ppermute(pred, ('sens', 'pts'), pairs))  6.66 us
    pallas_call x1, Pallas kernels, forward(): pl.pallas_call(forward_kernel, out_shape=(pltpu.VMEM((sensors * count, le...  5.55 us
    ppermute x1, starting transfers between devices, local(): received.append(lax.ppermute(rest[(j - 1) * own:j * own], 'sens', pairs))  4.29 us
    ppermute x1, starting transfers between devices, local(): halos.append(lax.ppermute(halos[0], 'sens', across))  3.31 us
    pallas_call x1, Pallas kernels, adjoint_others(): pl.pallas_call(functools.partial(others_kernel, own, count), out_shape=(p...  3.08 us
    ppermute x6, waiting for transfers between devices, local(): more.append(lax.ppermute(pred, ('sens', 'pts'), pairs))  2.49 us
    pallas_call x1, Pallas kernels, adjoint_own(): pl.pallas_call(functools.partial(own_kernel, count), out_shape=pltpu.VMEM...  1.62 us
    ppermute x1, starting transfers between devices, local(): halos.append(lax.ppermute(edge, ('sens', 'pts'), links))  1.21 us
  transfers between devices with their start and end apart: 9, of which 3 were waited for; matrix products, arithmetic and copies ran while one was open for 0% of the time, Pallas kernels for 8%

profile of v6, /device:TPU:3, one launch (start us, length us, event | category | flops | bytes accessed | tf_op | source)
XLA Modules:
  0.0 30.9 jit_solution(12037438740205648051)
XLA Ops:
  0.0 5.5 %shard_map.100 = (f32[64,384]{1,0:T(8,128)S(1)}, f32[3,3,512,128]{3,2,1,0:T(8,128)S(1)}, bf16[768,768]{1,0:T(8,128)(2,1)S(1)}, bf16[1536,384]{1,0:T(8,128)(2,1)S...) custom-call(f32[8,64,384]{2,1,0:T(8,128)} %kern_hbm.1, ...), custom_call_target="tpu_custom_call" | custom-call | tf_op jit(solution)/shard_map/pallas_call | solution.py:193
  5.6 0.0 copy-start.3
  5.6 0.0 copy-start.4
  5.6 3.4 %collective-permute-start.2 = (f32[64,384]{1,0:T(8,128)S(1)}, f32[64,384]{1,0:T(8,128)S(1)}, u32[]{:S(2)}, u32[]{:S(2)}) collective-permute-start(f32[64,384]{1,0:T(8,128)S(1)} %get-tuple-element.20), channel_id=1, source_target_pairs={{0,3},{1,2},{2,1},{3,0},{4,7},{5,6},{6,5},{7,4},{8,11},{9,10},{10,... | collective-permute-start | bytes 294920 | tf_op jit(solution)/shard_map/ppermute | solution.py:477
  9.0 0.0 collective-permute-start.1
  9.0 0.4 %collective-permute-start = (f32[64,384]{1,0:T(8,128)S(1)}, f32[64,384]{1,0:T(8,128)S(1)}, u32[]{:S(2)}, u32[]{:S(2)}) collective-permute-start(f32[64,384]{1,0:T(8,128)S(1)} %get-tuple-element.20), channel_id=1, source_target_pairs={{0,2},{1,3},{2,0},{3,1},{4,6},{5,7},{6,4},{7,5},{8,10},{9,11},{10,... | collective-permute-start | bytes 294920 | tf_op jit(solution)/shard_map/ppermute | solution.py:477
  9.3 1.2 %collective-permute-start.6 = (f32[8,16,384]{2,1,0:T(8,128)S(1)}, f32[8,16,384]{2,1,0:T(8,128)S(1)}, u32[]{:S(2)}, u32[]{:S(2)}) collective-permute-start(f32[8,16,384]{2,1,0:T(8,128)S(1)} %get-tuple-element.24), channel_id=1, source_target_pairs={{0,1},{1,0},{2,3},{3,2},{4,5},{5,4},{6,7},{7,6},{8,9},{9,8},{10,11... | collective-permute-start | bytes 589832 | tf_op jit(solution)/shard_map/ppermute | solution.py:479
  10.6 0.7 %shard_map.101 = (bf16[768,1536]{1,0:T(8,128)(2,1)S(1)}, bf16[64,288]{1,0:T(8,128)(2,1)S(1)}) custom-call(f32[4,384,384]{2,1,0:T(8,128)S(1)} %get-tuple-element.21.corr_ref, f32[1,64]{1,0:T(1,128)S(1)} %bitcast.1, f32[4,64]{1,0:T(4,128)S(1)} %copy-done, s32[4,64]{1,0:T(4,128)S(1)} %copy-done.1), custom_call_target="tpu_custom_call" | custom-call | tf_op jit(solution)/shard_map/pallas_call | solution.py:405
  11.3 0.0 collective-permute-done.2
  11.3 2.2 %collective-permute-done.1 = f32[64,384]{1,0:T(8,128)S(1)} collective-permute-done((f32[64,384]{1,0:T(8,128)S(1)}, f32[64,384]{1,0:T(8,128)S(1)}, u32[]{:S(2)}, u32[]{:S(2)}) %collective-permute-start.1) | collective-permute-done | bytes 98336 | tf_op jit(solution)/shard_map/ppermute | solution.py:477
  13.5 0.3 collective-permute-done
  13.8 1.3 %collective-permute-start.5 = (f32[64,384]{1,0:T(8,128)S(1)}, f32[64,384]{1,0:T(8,128)S(1)}, u32[]{:S(2)}, u32[]{:S(2)}) collective-permute-start(f32[64,384]{1,0:T(8,128)S(1)} %add_add_fusion.1), channel_id=1, source_target_pairs={{0,12},{1,13},{2,14},{3,15},{4,8},{5,9},{6,10},{7,11},{8,4},{9,5},... | collective-permute-start | bytes 294920 | tf_op jit(solution)/shard_map/ppermute | solution.py:477
  15.1 1.2 %collective-permute-start.4 = (f32[64,384]{1,0:T(8,128)S(1)}, f32[64,384]{1,0:T(8,128)S(1)}, u32[]{:S(2)}, u32[]{:S(2)}) collective-permute-start(f32[64,384]{1,0:T(8,128)S(1)} %add_add_fusion.1), channel_id=1, source_target_pairs={{0,8},{1,9},{2,10},{3,11},{4,12},{5,13},{6,14},{7,15},{8,0},{9,1},... | collective-permute-start | bytes 294920 | tf_op jit(solution)/shard_map/ppermute | solution.py:477
  16.3 0.4 %collective-permute-start.3 = (f32[64,384]{1,0:T(8,128)S(1)}, f32[64,384]{1,0:T(8,128)S(1)}, u32[]{:S(2)}, u32[]{:S(2)}) collective-permute-start(f32[64,384]{1,0:T(8,128)S(1)} %add_add_fusion.1), channel_id=1, source_target_pairs={{0,4},{1,5},{2,6},{3,7},{4,0},{5,1},{6,2},{7,3},{8,12},{9,13},{10,... | collective-permute-start | bytes 294920 | tf_op jit(solution)/shard_map/ppermute | solution.py:477
  16.7 0.0 collective-permute-done.6.mine_ref
  16.7 3.3 %collective-permute-start.7 = (f32[8,16,384]{2,1,0:T(8,128)S(1)}, f32[8,16,384]{2,1,0:T(8,128)S(1)}, u32[]{:S(2)}, u32[]{:S(2)}) collective-permute-start(f32[8,16,384]{2,1,0:T(8,128)S(1)} %collective-permute-done.6.mine_ref), channel_id=1, source_target_pairs={{0,16},{16,0},{1,17},{17,1},{2,18},{18,2},{3,19},{19,3},{4,20},{20... | collective-permute-start | bytes 589832 | tf_op jit(solution)/shard_map/ppermute | solution.py:484
  20.0 0.0 collective-permute-done.5
  20.0 0.0 collective-permute-done.4
  20.1 0.0 collective-permute-done.3
  20.1 1.0 %collective-permute-done.7.other_ref = f32[8,16,384]{2,1,0:T(8,128)S(1)} collective-permute-done((f32[8,16,384]{2,1,0:T(8,128)S(1)}, f32[8,16,384]{2,1,0:T(8,128)S(1)}, u32[]{:S(2)}, u32[]{:S(2)}) %collective-permute-start.7) | collective-permute-done | bytes 196640 | tf_op jit(solution)/shard_map/ppermute | solution.py:484
  21.1 3.1 %shard_map.102 = (f32[4,64,384]{2,1,0:T(8,128)S(1)}, f32[3,3,64,128]{3,2,1,0:T(8,128)S(1)}) custom-call(f32[8]{0:T(128)S(1)} %copy-done.3, s32[8]{0:T(128)S(1)} %copy-done.4, f32[64,384]{1,0:T(8,128)S(1)} %add_add_fusion.pred_ref, bf16[768,1536]{1,0:T(8,128)(2,1)S(1)} %get-tuple-element.26.corr_ref, f32[3,3,512,128]{3,2,1,0:T(8,128)S(1)} %get-tuple-element.27.khat_ref, ...), custom_call_target="tpu_custom_call" | custom-call | flops 1 | bytes 1 | tf_op jit(solution)/shard_map/pallas_call | solution.py:346
  24.2 4.3 %collective-permute-start.8 = (f32[4,64,384]{2,1,0:T(8,128)S(1)}, f32[4,64,384]{2,1,0:T(8,128)S(1)}, u32[]{:S(2)}, u32[]{:S(2)}) collective-permute-start(f32[4,64,384]{2,1,0:T(8,128)S(1)} %get-tuple-element.34), channel_id=1, source_target_pairs={{0,16},{16,0},{1,17},{17,1},{2,18},{18,2},{3,19},{19,3},{4,20},{20... | collective-permute-start | bytes 1179656 | tf_op jit(solution)/shard_map/ppermute | solution.py:491
  28.5 1.6 %shard_map.103.refs_0_ = f32[4,64,384]{2,1,0:T(8,128)S(1)} custom-call(f32[3,3,64,128]{3,2,1,0:T(8,128)S(1)} %get-tuple-element.30.rhat_ref, f32[3,3,512,128]{3,2,1,0:T(8,128)S(1)} %get-tuple-element.27.khat_ref, bf16[1536,384]{1,0:T(8,128)(2,1)S(1)} %get-tuple-element.29.inverse_ref, f32[8,64,384]{2,1,0:T(8,128)S(1)} %get-tuple-element.31.vec_ref, ...), custom_call_target="tpu_custom_call" | custom-call | flops 452984832 | bytes 2359296 | tf_op jit(solution)/shard_map/pallas_call | solution.py:364
  30.1 0.8 %shard_map.104 = f32[4,64,384]{2,1,0:T(8,128)} custom-call(f32[4,64,384]{2,1,0:T(8,128)S(1)} %shard_map.103.refs_0_, f32[4,64,384]{2,1,0:T(8,128)S(1)} %collective-permute-done.8.refs_1_), custom_call_target="tpu_custom_call" | custom-call | tf_op jit(solution)/shard_map/pallas_call | solution.py:426
  (11 shorter events, 0.1 us)
Async XLA Ops:
  0.0 10.6 %copy-start.1 = (s32[4,64]{1,0:T(4,128)S(1)}, s32[4,64]{1,0:T(4,128)}, u32[]{:S(2)}) copy-start(s32[4,64]{1,0:T(4,128)} %near_ref.1) | copy-start | bytes 3076
  0.0 10.6 %copy-start = (f32[4,64]{1,0:T(4,128)S(1)}, f32[4,64]{1,0:T(4,128)}, u32[]{:S(2)}) copy-start(f32[4,64]{1,0:T(4,128)} %coup_ref.1) | copy-start | bytes 3076
  0.0 10.6 %copy-start.2 = (f32[64]{0:T(128)S(1)}, f32[64]{0:T(128)}, u32[]{:S(2)}) copy-start(f32[64]{0:T(128)} %param.15) | copy-start | bytes 772
  5.6 15.6 %copy-start.3 = (f32[8]{0:T(128)S(1)}, f32[8]{0:T(128)}, u32[]{:S(2)}) copy-start(f32[8]{0:T(128)} %scale_ref.1) | copy-start | bytes 100
  5.6 15.5 %copy-start.4 = (s32[8]{0:T(128)S(1)}, s32[8]{0:T(128)}, u32[]{:S(2)}) copy-start(s32[8]{0:T(128)} %group_ref.1) | copy-start | bytes 100
  5.6 5.7 %collective-permute-start.2 = (f32[64,384]{1,0:T(8,128)S(1)}, f32[64,384]{1,0:T(8,128)S(1)}, u32[]{:S(2)}, u32[]{:S(2)}) collective-permute-start(f32[64,384]{1,0:T(8,128)S(1)} %get-tuple-element.20), channel_id=1, source_target_pairs={{0,3},{1,2},{2,1},{3,0},{4,7},{5,6},{6,5},{7,4},{8,11},{9,10},{10,... | collective-permute-start | bytes 294920 | tf_op jit(solution)/shard_map/ppermute | solution.py:477
  9.0 4.5 %collective-permute-start.1 = (f32[64,384]{1,0:T(8,128)S(1)}, f32[64,384]{1,0:T(8,128)S(1)}, u32[]{:S(2)}, u32[]{:S(2)}) collective-permute-start(f32[64,384]{1,0:T(8,128)S(1)} %get-tuple-element.20), channel_id=1, source_target_pairs={{0,1},{1,0},{2,3},{3,2},{4,5},{5,4},{6,7},{7,6},{8,9},{9,8},{10,11... | collective-permute-start | bytes 294920 | tf_op jit(solution)/shard_map/ppermute | solution.py:477
  9.0 4.8 %collective-permute-start = (f32[64,384]{1,0:T(8,128)S(1)}, f32[64,384]{1,0:T(8,128)S(1)}, u32[]{:S(2)}, u32[]{:S(2)}) collective-permute-start(f32[64,384]{1,0:T(8,128)S(1)} %get-tuple-element.20), channel_id=1, source_target_pairs={{0,2},{1,3},{2,0},{3,1},{4,6},{5,7},{6,4},{7,5},{8,10},{9,11},{10,... | collective-permute-start | bytes 294920 | tf_op jit(solution)/shard_map/ppermute | solution.py:477
  9.3 7.4 %collective-permute-start.6 = (f32[8,16,384]{2,1,0:T(8,128)S(1)}, f32[8,16,384]{2,1,0:T(8,128)S(1)}, u32[]{:S(2)}, u32[]{:S(2)}) collective-permute-start(f32[8,16,384]{2,1,0:T(8,128)S(1)} %get-tuple-element.24), channel_id=1, source_target_pairs={{0,1},{1,0},{2,3},{3,2},{4,5},{5,4},{6,7},{7,6},{8,9},{9,8},{10,11... | collective-permute-start | bytes 589832 | tf_op jit(solution)/shard_map/ppermute | solution.py:479
  13.8 6.2 %collective-permute-start.5 = (f32[64,384]{1,0:T(8,128)S(1)}, f32[64,384]{1,0:T(8,128)S(1)}, u32[]{:S(2)}, u32[]{:S(2)}) collective-permute-start(f32[64,384]{1,0:T(8,128)S(1)} %add_add_fusion.1), channel_id=1, source_target_pairs={{0,12},{1,13},{2,14},{3,15},{4,8},{5,9},{6,10},{7,11},{8,4},{9,5},... | collective-permute-start | bytes 294920 | tf_op jit(solution)/shard_map/ppermute | solution.py:477
  15.1 4.9 %collective-permute-start.4 = (f32[64,384]{1,0:T(8,128)S(1)}, f32[64,384]{1,0:T(8,128)S(1)}, u32[]{:S(2)}, u32[]{:S(2)}) collective-permute-start(f32[64,384]{1,0:T(8,128)S(1)} %add_add_fusion.1), channel_id=1, source_target_pairs={{0,8},{1,9},{2,10},{3,11},{4,12},{5,13},{6,14},{7,15},{8,0},{9,1},... | collective-permute-start | bytes 294920 | tf_op jit(solution)/shard_map/ppermute | solution.py:477
  16.3 3.7 %collective-permute-start.3 = (f32[64,384]{1,0:T(8,128)S(1)}, f32[64,384]{1,0:T(8,128)S(1)}, u32[]{:S(2)}, u32[]{:S(2)}) collective-permute-start(f32[64,384]{1,0:T(8,128)S(1)} %add_add_fusion.1), channel_id=1, source_target_pairs={{0,4},{1,5},{2,6},{3,7},{4,0},{5,1},{6,2},{7,3},{8,12},{9,13},{10,... | collective-permute-start | bytes 294920 | tf_op jit(solution)/shard_map/ppermute | solution.py:477
  16.7 4.4 %collective-permute-start.7 = (f32[8,16,384]{2,1,0:T(8,128)S(1)}, f32[8,16,384]{2,1,0:T(8,128)S(1)}, u32[]{:S(2)}, u32[]{:S(2)}) collective-permute-start(f32[8,16,384]{2,1,0:T(8,128)S(1)} %collective-permute-done.6.mine_ref), channel_id=1, source_target_pairs={{0,16},{16,0},{1,17},{17,1},{2,18},{18,2},{3,19},{19,3},{4,20},{20... | collective-permute-start | bytes 589832 | tf_op jit(solution)/shard_map/ppermute | solution.py:484
  24.2 5.9 %collective-permute-start.8 = (f32[4,64,384]{2,1,0:T(8,128)S(1)}, f32[4,64,384]{2,1,0:T(8,128)S(1)}, u32[]{:S(2)}, u32[]{:S(2)}) collective-permute-start(f32[4,64,384]{2,1,0:T(8,128)S(1)} %get-tuple-element.34), channel_id=1, source_target_pairs={{0,16},{16,0},{1,17},{17,1},{2,18},{18,2},{3,19},{19,3},{4,20},{20... | collective-permute-start | bytes 1179656 | tf_op jit(solution)/shard_map/ppermute | solution.py:491

commit v7 on v6

--- a/solution.py
+++ b/solution.py
@@ -11,7 +11,6 @@
 from jax.sharding import PartitionSpec as P
 
 COLS = 16
-ORDER = ((1, 0, 2), (0, 1, 2))
 LANES = 128
 SUB = 8
 F32 = jnp.float32
@@ -267,10 +266,9 @@
 def others_kernel(
     own,
     count,
-    scale_ref,
-    group_ref,
     pred_ref,
     corr_ref,
+    pick_ref,
     khat_ref,
     table_ref,
     inverse_ref,
@@ -279,24 +277,22 @@
     high_ref,
     low_ref,
 ):
-    sensors = scale_ref.shape[0]
     length = pred_ref.shape[1]
     groups = corr_ref.shape[1] // length
+    times = length // LANES
+
+    def rowwise(g):
+        return jnp.concatenate([pick_ref[g]] * times, axis=1)
+
     pred = pred_ref[...]
     high, low = split(pred)
-    upper, lower = corr_ref[:length], corr_ref[length:]
-    mixed = dot(
-        jnp.concatenate([high, high, low], axis=1), jnp.concatenate([upper, lower, upper], axis=0)
-    )
-    whole = []
-    for s in range(sensors):
-        at = slice(s * count, (s + 1) * count)
-        value = pred[at]
-        for g in range(groups):
-            weight = jnp.where(group_ref[s] == g, 1.0, 0.0)
-            value = value + weight * mixed[at, g * length : (g + 1) * length]
-        whole.append(value * (scale_ref[s] * (1.0 / (length * length))))
-    high, low = split(jnp.concatenate(whole, axis=0))
+    lhs = jnp.concatenate([high, high, low], axis=1)
+    whole = rowwise(groups) * pred
+    for g in range(groups):
+        lanes = slice(g * length, (g + 1) * length)
+        upper, lower = corr_ref[:length, lanes], corr_ref[length:, lanes]
+        whole = whole + rowwise(g) * dot(lhs, jnp.concatenate([upper, lower, upper], axis=0))
+    high, low = split(whole)
     upper, lower = table_ref[:length], table_ref[length:]
     hat = dot(
         jnp.concatenate([high, high, low], axis=1), jnp.concatenate([upper, lower, upper], axis=0)
@@ -337,11 +333,10 @@
         out_ref[k] = out_ref[k] + dot(weight, jnp.concatenate([high, low, high], axis=0))
 
 
-def adjoint_others(pred, scale, group, correlation, khat, table, inverse, own, count):
+def adjoint_others(pred, correlation, pick, khat, table, inverse, own, count):
     rows, length = pred.shape
     points = khat.shape[2] // (rows // count)
     vmem = pl.BlockSpec(memory_space=pltpu.VMEM)
-    smem = pl.BlockSpec(memory_space=pltpu.SMEM)
     some = count - own
     return pl.pallas_call(
         functools.partial(others_kernel, own, count),
@@ -349,12 +344,12 @@
             pltpu.VMEM((some, points, length), F32),
             pltpu.VMEM((3, length // LANES, rows, LANES), F32),
         ),
-        in_specs=[smem] * 2 + [vmem] * 5,
+        in_specs=[vmem] * 6,
         out_specs=[vmem, vmem],
         scratch_shapes=[pltpu.VMEM((some * points, 2 * length), BF16)] * 2,
         compiler_params=pltpu.CompilerParams(vmem_limit_bytes=12 * 1024 * 1024),
         cost_estimate=pl.CostEstimate(flops=1, bytes_accessed=1, transcendentals=0),
-    )(scale, group, *map(in_vmem, (pred, correlation, khat, table, inverse)))
+    )(*map(in_vmem, (pred, correlation, pick, khat, table, inverse)))
 
 
 def adjoint_own(rhat, khat, inverse, vectors, weight, halos, own):
@@ -374,8 +369,22 @@
     )(*map(in_vmem, operands))
 
 
-def ready_kernel(halo, corr_ref, stiff_ref, coup_ref, near_ref, out_ref, weight_ref):
+def ready_kernel(
+    halo, scale_ref, group_ref, corr_ref, stiff_ref, coup_ref, near_ref, out_ref, pick_ref, weight_ref
+):
     groups, length, _ = corr_ref.shape
+    sensors = scale_ref.shape[0]
+    sensor = lax.broadcasted_iota(jnp.int32, pick_ref.shape[1:], 0) // (pick_ref.shape[1] // sensors)
+    factor = jnp.zeros(sensor.shape, F32)
+    member = jnp.zeros(sensor.shape, jnp.int32)
+    for s in range(sensors):
+        factor = jnp.where(sensor == s, scale_ref[s], factor)
+        member = jnp.where(sensor == s, group_ref[s], member)
+    factor = factor * (1.0 / (length * length))
+    for g in range(groups):
+        pick_ref[g] = jnp.where(member == g, factor, 0.0)
+    pick_ref[groups] = factor
+
     for g in range(groups):
         lanes = slice(g * length, (g + 1) * length)
         out_ref[:length, lanes], out_ref[length:, lanes] = split(corr_ref[g].T)
@@ -398,20 +407,22 @@
         weight_ref[:, i * span : (i + 1) * span] = part
 
 
-def ready(correlation, stiffness, couplings, neighbors):
+def ready(rows, scale, group, correlation, stiffness, couplings, neighbors):
     groups, length, _ = correlation.shape
     points = stiffness.shape[0]
     vmem = pl.BlockSpec(memory_space=pltpu.VMEM)
+    smem = pl.BlockSpec(memory_space=pltpu.SMEM)
     return pl.pallas_call(
         functools.partial(ready_kernel, COLS),
         out_shape=(
             pltpu.VMEM((2 * length, groups * length), BF16),
+            pltpu.VMEM((groups + 1, rows, LANES), F32),
             pltpu.VMEM((points, 3 * (points + 2 * COLS)), BF16),
         ),
-        in_specs=[vmem] * 4,
-        out_specs=[vmem] * 2,
+        in_specs=[smem] * 2 + [vmem] * 4,
+        out_specs=[vmem] * 3,
         compiler_params=pltpu.CompilerParams(vmem_limit_bytes=8 * 1024 * 1024),
-    )(*map(in_vmem, (correlation, stiffness[None], couplings, neighbors)))
+    )(scale, group, *map(in_vmem, (correlation, stiffness[None], couplings, neighbors)))
 
 
 def add_kernel(*refs):
@@ -440,8 +451,7 @@
         masks.append([low])
         if bits:
             high, *bits = bits
-            both = [low, high, low + high]
-            masks[-1] = [both[i] for i in (ORDER[1] if len(masks) > 1 else ORDER[0])]
+            masks[-1] = [low + high, low, high]
     turned = list(masks)
     if len(masks) > 1 and len(masks[0]) == len(masks[1]):
         turned[0], turned[1] = masks[1], masks[0]
@@ -457,7 +467,9 @@
     pred, khat, table, inverse, vectors, correlation, edge = forward(
         kernel, vectors, table, inverse, correlation, own
     )
-    correlation, weight = ready(correlation, stiffness, couplings, neighbors)
+    correlation, pick, weight = ready(
+        pred.shape[0], noise_scale, sensor_group, correlation, stiffness, couplings, neighbors
+    )
 
     links = []
     for s in range(n_sens):
@@ -484,7 +496,7 @@
             halos.append(lax.ppermute(halos[0], "sens", across))
     pred, halos[1] = lax.optimization_barrier((pred, halos[1]))
 
-    rest, rhat = adjoint_others(pred, noise_scale, sensor_group, correlation, khat, table, inverse, own, count)
+    rest, rhat = adjoint_others(pred, correlation, pick, khat, table, inverse, own, count)
     received = []
     for j in range(1, n_sens):
         pairs = [(s, (s + j) % n_sens) for s in range(n_sens)]

time: 31.1 us -> 30.3 us (0.974)
  waiting for transfers between devices: 3.52 us -> 2.96 us
    pallas_call x1, Pallas kernels: 3.08 us -> 2.39 us  [adjoint_others(): pl.pallas_call(functools.partial(others_kernel, own, count), out_shape=(p...]
    ppermute x1, starting transfers between devices: 3.31 us -> 2.75 us  [local(): halos.append(lax.ppermute(halos[0], 'sens', across))]
    ppermute x6, starting transfers between devices: 6.66 us -> 7.22 us  [local(): more.append(lax.ppermute(pred, ('sens', 'pts'), pairs))]
    ppermute x6, waiting for transfers between devices: 2.49 us -> 1.93 us  [local(): more.append(lax.ppermute(pred, ('sens', 'pts'), pairs))]
    pallas_call x1, Pallas kernels: 0.74 us -> 1.28 us  [ready(): pl.pallas_call(functools.partial(ready_kernel, COLS), out_shape=(pltpu.VM...]
  transfers between devices with their start and end apart: 9 -> 9, of which waited for: 3 -> 2; matrix products, arithmetic and copies ran while one was open for 0% -> 0% of each run, Pallas kernels for 8% -> 9%
where the time goes in v7:
time: 30.3 us; the launch traced here: 29.9 us
  starting transfers between devices  15.2 us (50%)
  Pallas kernels  11.5 us (38%)
  waiting for transfers between devices  2.96 us (10%)
    ppermute x6, starting transfers between devices, local(): more.append(lax.ppermute(pred, ('sens', 'pts'), pairs))  7.22 us
    pallas_call x1, Pallas kernels, forward(): pl.pallas_call(forward_kernel, out_shape=(pltpu.VMEM((sensors * count, le...  5.56 us
    ppermute x1, starting transfers between devices, local(): received.append(lax.ppermute(rest[(j - 1) * own:j * own], 'sens', pairs))  4.06 us
    ppermute x1, starting transfers between devices, local(): halos.append(lax.ppermute(halos[0], 'sens', across))  2.75 us
    pallas_call x1, Pallas kernels, adjoint_others(): pl.pallas_call(functools.partial(others_kernel, own, count), out_shape=(p...  2.39 us
    ppermute x6, waiting for transfers between devices, local(): more.append(lax.ppermute(pred, ('sens', 'pts'), pairs))  1.93 us
    pallas_call x1, Pallas kernels, adjoint_own(): pl.pallas_call(functools.partial(own_kernel, count), out_shape=pltpu.VMEM...  1.5 us
    pallas_call x1, Pallas kernels, ready(): pl.pallas_call(functools.partial(ready_kernel, COLS), out_shape=(pltpu.VM...  1.28 us
  transfers between devices with their start and end apart: 9, of which 2 were waited for; matrix products, arithmetic and copies ran while one was open for 0% of the time, Pallas kernels for 9%

profile of v7, /device:TPU:3, one launch (start us, length us, event | category | flops | bytes accessed | tf_op | source)
XLA Modules:
  0.0 29.9 jit_solution(281485033218675226)
XLA Ops:
  0.0 5.6 %shard_map.100 = (f32[64,384]{1,0:T(8,128)S(1)}, f32[3,3,512,128]{3,2,1,0:T(8,128)S(1)}, bf16[768,768]{1,0:T(8,128)(2,1)S(1)}, bf16[1536,384]{1,0:T(8,128)(2,1)S...) custom-call(f32[8,64,384]{2,1,0:T(8,128)} %kern_hbm.1, ...), custom_call_target="tpu_custom_call" | custom-call | tf_op jit(solution)/shard_map/pallas_call | solution.py:192
  5.6 3.4 %collective-permute-start = (f32[64,384]{1,0:T(8,128)S(1)}, f32[64,384]{1,0:T(8,128)S(1)}, u32[]{:S(2)}, u32[]{:S(2)}) collective-permute-start(f32[64,384]{1,0:T(8,128)S(1)} %get-tuple-element.21), channel_id=1, source_target_pairs={{0,3},{1,2},{2,1},{3,0},{4,7},{5,6},{6,5},{7,4},{8,11},{9,10},{10,... | collective-permute-start | bytes 294920 | tf_op jit(solution)/shard_map/ppermute | solution.py:489
  9.0 0.0 collective-permute-start.1
  9.0 0.4 %collective-permute-start.2 = (f32[64,384]{1,0:T(8,128)S(1)}, f32[64,384]{1,0:T(8,128)S(1)}, u32[]{:S(2)}, u32[]{:S(2)}) collective-permute-start(f32[64,384]{1,0:T(8,128)S(1)} %get-tuple-element.21), channel_id=1, source_target_pairs={{0,2},{1,3},{2,0},{3,1},{4,6},{5,7},{6,4},{7,5},{8,10},{9,11},{10,... | collective-permute-start | bytes 294920 | tf_op jit(solution)/shard_map/ppermute | solution.py:489
  9.4 1.2 %collective-permute-start.6 = (f32[8,16,384]{2,1,0:T(8,128)S(1)}, f32[8,16,384]{2,1,0:T(8,128)S(1)}, u32[]{:S(2)}, u32[]{:S(2)}) collective-permute-start(f32[8,16,384]{2,1,0:T(8,128)S(1)} %get-tuple-element.25), channel_id=1, source_target_pairs={{0,1},{1,0},{2,3},{3,2},{4,5},{5,4},{6,7},{7,6},{8,9},{9,8},{10,11... | collective-permute-start | bytes 589832 | tf_op jit(solution)/shard_map/ppermute | solution.py:491
  10.6 0.0 copy-done
  10.6 1.3 %shard_map.101 = (bf16[768,1536]{1,0:T(8,128)(2,1)S(1)}, f32[5,64,128]{2,1,0:T(8,128)S(1)}, bf16[64,288]{1,0:T(8,128)(2,1)S(1)}) custom-call(f32[8]{0:T(128)S(1)} %copy-done.2, s32[8]{0:T(128)S(1)} %copy-done.3, f32[4,384,384]{2,1,0:T(8,128)S(1)} %get-tuple-element.22.corr_ref, f32[1,64]{1,0:T(1,128)S(1)} %bitcast.1, f32[4,64]{1,0:T(4,128)S(1)} %copy-done, ...), custom_call_target="tpu_custom_call" | custom-call | tf_op jit(solution)/shard_map/pallas_call | solution.py:415
  11.9 0.0 collective-permute-done
  11.9 1.9 %collective-permute-done.1 = f32[64,384]{1,0:T(8,128)S(1)} collective-permute-done((f32[64,384]{1,0:T(8,128)S(1)}, f32[64,384]{1,0:T(8,128)S(1)}, u32[]{:S(2)}, u32[]{:S(2)}) %collective-permute-start.1) | collective-permute-done | bytes 98336 | tf_op jit(solution)/shard_map/ppermute | solution.py:489
  13.8 0.0 collective-permute-done.2
  13.8 1.3 %collective-permute-start.3 = (f32[64,384]{1,0:T(8,128)S(1)}, f32[64,384]{1,0:T(8,128)S(1)}, u32[]{:S(2)}, u32[]{:S(2)}) collective-permute-start(f32[64,384]{1,0:T(8,128)S(1)} %add_add_fusion.1), channel_id=1, source_target_pairs={{0,12},{1,13},{2,14},{3,15},{4,8},{5,9},{6,10},{7,11},{8,4},{9,5},... | collective-permute-start | bytes 294920 | tf_op jit(solution)/shard_map/ppermute | solution.py:489
  15.1 1.2 %collective-permute-start.4 = (f32[64,384]{1,0:T(8,128)S(1)}, f32[64,384]{1,0:T(8,128)S(1)}, u32[]{:S(2)}, u32[]{:S(2)}) collective-permute-start(f32[64,384]{1,0:T(8,128)S(1)} %add_add_fusion.1), channel_id=1, source_target_pairs={{0,4},{1,5},{2,6},{3,7},{4,0},{5,1},{6,2},{7,3},{8,12},{9,13},{10,... | collective-permute-start | bytes 294920 | tf_op jit(solution)/shard_map/ppermute | solution.py:489
  16.3 1.0 %collective-permute-start.5 = (f32[64,384]{1,0:T(8,128)S(1)}, f32[64,384]{1,0:T(8,128)S(1)}, u32[]{:S(2)}, u32[]{:S(2)}) collective-permute-start(f32[64,384]{1,0:T(8,128)S(1)} %add_add_fusion.1), channel_id=1, source_target_pairs={{0,8},{1,9},{2,10},{3,11},{4,12},{5,13},{6,14},{7,15},{8,0},{9,1},... | collective-permute-start | bytes 294920 | tf_op jit(solution)/shard_map/ppermute | solution.py:489
  17.3 0.0 collective-permute-done.6.mine_ref
  17.3 2.7 %collective-permute-start.7 = (f32[8,16,384]{2,1,0:T(8,128)S(1)}, f32[8,16,384]{2,1,0:T(8,128)S(1)}, u32[]{:S(2)}, u32[]{:S(2)}) collective-permute-start(f32[8,16,384]{2,1,0:T(8,128)S(1)} %collective-permute-done.6.mine_ref), channel_id=1, source_target_pairs={{0,16},{16,0},{1,17},{17,1},{2,18},{18,2},{3,19},{19,3},{4,20},{20... | collective-permute-start | bytes 589832 | tf_op jit(solution)/shard_map/ppermute | solution.py:496
  20.1 0.0 collective-permute-done.3
  20.1 0.0 collective-permute-done.4
  20.1 0.0 collective-permute-done.5
  20.1 1.0 %collective-permute-done.7.other_ref = f32[8,16,384]{2,1,0:T(8,128)S(1)} collective-permute-done((f32[8,16,384]{2,1,0:T(8,128)S(1)}, f32[8,16,384]{2,1,0:T(8,128)S(1)}, u32[]{:S(2)}, u32[]{:S(2)}) %collective-permute-start.7) | collective-permute-done | bytes 196640 | tf_op jit(solution)/shard_map/ppermute | solution.py:496
  21.1 2.4 %shard_map.102 = (f32[4,64,384]{2,1,0:T(8,128)S(1)}, f32[3,3,64,128]{3,2,1,0:T(8,128)S(1)}) custom-call(f32[64,384]{1,0:T(8,128)S(1)} %add_add_fusion.pred_ref, bf16[768,1536]{1,0:T(8,128)(2,1)S(1)} %get-tuple-element.27.corr_ref, f32[5,64,128]{2,1,0:T(8,128)S(1)} %get-tuple-element.28.pick_ref, f32[3,3,512,128]{3,2,1,0:T(8,128)S(1)} %get-tuple-element.29.khat_ref, ...), custom_call_target="tpu_custom_call" | custom-call | flops 1 | bytes 1 | tf_op jit(solution)/shard_map/pallas_call | solution.py:341
  23.5 4.1 %collective-permute-start.8 = (f32[4,64,384]{2,1,0:T(8,128)S(1)}, f32[4,64,384]{2,1,0:T(8,128)S(1)}, u32[]{:S(2)}, u32[]{:S(2)}) collective-permute-start(f32[4,64,384]{2,1,0:T(8,128)S(1)} %get-tuple-element.36), channel_id=1, source_target_pairs={{0,16},{16,0},{1,17},{17,1},{2,18},{18,2},{3,19},{19,3},{4,20},{20... | collective-permute-start | bytes 1179656 | tf_op jit(solution)/shard_map/ppermute | solution.py:503
  27.6 1.5 %shard_map.103.refs_0_ = f32[4,64,384]{2,1,0:T(8,128)S(1)} custom-call(f32[3,3,64,128]{3,2,1,0:T(8,128)S(1)} %get-tuple-element.32.rhat_ref, f32[3,3,512,128]{3,2,1,0:T(8,128)S(1)} %get-tuple-element.29.khat_ref, bf16[1536,384]{1,0:T(8,128)(2,1)S(1)} %get-tuple-element.31.inverse_ref, f32[8,64,384]{2,1,0:T(8,128)S(1)} %get-tuple-element.33.vec_ref, ...), custom_call_target="tpu_custom_call" | custom-call | flops 452984832 | bytes 2359296 | tf_op jit(solution)/shard_map/pallas_call | solution.py:359
  29.1 0.0 collective-permute-done.8.refs_1_
  29.1 0.8 %shard_map.104 = f32[4,64,384]{2,1,0:T(8,128)} custom-call(f32[4,64,384]{2,1,0:T(8,128)S(1)} %shard_map.103.refs_0_, f32[4,64,384]{2,1,0:T(8,128)S(1)} %collective-permute-done.8.refs_1_), custom_call_target="tpu_custom_call" | custom-call | tf_op jit(solution)/shard_map/pallas_call | solution.py:437
  (11 shorter events, 0.1 us)
Async XLA Ops:
  0.0 10.6 %copy-start.4 = (f32[64]{0:T(128)S(1)}, f32[64]{0:T(128)}, u32[]{:S(2)}) copy-start(f32[64]{0:T(128)} %param.15) | copy-start | bytes 772
  0.0 10.6 %copy-start.2 = (f32[8]{0:T(128)S(1)}, f32[8]{0:T(128)}, u32[]{:S(2)}) copy-start(f32[8]{0:T(128)} %scale_ref.1) | copy-start | bytes 100
  0.0 10.6 %copy-start.3 = (s32[8]{0:T(128)S(1)}, s32[8]{0:T(128)}, u32[]{:S(2)}) copy-start(s32[8]{0:T(128)} %group_ref.1) | copy-start | bytes 100
  0.0 10.6 %copy-start = (f32[4,64]{1,0:T(4,128)S(1)}, f32[4,64]{1,0:T(4,128)}, u32[]{:S(2)}) copy-start(f32[4,64]{1,0:T(4,128)} %coup_ref.1) | copy-start | bytes 3076
  0.0 10.6 %copy-start.1 = (s32[4,64]{1,0:T(4,128)S(1)}, s32[4,64]{1,0:T(4,128)}, u32[]{:S(2)}) copy-start(s32[4,64]{1,0:T(4,128)} %near_ref.1) | copy-start | bytes 3076
  5.6 6.3 %collective-permute-start = (f32[64,384]{1,0:T(8,128)S(1)}, f32[64,384]{1,0:T(8,128)S(1)}, u32[]{:S(2)}, u32[]{:S(2)}) collective-permute-start(f32[64,384]{1,0:T(8,128)S(1)} %get-tuple-element.21), channel_id=1, source_target_pairs={{0,3},{1,2},{2,1},{3,0},{4,7},{5,6},{6,5},{7,4},{8,11},{9,10},{10,... | collective-permute-start | bytes 294920 | tf_op jit(solution)/shard_map/ppermute | solution.py:489
  9.0 4.8 %collective-permute-start.1 = (f32[64,384]{1,0:T(8,128)S(1)}, f32[64,384]{1,0:T(8,128)S(1)}, u32[]{:S(2)}, u32[]{:S(2)}) collective-permute-start(f32[64,384]{1,0:T(8,128)S(1)} %get-tuple-element.21), channel_id=1, source_target_pairs={{0,1},{1,0},{2,3},{3,2},{4,5},{5,4},{6,7},{7,6},{8,9},{9,8},{10,11... | collective-permute-start | bytes 294920 | tf_op jit(solution)/shard_map/ppermute | solution.py:489
  9.0 4.8 %collective-permute-start.2 = (f32[64,384]{1,0:T(8,128)S(1)}, f32[64,384]{1,0:T(8,128)S(1)}, u32[]{:S(2)}, u32[]{:S(2)}) collective-permute-start(f32[64,384]{1,0:T(8,128)S(1)} %get-tuple-element.21), channel_id=1, source_target_pairs={{0,2},{1,3},{2,0},{3,1},{4,6},{5,7},{6,4},{7,5},{8,10},{9,11},{10,... | collective-permute-start | bytes 294920 | tf_op jit(solution)/shard_map/ppermute | solution.py:489
  9.4 8.0 %collective-permute-start.6 = (f32[8,16,384]{2,1,0:T(8,128)S(1)}, f32[8,16,384]{2,1,0:T(8,128)S(1)}, u32[]{:S(2)}, u32[]{:S(2)}) collective-permute-start(f32[8,16,384]{2,1,0:T(8,128)S(1)} %get-tuple-element.25), channel_id=1, source_target_pairs={{0,1},{1,0},{2,3},{3,2},{4,5},{5,4},{6,7},{7,6},{8,9},{9,8},{10,11... | collective-permute-start | bytes 589832 | tf_op jit(solution)/shard_map/ppermute | solution.py:491
  13.8 6.2 %collective-permute-start.3 = (f32[64,384]{1,0:T(8,128)S(1)}, f32[64,384]{1,0:T(8,128)S(1)}, u32[]{:S(2)}, u32[]{:S(2)}) collective-permute-start(f32[64,384]{1,0:T(8,128)S(1)} %add_add_fusion.1), channel_id=1, source_target_pairs={{0,12},{1,13},{2,14},{3,15},{4,8},{5,9},{6,10},{7,11},{8,4},{9,5},... | collective-permute-start | bytes 294920 | tf_op jit(solution)/shard_map/ppermute | solution.py:489
  15.1 4.9 %collective-permute-start.4 = (f32[64,384]{1,0:T(8,128)S(1)}, f32[64,384]{1,0:T(8,128)S(1)}, u32[]{:S(2)}, u32[]{:S(2)}) collective-permute-start(f32[64,384]{1,0:T(8,128)S(1)} %add_add_fusion.1), channel_id=1, source_target_pairs={{0,4},{1,5},{2,6},{3,7},{4,0},{5,1},{6,2},{7,3},{8,12},{9,13},{10,... | collective-permute-start | bytes 294920 | tf_op jit(solution)/shard_map/ppermute | solution.py:489
  16.3 3.7 %collective-permute-start.5 = (f32[64,384]{1,0:T(8,128)S(1)}, f32[64,384]{1,0:T(8,128)S(1)}, u32[]{:S(2)}, u32[]{:S(2)}) collective-permute-start(f32[64,384]{1,0:T(8,128)S(1)} %add_add_fusion.1), channel_id=1, source_target_pairs={{0,8},{1,9},{2,10},{3,11},{4,12},{5,13},{6,14},{7,15},{8,0},{9,1},... | collective-permute-start | bytes 294920 | tf_op jit(solution)/shard_map/ppermute | solution.py:489
  17.3 3.8 %collective-permute-start.7 = (f32[8,16,384]{2,1,0:T(8,128)S(1)}, f32[8,16,384]{2,1,0:T(8,128)S(1)}, u32[]{:S(2)}, u32[]{:S(2)}) collective-permute-start(f32[8,16,384]{2,1,0:T(8,128)S(1)} %collective-permute-done.6.mine_ref), channel_id=1, source_target_pairs={{0,16},{16,0},{1,17},{17,1},{2,18},{18,2},{3,19},{19,3},{4,20},{20... | collective-permute-start | bytes 589832 | tf_op jit(solution)/shard_map/ppermute | solution.py:496
  23.5 5.6 %collective-permute-start.8 = (f32[4,64,384]{2,1,0:T(8,128)S(1)}, f32[4,64,384]{2,1,0:T(8,128)S(1)}, u32[]{:S(2)}, u32[]{:S(2)}) collective-permute-start(f32[4,64,384]{2,1,0:T(8,128)S(1)} %get-tuple-element.36), channel_id=1, source_target_pairs={{0,16},{16,0},{1,17},{17,1},{2,18},{18,2},{3,19},{19,3},{4,20},{20... | collective-permute-start | bytes 1179656 | tf_op jit(solution)/shard_map/ppermute | solution.py:503

commit v8 on v7

--- a/solution.py
+++ b/solution.py
@@ -115,8 +115,8 @@
     copies = [
         pltpu.make_async_copy(source, target, sems.at[i]) for i, (source, target) in enumerate(pairs)
     ]
-    for i in (0, 2, 1, *range(3, len(copies))):
-        copies[i].start()
+    for copy in copies:
+        copy.start()
 
     def fill(source_ref, halves, first):
         for i in range(source_ref.shape[0]):
@@ -166,7 +166,6 @@
     copies[0].wait()
     fill(kern_ref, kern_halves, None)
     copies[2].wait()
-    kern_column(0)
     copies[1].wait()
     fill(vec_ref, vec_halves, shift)
     edge = rows_at(upper_edge * (points - halo), halo)
@@ -174,6 +173,7 @@
         edge_ref[k] = vec_ref[sens // 2 * both + k, edge]
     for copy in copies[3:-1]:
         copy.wait()
+    kern_column(0)
     vec_column(0)
     for col in range(cols):
         if col + 1 < cols:

time: 30.3 us -> 30.2 us (level)
  no operation moved by 1% of the time
where the time goes in v8:
time: 30.2 us; the launch traced here: 29.7 us
  starting transfers between devices  15.2 us (50%)
  Pallas kernels  11.4 us (38%)
  waiting for transfers between devices  2.96 us (10%)
    ppermute x6, starting transfers between devices, local(): more.append(lax.ppermute(pred, ('sens', 'pts'), pairs))  7.21 us
    pallas_call x1, Pallas kernels, forward(): pl.pallas_call(forward_kernel, out_shape=(pltpu.VMEM((sensors * count, le...  5.42 us
    ppermute x1, starting transfers between devices, local(): received.append(lax.ppermute(rest[(j - 1) * own:j * own], 'sens', pairs))  4.06 us
    ppermute x1, starting transfers between devices, local(): halos.append(lax.ppermute(halos[0], 'sens', across))  2.76 us
    pallas_call x1, Pallas kernels, adjoint_others(): pl.pallas_call(functools.partial(others_kernel, own, count), out_shape=(p...  2.39 us
    ppermute x6, waiting for transfers between devices, local(): more.append(lax.ppermute(pred, ('sens', 'pts'), pairs))  1.93 us
    pallas_call x1, Pallas kernels, adjoint_own(): pl.pallas_call(functools.partial(own_kernel, count), out_shape=pltpu.VMEM...  1.5 us
    pallas_call x1, Pallas kernels, ready(): pl.pallas_call(functools.partial(ready_kernel, COLS), out_shape=(pltpu.VM...  1.28 us
  transfers between devices with their start and end apart: 9, of which 2 were waited for; matrix products, arithmetic and copies ran while one was open for 0% of the time, Pallas kernels for 9%

profile of v8, /device:TPU:3, one launch (start us, length us, event | category | flops | bytes accessed | tf_op | source)
XLA Modules:
  0.0 29.7 jit_solution(16750975685687864074)
XLA Ops:
  0.0 5.4 %shard_map.100 = (f32[64,384]{1,0:T(8,128)S(1)}, f32[3,3,512,128]{3,2,1,0:T(8,128)S(1)}, bf16[768,768]{1,0:T(8,128)(2,1)S(1)}, bf16[1536,384]{1,0:T(8,128)(2,1)S...) custom-call(f32[8,64,384]{2,1,0:T(8,128)} %kern_hbm.1, ...), custom_call_target="tpu_custom_call" | custom-call | tf_op jit(solution)/shard_map/pallas_call | solution.py:192
  5.5 3.4 %collective-permute-start = (f32[64,384]{1,0:T(8,128)S(1)}, f32[64,384]{1,0:T(8,128)S(1)}, u32[]{:S(2)}, u32[]{:S(2)}) collective-permute-start(f32[64,384]{1,0:T(8,128)S(1)} %get-tuple-element.21), channel_id=1, source_target_pairs={{0,3},{1,2},{2,1},{3,0},{4,7},{5,6},{6,5},{7,4},{8,11},{9,10},{10,... | collective-permute-start | bytes 294920 | tf_op jit(solution)/shard_map/ppermute | solution.py:489
  8.8 0.0 collective-permute-start.1
  8.8 0.4 %collective-permute-start.2 = (f32[64,384]{1,0:T(8,128)S(1)}, f32[64,384]{1,0:T(8,128)S(1)}, u32[]{:S(2)}, u32[]{:S(2)}) collective-permute-start(f32[64,384]{1,0:T(8,128)S(1)} %get-tuple-element.21), channel_id=1, source_target_pairs={{0,2},{1,3},{2,0},{3,1},{4,6},{5,7},{6,4},{7,5},{8,10},{9,11},{10,... | collective-permute-start | bytes 294920 | tf_op jit(solution)/shard_map/ppermute | solution.py:489
  9.2 1.2 %collective-permute-start.6 = (f32[8,16,384]{2,1,0:T(8,128)S(1)}, f32[8,16,384]{2,1,0:T(8,128)S(1)}, u32[]{:S(2)}, u32[]{:S(2)}) collective-permute-start(f32[8,16,384]{2,1,0:T(8,128)S(1)} %get-tuple-element.25), channel_id=1, source_target_pairs={{0,1},{1,0},{2,3},{3,2},{4,5},{5,4},{6,7},{7,6},{8,9},{9,8},{10,11... | collective-permute-start | bytes 589832 | tf_op jit(solution)/shard_map/ppermute | solution.py:491
  10.4 0.0 copy-done
  10.4 1.3 %shard_map.101 = (bf16[768,1536]{1,0:T(8,128)(2,1)S(1)}, f32[5,64,128]{2,1,0:T(8,128)S(1)}, bf16[64,288]{1,0:T(8,128)(2,1)S(1)}) custom-call(f32[8]{0:T(128)S(1)} %copy-done.2, s32[8]{0:T(128)S(1)} %copy-done.3, f32[4,384,384]{2,1,0:T(8,128)S(1)} %get-tuple-element.22.corr_ref, f32[1,64]{1,0:T(1,128)S(1)} %bitcast.1, f32[4,64]{1,0:T(4,128)S(1)} %copy-done, ...), custom_call_target="tpu_custom_call" | custom-call | tf_op jit(solution)/shard_map/pallas_call | solution.py:415
  11.7 0.0 collective-permute-done
  11.7 1.9 %collective-permute-done.1 = f32[64,384]{1,0:T(8,128)S(1)} collective-permute-done((f32[64,384]{1,0:T(8,128)S(1)}, f32[64,384]{1,0:T(8,128)S(1)}, u32[]{:S(2)}, u32[]{:S(2)}) %collective-permute-start.1) | collective-permute-done | bytes 98336 | tf_op jit(solution)/shard_map/ppermute | solution.py:489
  13.7 0.0 collective-permute-done.2
  13.7 1.3 %collective-permute-start.3 = (f32[64,384]{1,0:T(8,128)S(1)}, f32[64,384]{1,0:T(8,128)S(1)}, u32[]{:S(2)}, u32[]{:S(2)}) collective-permute-start(f32[64,384]{1,0:T(8,128)S(1)} %add_add_fusion.1), channel_id=1, source_target_pairs={{0,12},{1,13},{2,14},{3,15},{4,8},{5,9},{6,10},{7,11},{8,4},{9,5},... | collective-permute-start | bytes 294920 | tf_op jit(solution)/shard_map/ppermute | solution.py:489
  15.0 1.2 %collective-permute-start.4 = (f32[64,384]{1,0:T(8,128)S(1)}, f32[64,384]{1,0:T(8,128)S(1)}, u32[]{:S(2)}, u32[]{:S(2)}) collective-permute-start(f32[64,384]{1,0:T(8,128)S(1)} %add_add_fusion.1), channel_id=1, source_target_pairs={{0,4},{1,5},{2,6},{3,7},{4,0},{5,1},{6,2},{7,3},{8,12},{9,13},{10,... | collective-permute-start | bytes 294920 | tf_op jit(solution)/shard_map/ppermute | solution.py:489
  16.2 1.0 %collective-permute-start.5 = (f32[64,384]{1,0:T(8,128)S(1)}, f32[64,384]{1,0:T(8,128)S(1)}, u32[]{:S(2)}, u32[]{:S(2)}) collective-permute-start(f32[64,384]{1,0:T(8,128)S(1)} %add_add_fusion.1), channel_id=1, source_target_pairs={{0,8},{1,9},{2,10},{3,11},{4,12},{5,13},{6,14},{7,15},{8,0},{9,1},... | collective-permute-start | bytes 294920 | tf_op jit(solution)/shard_map/ppermute | solution.py:489
  17.2 0.0 collective-permute-done.6.mine_ref
  17.2 2.8 %collective-permute-start.7 = (f32[8,16,384]{2,1,0:T(8,128)S(1)}, f32[8,16,384]{2,1,0:T(8,128)S(1)}, u32[]{:S(2)}, u32[]{:S(2)}) collective-permute-start(f32[8,16,384]{2,1,0:T(8,128)S(1)} %collective-permute-done.6.mine_ref), channel_id=1, source_target_pairs={{0,16},{16,0},{1,17},{17,1},{2,18},{18,2},{3,19},{19,3},{4,20},{20... | collective-permute-start | bytes 589832 | tf_op jit(solution)/shard_map/ppermute | solution.py:496
  19.9 0.0 collective-permute-done.3
  19.9 0.0 collective-permute-done.4
  19.9 0.0 collective-permute-done.5
  20.0 1.0 %collective-permute-done.7.other_ref = f32[8,16,384]{2,1,0:T(8,128)S(1)} collective-permute-done((f32[8,16,384]{2,1,0:T(8,128)S(1)}, f32[8,16,384]{2,1,0:T(8,128)S(1)}, u32[]{:S(2)}, u32[]{:S(2)}) %collective-permute-start.7) | collective-permute-done | bytes 196640 | tf_op jit(solution)/shard_map/ppermute | solution.py:496
  21.0 2.4 %shard_map.102 = (f32[4,64,384]{2,1,0:T(8,128)S(1)}, f32[3,3,64,128]{3,2,1,0:T(8,128)S(1)}) custom-call(f32[64,384]{1,0:T(8,128)S(1)} %add_add_fusion.pred_ref, bf16[768,1536]{1,0:T(8,128)(2,1)S(1)} %get-tuple-element.27.corr_ref, f32[5,64,128]{2,1,0:T(8,128)S(1)} %get-tuple-element.28.pick_ref, f32[3,3,512,128]{3,2,1,0:T(8,128)S(1)} %get-tuple-element.29.khat_ref, ...), custom_call_target="tpu_custom_call" | custom-call | flops 1 | bytes 1 | tf_op jit(solution)/shard_map/pallas_call | solution.py:341
  23.4 4.1 %collective-permute-start.8 = (f32[4,64,384]{2,1,0:T(8,128)S(1)}, f32[4,64,384]{2,1,0:T(8,128)S(1)}, u32[]{:S(2)}, u32[]{:S(2)}) collective-permute-start(f32[4,64,384]{2,1,0:T(8,128)S(1)} %get-tuple-element.36), channel_id=1, source_target_pairs={{0,16},{16,0},{1,17},{17,1},{2,18},{18,2},{3,19},{19,3},{4,20},{20... | collective-permute-start | bytes 1179656 | tf_op jit(solution)/shard_map/ppermute | solution.py:503
  27.4 1.5 %shard_map.103.refs_0_ = f32[4,64,384]{2,1,0:T(8,128)S(1)} custom-call(f32[3,3,64,128]{3,2,1,0:T(8,128)S(1)} %get-tuple-element.32.rhat_ref, f32[3,3,512,128]{3,2,1,0:T(8,128)S(1)} %get-tuple-element.29.khat_ref, bf16[1536,384]{1,0:T(8,128)(2,1)S(1)} %get-tuple-element.31.inverse_ref, f32[8,64,384]{2,1,0:T(8,128)S(1)} %get-tuple-element.33.vec_ref, ...), custom_call_target="tpu_custom_call" | custom-call | flops 452984832 | bytes 2359296 | tf_op jit(solution)/shard_map/pallas_call | solution.py:359
  28.9 0.0 collective-permute-done.8.refs_1_
  29.0 0.8 %shard_map.104 = f32[4,64,384]{2,1,0:T(8,128)} custom-call(f32[4,64,384]{2,1,0:T(8,128)S(1)} %shard_map.103.refs_0_, f32[4,64,384]{2,1,0:T(8,128)S(1)} %collective-permute-done.8.refs_1_), custom_call_target="tpu_custom_call" | custom-call | tf_op jit(solution)/shard_map/pallas_call | solution.py:437
  (11 shorter events, 0.1 us)
Async XLA Ops:
  0.0 10.4 %copy-start.4 = (f32[64]{0:T(128)S(1)}, f32[64]{0:T(128)}, u32[]{:S(2)}) copy-start(f32[64]{0:T(128)} %param.15) | copy-start | bytes 772
  0.0 10.4 %copy-start.2 = (f32[8]{0:T(128)S(1)}, f32[8]{0:T(128)}, u32[]{:S(2)}) copy-start(f32[8]{0:T(128)} %scale_ref.1) | copy-start | bytes 100
  0.0 10.4 %copy-start.3 = (s32[8]{0:T(128)S(1)}, s32[8]{0:T(128)}, u32[]{:S(2)}) copy-start(s32[8]{0:T(128)} %group_ref.1) | copy-start | bytes 100
  0.0 10.4 %copy-start = (f32[4,64]{1,0:T(4,128)S(1)}, f32[4,64]{1,0:T(4,128)}, u32[]{:S(2)}) copy-start(f32[4,64]{1,0:T(4,128)} %coup_ref.1) | copy-start | bytes 3076
  0.0 10.4 %copy-start.1 = (s32[4,64]{1,0:T(4,128)S(1)}, s32[4,64]{1,0:T(4,128)}, u32[]{:S(2)}) copy-start(s32[4,64]{1,0:T(4,128)} %near_ref.1) | copy-start | bytes 3076
  5.5 6.3 %collective-permute-start = (f32[64,384]{1,0:T(8,128)S(1)}, f32[64,384]{1,0:T(8,128)S(1)}, u32[]{:S(2)}, u32[]{:S(2)}) collective-permute-start(f32[64,384]{1,0:T(8,128)S(1)} %get-tuple-element.21), channel_id=1, source_target_pairs={{0,3},{1,2},{2,1},{3,0},{4,7},{5,6},{6,5},{7,4},{8,11},{9,10},{10,... | collective-permute-start | bytes 294920 | tf_op jit(solution)/shard_map/ppermute | solution.py:489
  8.8 4.8 %collective-permute-start.1 = (f32[64,384]{1,0:T(8,128)S(1)}, f32[64,384]{1,0:T(8,128)S(1)}, u32[]{:S(2)}, u32[]{:S(2)}) collective-permute-start(f32[64,384]{1,0:T(8,128)S(1)} %get-tuple-element.21), channel_id=1, source_target_pairs={{0,1},{1,0},{2,3},{3,2},{4,5},{5,4},{6,7},{7,6},{8,9},{9,8},{10,11... | collective-permute-start | bytes 294920 | tf_op jit(solution)/shard_map/ppermute | solution.py:489
  8.8 4.8 %collective-permute-start.2 = (f32[64,384]{1,0:T(8,128)S(1)}, f32[64,384]{1,0:T(8,128)S(1)}, u32[]{:S(2)}, u32[]{:S(2)}) collective-permute-start(f32[64,384]{1,0:T(8,128)S(1)} %get-tuple-element.21), channel_id=1, source_target_pairs={{0,2},{1,3},{2,0},{3,1},{4,6},{5,7},{6,4},{7,5},{8,10},{9,11},{10,... | collective-permute-start | bytes 294920 | tf_op jit(solution)/shard_map/ppermute | solution.py:489
  9.2 8.0 %collective-permute-start.6 = (f32[8,16,384]{2,1,0:T(8,128)S(1)}, f32[8,16,384]{2,1,0:T(8,128)S(1)}, u32[]{:S(2)}, u32[]{:S(2)}) collective-permute-start(f32[8,16,384]{2,1,0:T(8,128)S(1)} %get-tuple-element.25), channel_id=1, source_target_pairs={{0,1},{1,0},{2,3},{3,2},{4,5},{5,4},{6,7},{7,6},{8,9},{9,8},{10,11... | collective-permute-start | bytes 589832 | tf_op jit(solution)/shard_map/ppermute | solution.py:491
  13.7 6.2 %collective-permute-start.3 = (f32[64,384]{1,0:T(8,128)S(1)}, f32[64,384]{1,0:T(8,128)S(1)}, u32[]{:S(2)}, u32[]{:S(2)}) collective-permute-start(f32[64,384]{1,0:T(8,128)S(1)} %add_add_fusion.1), channel_id=1, source_target_pairs={{0,12},{1,13},{2,14},{3,15},{4,8},{5,9},{6,10},{7,11},{8,4},{9,5},... | collective-permute-start | bytes 294920 | tf_op jit(solution)/shard_map/ppermute | solution.py:489
  15.0 5.0 %collective-permute-start.4 = (f32[64,384]{1,0:T(8,128)S(1)}, f32[64,384]{1,0:T(8,128)S(1)}, u32[]{:S(2)}, u32[]{:S(2)}) collective-permute-start(f32[64,384]{1,0:T(8,128)S(1)} %add_add_fusion.1), channel_id=1, source_target_pairs={{0,4},{1,5},{2,6},{3,7},{4,0},{5,1},{6,2},{7,3},{8,12},{9,13},{10,... | collective-permute-start | bytes 294920 | tf_op jit(solution)/shard_map/ppermute | solution.py:489
  16.2 3.8 %collective-permute-start.5 = (f32[64,384]{1,0:T(8,128)S(1)}, f32[64,384]{1,0:T(8,128)S(1)}, u32[]{:S(2)}, u32[]{:S(2)}) collective-permute-start(f32[64,384]{1,0:T(8,128)S(1)} %add_add_fusion.1), channel_id=1, source_target_pairs={{0,8},{1,9},{2,10},{3,11},{4,12},{5,13},{6,14},{7,15},{8,0},{9,1},... | collective-permute-start | bytes 294920 | tf_op jit(solution)/shard_map/ppermute | solution.py:489
  17.2 3.8 %collective-permute-start.7 = (f32[8,16,384]{2,1,0:T(8,128)S(1)}, f32[8,16,384]{2,1,0:T(8,128)S(1)}, u32[]{:S(2)}, u32[]{:S(2)}) collective-permute-start(f32[8,16,384]{2,1,0:T(8,128)S(1)} %collective-permute-done.6.mine_ref), channel_id=1, source_target_pairs={{0,16},{16,0},{1,17},{17,1},{2,18},{18,2},{3,19},{19,3},{4,20},{20... | collective-permute-start | bytes 589832 | tf_op jit(solution)/shard_map/ppermute | solution.py:496
  23.4 5.6 %collective-permute-start.8 = (f32[4,64,384]{2,1,0:T(8,128)S(1)}, f32[4,64,384]{2,1,0:T(8,128)S(1)}, u32[]{:S(2)}, u32[]{:S(2)}) collective-permute-start(f32[4,64,384]{2,1,0:T(8,128)S(1)} %get-tuple-element.36), channel_id=1, source_target_pairs={{0,16},{16,0},{1,17},{17,1},{2,18},{18,2},{3,19},{19,3},{4,20},{20... | collective-permute-start | bytes 1179656 | tf_op jit(solution)/shard_map/ppermute | solution.py:503
